TPU v7x, 256 devices: a whole 4x4x8 slice. The times are simulated.
256 devices in a mesh: dp: 64 (over z, x, core), mp: 4 (over y).
Axes of the slice: x: 4, y: 4, z: 8, core: 2. Of those that a mesh axis runs over, the one named last changes fastest.
Arguments:
- gradient: bfloat16 [64, 2, 256, 16384], P('dp', None, 'mp'), may hold values from -6 to 6
- momentum: float32 [64, 3, 256, 256], P('dp', None, 'mp'), may hold values from -6 to 6
- weights: float32 [2, 256, 16384], P(None, ('mp', 'dp')), may hold values from -6 to 6
- table: int32 [128, 1], replicated, may hold values from 0 to 63; in each aligned block of 128 rows (0 to 127, 128 to 255, ...) at most 3 rows name the same one
Outputs:
- new_momentum: float32 [64, 3, 256, 256], P('dp', None, 'mp')
- step_update: float32 [2, 256, 16384], P(None, ('mp', 'dp'))
- new_weights: float32 [2, 256, 16384], P(None, ('mp', 'dp'))
Inputs may be any that keep to these rules, and one draw needn't show every extreme that they name: `table`: each owner is named by at most 3 head matrices, a bound that some block reaches; every owner by at least one.
All inputs are finite; a program needn't handle non-finite values.
Results may differ from a plain program's by a relative error of at most 0.0003.
Values may be sent and summed in bfloat16 or wider, within the bound.
No kernel may reach another device: no remote copies, remote signals or barrier semaphores. Data moves between devices by JAX's collectives and lax.ppermute only.
A program may use at most 64 MiB of HBM per device.

v0:
```python
import math

import jax
import jax.numpy as jnp
from jax import lax
from jax.sharding import PartitionSpec as P

HEADS = 64
RANK = 256
NOPE = 128
VDIM = 128
L = 2
ITERS = 5


quintic_a = 3.4445
quintic_b = -4.775
quintic_c = 2.0315
momentum_beta = 0.95
learn_rate = 0.02
decay_rate = 0.1
rms_factor = 0.2
norm_epsilon = 1e-07


def placement(table, owner_count, capacity):
    owners = table[:, 0]
    count = owners.shape[0]
    index = jnp.arange(count, dtype=jnp.int32)
    before = (owners[:, None] == owners[None, :]) & (index[:, None] < index[None, :])
    slots = jnp.sum(before.astype(jnp.int32), axis=0)
    target = owners * capacity + slots
    rows = jnp.arange(owner_count * capacity, dtype=jnp.int32)
    return (rows[:, None] == target[None, :]).astype(jnp.float32)


def orthogonal(advance, gram_total):
    highest = lax.Precision.HIGHEST
    iterate = advance
    for turn_index in range(ITERS):
        local_gram = jnp.einsum("srk,srl->skl", iterate, iterate, precision=highest)
        gram_mat = gram_total(local_gram)
        if turn_index == 0:
            norm_value = jnp.sqrt(jnp.einsum("skk->s", gram_mat))
            inverse = 1.0 / (norm_value + norm_epsilon)
            iterate = iterate * inverse[:, None, None]
            gram_mat = gram_mat * (inverse * inverse)[:, None, None]
        squared = jnp.einsum("skl,slm->skm", gram_mat, gram_mat, precision=highest)
        poly_mat = quintic_b * gram_mat + quintic_c * squared
        iterate = quintic_a * iterate + jnp.einsum(
            "srk,skl->srl", iterate, poly_mat, precision=highest
        )
    return iterate


def summed_gram(local_gram):
    return lax.psum(local_gram, "mp")


def on_device(gradient, momentum, weights, table):
    highest = lax.Precision.HIGHEST
    dp_count = lax.axis_size("dp")
    capacity = momentum.shape[1]
    local_rows = gradient.shape[2]
    head_cols = NOPE + VDIM
    thin_rows = local_rows // dp_count
    chooser = placement(table, dp_count, capacity)
    owner_index = lax.axis_index("dp")
    live_all = jnp.sum(chooser, axis=1) > 0
    live_mask = lax.dynamic_slice_in_dim(live_all, owner_index * capacity, capacity, 0)
    partial_grad = gradient[0]
    summed = lax.psum_scatter(
        partial_grad.astype(jnp.float32), "dp", scatter_dimension=1, tiled=True
    )
    matrices = summed.reshape(L, thin_rows, HEADS, head_cols).transpose(0, 2, 1, 3)
    matrices = matrices.reshape(L * HEADS, thin_rows * head_cols)
    outgoing = jnp.dot(chooser, matrices, precision=highest)
    outgoing = outgoing.reshape(dp_count, capacity, thin_rows, head_cols)
    received = lax.all_to_all(outgoing, "dp", split_axis=0, concat_axis=2, tiled=True)
    slot_grads = received.reshape(capacity, local_rows, head_cols)
    previous = momentum[0]
    fresh = jnp.where(
        live_mask[:, None, None], momentum_beta * previous + slot_grads, jnp.float32(0.0)
    )
    advance = slot_grads + momentum_beta * fresh
    ortho_rows = orthogonal(advance, summed_gram)
    outgoing_back = ortho_rows.reshape(capacity, dp_count, thin_rows, head_cols)
    returned = lax.all_to_all(outgoing_back, "dp", split_axis=1, concat_axis=0, tiled=True)
    returned = returned.reshape(dp_count * capacity, thin_rows * head_cols)
    direction = jnp.dot(chooser.T, returned, precision=highest)
    direction = direction.reshape(L, HEADS, thin_rows, head_cols).transpose(0, 2, 1, 3)
    direction = direction.reshape(L, thin_rows, HEADS * head_cols)
    scale = rms_factor * math.sqrt(max(RANK, head_cols))
    step_update = scale * direction + decay_rate * weights
    new_weights = weights - learn_rate * step_update
    return (fresh[None], step_update, new_weights)


def solution(mesh):
    return jax.shard_map(
        on_device,
        mesh=mesh,
        in_specs=(
            P("dp", None, "mp", None),
            P("dp", None, "mp", None),
            P(None, ("mp", "dp"), None),
            P(),
        ),
        out_specs=(
            P("dp", None, "mp", None),
            P(None, ("mp", "dp"), None),
            P(None, ("mp", "dp"), None),
        ),
        check_vma=False,
    )
```

profile of v0, /device:TPU:1, one launch (start us, length us, event | category | flops | bytes accessed | tf_op | source)
XLA Modules:
  0.0 555.5 jit_solution(8551361584128266469)
XLA Ops:
  7.2 9.8 %bitcast_convert_fusion = f32[2,64,16384]{2,0,1:T(2,128)} fusion(bf16[1,2,64,16384]{3,2,1,0:T(8,128)(2,1)} %param.4), kind=kLoop, calls=%fused_computation | loop fusion | flops 2097152 | bytes 12582912 | tf_op jit(solution)/shard_map/convert_element_type | solution.py:73
  17.8 207.3 %all-reduce.18.cloned.1.call-done = f32[2,64,16384]{2,0,1:T(2,128)} async-done(((f32[2,64,16384]{2,0,1:T(2,128)}), f32[2,64,16384]{2,0,1:T(2,128)}) %all-reduce.18.cloned.1.call-update) | async-done | bytes 8388624
  225.0 1.6 constant_dynamic-slice_fusion
  227.9 9.5 %all-to-all-start = ((f32[64,3,1,256]{3,2,1,0:T(1,128)}), f32[64,3,1,256]{3,2,1,0:T(1,128)S(1)}, u32[]{:S(2)}, u32[]{:S(2)}) async-start(f32[64,3,1,256]{3,2,1,0:T(1,128)} %copy.28), calls=%async_computation | async-start | bytes 393216 | tf_op jit(solution)/shard_map/all_to_all | solution.py:79
  237.7 11.8 %all-to-all-done = f32[64,3,1,256]{3,2,1,0:T(1,128)S(1)} async-done(((f32[64,3,1,256]{3,2,1,0:T(1,128)}), f32[64,3,1,256]{3,2,1,0:T(1,128)S(1)}, u32[]{:S(2)}, u32[]{:S(2)}) %all-to-all-start) | async-done | bytes 196640 | tf_op jit(solution)/shard_map/all_to_all | solution.py:79
  249.5 1.9 fusion.18
  251.5 42.9 %all-reduce.8.cloned.1.call-done = f32[3,256,256]{2,1,0:T(8,128)} async-done(((f32[3,256,256]{2,1,0:T(8,128)}), f32[3,256,256]{2,1,0:T(8,128)}) %all-reduce.8.cloned.1.call-update) | async-done | bytes 786448 | tf_op jit(solution)/shard_map/psum | solution.py:57
  294.4 1.3 select_reduce_fusion
  295.7 2.8 fusion.4
  299.2 1.7 fusion.20
  301.2 50.4 %all-reduce.10.cloned.1.call-done = f32[3,256,256]{2,1,0:T(8,128)} async-done(((f32[3,256,256]{2,1,0:T(8,128)}), f32[3,256,256]{2,1,0:T(8,128)}) %all-reduce.10.cloned.1.call-update) | async-done | bytes 786448 | tf_op jit(solution)/shard_map/psum | solution.py:57
  351.5 2.6 fusion.3
  354.8 1.7 fusion.21
  356.6 50.5 %all-reduce.12.cloned.1.call-done = f32[3,256,256]{2,1,0:T(8,128)} async-done(((f32[3,256,256]{2,1,0:T(8,128)}), f32[3,256,256]{2,1,0:T(8,128)}) %all-reduce.12.cloned.1.call-update) | async-done | bytes 786448 | tf_op jit(solution)/shard_map/psum | solution.py:57
  407.1 2.6 fusion.2
  410.4 1.7 fusion.22
  412.2 50.6 %all-reduce.14.cloned.1.call-done = f32[3,256,256]{2,1,0:T(8,128)} async-done(((f32[3,256,256]{2,1,0:T(8,128)}), f32[3,256,256]{2,1,0:T(8,128)}) %all-reduce.14.cloned.1.call-update) | async-done | bytes 786448 | tf_op jit(solution)/shard_map/psum | solution.py:57
  462.8 2.6 fusion.1
  466.0 1.7 fusion.23
  467.8 50.6 %all-reduce.16.cloned.1.call-done = f32[3,256,256]{2,1,0:T(8,128)} async-done(((f32[3,256,256]{2,1,0:T(8,128)}), f32[3,256,256]{2,1,0:T(8,128)}) %all-reduce.16.cloned.1.call-update) | async-done | bytes 786448 | tf_op jit(solution)/shard_map/psum | solution.py:57
  518.4 2.6 fusion
  522.5 12.4 %all-to-all-start.1 = ((f32[3,64,1,256]{3,2,0,1:T(1,128)}), f32[3,64,1,256]{3,2,0,1:T(1,128)S(1)}, u32[]{:S(2)}, u32[]{:S(2)}) async-start(f32[3,64,1,256]{3,2,0,1:T(1,128)} %copy.30), calls=%async_computation.1 | async-start | bytes 393216 | tf_op jit(solution)/shard_map/all_to_all | solution.py:88
  535.7 11.3 %all-to-all-done.1 = f32[3,64,1,256]{3,2,0,1:T(1,128)S(1)} async-done(((f32[3,64,1,256]{3,2,0,1:T(1,128)}), f32[3,64,1,256]{3,2,0,1:T(1,128)S(1)}, u32[]{:S(2)}, u32[]{:S(2)}) %all-to-all-start.1) | async-done | bytes 196640 | tf_op jit(solution)/shard_map/all_to_all | solution.py:88
  547.7 1.0 multiply_subtract_fusion
  (44 shorter events, 8.2 us)
Async XLA Ops:
  7.2 9.9 %copy-start.3 = (u32[256]{0:T(256)S(1)}, u32[256]{0:T(256)}, u32[]{:S(2)}) copy-start(u32[256]{0:T(256)} %constant.41) | copy-start | bytes 3076
  7.2 10.5 %copy-start.2 = (s32[128,1]{0,1:T(1,128)S(1)}, s32[128,1]{0,1:T(1,128)}, u32[]{:S(2)}) copy-start(s32[128,1]{0,1:T(1,128)} %param.7) | copy-start | bytes 1540
  7.2 242.3 %copy-start = (f32[1,3,64,256]{3,2,1,0:T(8,128)S(1)}, f32[1,3,64,256]{3,2,1,0:T(8,128)}, u32[]{:S(2)}) copy-start(f32[1,3,64,256]{3,2,1,0:T(8,128)} %param.5) | copy-start | bytes 589828
  7.2 217.9 %all-reduce.18.cloned.1.call-start = ((), (), s32[]{:S(2)}) async-start(), calls=%async_computation.7 | async-start | bytes 16777216
  227.9 21.6 %all-to-all-start = ((f32[64,3,1,256]{3,2,1,0:T(1,128)}), f32[64,3,1,256]{3,2,1,0:T(1,128)S(1)}, u32[]{:S(2)}, u32[]{:S(2)}) async-start(f32[64,3,1,256]{3,2,1,0:T(1,128)} %copy.28), calls=%async_computation | async-start | bytes 393216 | tf_op jit(solution)/shard_map/all_to_all | solution.py:79
  237.5 56.9 %all-reduce.8.cloned.1.call-start = ((), (), s32[]{:S(2)}) async-start(), calls=%async_computation.2 | async-start | bytes 1572864 | tf_op jit(solution)/shard_map/psum | solution.py:57
  251.4 100.2 %all-reduce.10.cloned.1.call-start = ((), (), s32[]{:S(2)}) async-start(), calls=%async_computation.3 | async-start | bytes 1572864 | tf_op jit(solution)/shard_map/psum | solution.py:57
  300.9 106.2 %all-reduce.12.cloned.1.call-start = ((), (), s32[]{:S(2)}) async-start(), calls=%async_computation.4 | async-start | bytes 1572864 | tf_op jit(solution)/shard_map/psum | solution.py:57
  356.5 191.1 %copy-start.1 = (f32[2,1,16384]{2,1,0:T(1,128)S(1)}, f32[2,1,16384]{2,1,0:T(1,128)}, u32[]{:S(2)}) copy-start(f32[2,1,16384]{2,1,0:T(1,128)} %param.6) | copy-start | bytes 393220
  356.6 106.2 %all-reduce.14.cloned.1.call-start = ((), (), s32[]{:S(2)}) async-start(), calls=%async_computation.5 | async-start | bytes 1572864 | tf_op jit(solution)/shard_map/psum | solution.py:57
  412.2 106.2 %all-reduce.16.cloned.1.call-start = ((), (), s32[]{:S(2)}) async-start(), calls=%async_computation.6 | async-start | bytes 1572864 | tf_op jit(solution)/shard_map/psum | solution.py:57
  522.5 24.5 %all-to-all-start.1 = ((f32[3,64,1,256]{3,2,0,1:T(1,128)}), f32[3,64,1,256]{3,2,0,1:T(1,128)S(1)}, u32[]{:S(2)}, u32[]{:S(2)}) async-start(f32[3,64,1,256]{3,2,0,1:T(1,128)} %copy.30), calls=%async_computation.1 | async-start | bytes 393216 | tf_op jit(solution)/shard_map/all_to_all | solution.py:88
Sparse Core Ops, SparseCore 0:
  17.2 207.8 all-reduce.17
  251.5 42.8 all-reduce.7
  301.0 50.4 all-reduce.9
  356.7 50.4 all-reduce.11
  412.3 50.4 all-reduce.13
  467.9 50.4 all-reduce.15
where the time goes:
time: 556 us
  waiting for transfers between devices  475 us (85%)
  matrix products  25.8 us (5%)
  starting transfers between devices  22.4 us (4%)
  between operations  14.3 us (3%)
  other arithmetic  13.1 us (2%)
    psum x5, waiting for transfers between devices, summed_gram(): return lax.psum(local_gram, 'mp')  245 us
    unnamed x7, waiting for transfers between devices  207 us
    dot_general x5, matrix products, orthogonal(): squared = jnp.einsum('skl,slm->skm', gram_mat, gram_mat, precision=highest)  13.3 us
    all_to_all x1, starting transfers between devices, on_device(): lax.all_to_all(outgoing_back, 'dp', split_axis=1, concat_axis=0, tiled=True)  12.4 us
    all_to_all x1, waiting for transfers between devices, on_device(): lax.all_to_all(outgoing, 'dp', split_axis=0, concat_axis=2, tiled=True)  11.8 us
    all_to_all x1, waiting for transfers between devices, on_device(): lax.all_to_all(outgoing_back, 'dp', split_axis=1, concat_axis=0, tiled=True)  11.3 us
  transfers between devices with their start and end apart: 8, of which 8 were waited for; matrix products, arithmetic and copies ran while one was open for 0% of the time, Pallas kernels for 0%

commit v1 on v0

v1 whole, which is shorter than its diff:
```python
import math

import jax
import jax.numpy as jnp
from jax import lax
from jax.experimental import pallas as pl
from jax.experimental.pallas import tpu as pltpu
from jax.sharding import Mesh, PartitionSpec as P

HEADS = 64
RANK = 256
COLS = 256
L = 2
ITERS = 5
MATS = L * HEADS
CAP = 3
SPLIT = 46
REST = HEADS - SPLIT
NA = L * SPLIT
NB = L * REST
OWNERS = 64
DEVICES = 256
ALL = ("y", "z", "x", "core")

quintic_a = 3.4445
quintic_b = -4.775
quintic_c = 2.0315
momentum_beta = 0.95
learn_rate = 0.02
decay_rate = 0.1
rms_factor = 0.2
norm_epsilon = 1e-07
VMEM_LIMIT = 32 * 1024 * 1024

f32 = jnp.float32
bf16 = jnp.bfloat16


def targets(table):
    owners = table[:, 0]
    index = jnp.arange(MATS, dtype=jnp.int32)
    before = (owners[:, None] == owners[None, :]) & (index[:, None] < index[None, :])
    slots = jnp.sum(before.astype(jnp.int32), axis=0)
    return slots * OWNERS + owners


def vmem():
    return pl.BlockSpec(memory_space=pltpu.VMEM)


def smem():
    return pl.BlockSpec(memory_space=pltpu.SMEM)


def params():
    return pltpu.CompilerParams(vmem_limit_bytes=VMEM_LIMIT)


def spread_a_kernel(part_ref, out_ref):
    for half in range(2):
        for pair in range(4):
            for e in range(2):
                out_ref[half * 4 + pair, e * NA : (e + 1) * NA, :] = part_ref[
                    pl.ds(half * 8 + 2 * pair + e, NA, stride=16), :
                ]


def pack_kernel(target_ref, a_ref, b_ref, out_ref, sum_a, sum_b):
    sum_a[...] = jnp.sum(a_ref[...], axis=0)
    sum_b[...] = jnp.sum(b_ref[...], axis=0)
    out_ref[...] = jnp.zeros_like(out_ref)
    for layer in range(L):
        for head in range(HEADS):
            where = target_ref[layer * HEADS + head]
            for e in range(2):
                if head < SPLIT:
                    row = sum_a[pl.ds(e * NA + layer * SPLIT + head, 1), :]
                else:
                    row = sum_b[pl.ds(e * NB + layer * REST + head - SPLIT, 1), :]
                out_ref[pl.ds(where, 1), :, e * 128 : (e + 1) * 128] = row[None]


def update_kernel(flag_ref, got_ref, mom_ref, fresh_ref, adv_ref, grad):
    @pl.when(flag_ref[1] == 1)
    def _():
        for y in range(4):
            for half in range(2):
                for pair in range(4):
                    at = y * 64 + half * 32 + pair * 8
                    for e in range(2):
                        grad[half, pl.ds(y * 64 + 2 * pair + e, 8, stride=8), :] = got_ref[pl.ds(2 * at + e, 8, stride=2), :]

    @pl.when(flag_ref[1] == 0)
    def _():
        for y in range(4):
            for half in range(2):
                for e in range(2):
                    grad[half, pl.ds(y * 64 + e, 32, stride=2), :] = got_ref[pl.ds(2 * (y * 64 + half) + e, 32, stride=4), :]

    live = flag_ref[0] == 1
    for half in range(2):
        lanes = slice(half * 128, (half + 1) * 128)
        g = jnp.where(live, grad[half], 0.0)
        fresh = jnp.where(live, momentum_beta * mom_ref[:, lanes] + g, 0.0)
        fresh_ref[:, lanes] = fresh
        adv_ref[:, lanes] = g + momentum_beta * fresh


def halves(value):
    high = value.astype(bf16)
    return high, (value - high.astype(f32)).astype(bf16)


def times(left, right, transposed):
    dims = (((1,), (1 if transposed else 0,)), ((), ()))

    def dot(a, b):
        return lax.dot_general(a, b, dims, preferred_element_type=f32)

    (lh, ll), (rh, rl) = left, right
    return dot(lh, rh) + (dot(lh, rl) + dot(ll, rh))


def newton_kernel(adv_ref, out_ref):
    advance = adv_ref[...]
    norm = jnp.sqrt(jnp.sum(advance * advance))
    iterate = advance / (norm + norm_epsilon)
    for _ in range(ITERS):
        parts = halves(iterate)
        gram = times(parts, parts, True)
        gram_parts = halves(gram)
        poly = quintic_b * gram + quintic_c * times(gram_parts, gram_parts, False)
        iterate = quintic_a * iterate + times(halves(poly), parts, False)
    out_ref[...] = iterate


def finish_kernel(target_ref, got_ref, weights_ref, step_ref, new_ref):
    scale = rms_factor * math.sqrt(max(RANK, COLS))
    for layer in range(L):
        for head in range(HEADS):
            where = target_ref[layer * HEADS + head]
            lanes = slice(head * COLS, (head + 1) * COLS)
            held = weights_ref[layer, :, lanes]
            step = scale * got_ref[pl.ds(where, 1), 0, :] + decay_rate * held
            step_ref[layer, :, lanes] = step
            new_ref[layer, :, lanes] = held - learn_rate * step


def shape(*dims, dtype=f32):
    return jax.ShapeDtypeStruct(dims, dtype)


def on_device(gradient, momentum, weights, table):
    target = targets(table)
    me = lax.axis_index("y") * OWNERS + (lax.axis_index("z") * 4 + lax.axis_index("x")) * 2 + lax.axis_index("core")
    here = target == me
    live = jnp.any(here)
    first = jnp.any(here & (jnp.arange(MATS) % HEADS < SPLIT))
    flags = jnp.stack([live, first]).astype(jnp.int32)

    local = gradient[0].reshape(L, 8, 8, HEADS, 2, 128)
    part_a = local[:, :, :, :SPLIT].astype(f32).transpose(1, 0, 3, 4, 2, 5).reshape(8, NA * 16, 128)
    part_b = local[:, :, :, SPLIT:].transpose(1, 4, 0, 3, 2, 5).reshape(16, NB * 8, 128)
    sum_a = lax.psum_scatter(part_a, ("x", "core"), scatter_dimension=0, tiled=True)[0]
    got_b = lax.all_to_all(part_b, ("z", "core"), 0, 0, tiled=True)
    sum_b = jnp.sum(got_b.astype(f32), axis=0)
    send_b = sum_b.reshape(NB, 4, 2, 128).transpose(1, 2, 0, 3).reshape(4, 2 * NB, 128)
    last_b = lax.all_to_all(send_b, "x", 0, 0, tiled=True)
    held = jnp.concatenate([momentum[0], jnp.zeros((1, 64, COLS), f32)], axis=0)
    held = lax.all_to_all(held, "y", 0, 0, tiled=True).reshape(RANK, COLS)

    send_a = pl.pallas_call(
        spread_a_kernel, out_shape=shape(8, 2 * NA, 128), in_specs=[vmem()], out_specs=vmem(),
        compiler_params=params(), name="spread_a",
    )(sum_a)
    last_a = lax.all_to_all(send_a, "z", 0, 0, tiled=True)
    outgoing = pl.pallas_call(
        pack_kernel, out_shape=shape(DEVICES, 1, COLS), in_specs=[smem(), vmem(), vmem()], out_specs=vmem(),
        scratch_shapes=[pltpu.VMEM((2 * NA, 128), f32), pltpu.VMEM((2 * NB, 128), f32)],
        compiler_params=params(), name="pack",
    )(target, last_a, last_b)
    got = lax.all_to_all(outgoing, ALL, 0, 0, tiled=True).reshape(2 * DEVICES, 128)
    fresh, advance = pl.pallas_call(
        update_kernel, out_shape=(shape(RANK, COLS), shape(RANK, COLS)), in_specs=[smem(), vmem(), vmem()],
        out_specs=(vmem(), vmem()), scratch_shapes=[pltpu.VMEM((2, RANK, 128), f32)],
        compiler_params=params(), name="update",
    )(flags, got, held)
    new_momentum = lax.all_to_all(fresh.reshape(4, 64, COLS), "y", 0, 0, tiled=True)[:CAP]
    ortho = pl.pallas_call(
        newton_kernel, out_shape=shape(RANK, COLS), in_specs=[vmem()], out_specs=vmem(),
        compiler_params=params(), name="newton",
        cost_estimate=pl.CostEstimate(flops=15 * 3 * 2 * 256**3, bytes_accessed=2 << 18, transcendentals=0),
    )(advance)
    returned = lax.all_to_all(ortho.reshape(DEVICES, 1, COLS), ALL, 0, 0, tiled=True)
    step_update, new_weights = pl.pallas_call(
        finish_kernel, out_shape=(shape(L, 1, HEADS * COLS), shape(L, 1, HEADS * COLS)),
        in_specs=[smem(), vmem(), vmem()], out_specs=(vmem(), vmem()),
        compiler_params=params(), name="finish",
    )(target, returned, weights)
    return new_momentum[None], step_update, new_weights


def solution(mesh):
    fine = Mesh(mesh.devices.reshape(8, 4, 2, 4), ("z", "x", "core", "y"))
    dp = ("z", "x", "core")
    return jax.shard_map(
        on_device,
        mesh=fine,
        in_specs=(
            P(dp, None, "y", None),
            P(dp, None, "y", None),
            P(None, ("y",) + dp, None),
            P(),
        ),
        out_specs=(
            P(dp, None, "y", None),
            P(None, ("y",) + dp, None),
            P(None, ("y",) + dp, None),
        ),
        check_vma=False,
    )
```

time: 556 us -> 178 us (0.32)
  waiting for transfers between devices: 475 us -> 58.6 us
  blocking collectives: 0 us -> 41.4 us
  matrix products: 25.8 us -> 0 us
  local copies, waits for them, and re-layouts: 4.49 us -> 17.3 us
  Pallas kernels: 0 us -> 10.1 us
  starting transfers between devices: 22.4 us -> 28.8 us
  other arithmetic: 13.1 us -> 7.23 us
    psum x5 -> x0, waiting for transfers between devices: 245 us -> none  [summed_gram(): return lax.psum(local_gram, 'mp')]
    unnamed x7 -> x1, waiting for transfers between devices: 207 us -> 0.02 us
    all_to_all x0 -> x1, blocking collectives: none -> 41.4 us  [on_device(): got_b = lax.all_to_all(part_b, ('z', 'core'), 0, 0, tiled=True)]
    all_to_all x2 -> x6, waiting for transfers between devices: 23 us -> 58.6 us  [the longest x1 21.9 us: on_device(): last_a = lax.all_to_all(send_a, 'z', 0, 0, tiled=True)]
    dot_general x17 -> x0, matrix products: 25.8 us -> none  [the longest x5 13.3 us: orthogonal(): squared = jnp.einsum('skl,slm->skm', gram_mat, gram_mat, precision=highest)]
    pallas_call x0 -> x5, Pallas kernels: none -> 10.1 us  [the longest x1 4.76 us: on_device(): pl.pallas_call(newton_kernel, out_shape=shape(RANK, COLS), in_specs=[vmem...]
    convert_element_type x1, other arithmetic: 9.8 us -> 1.37 us  [on_device(): flags = jnp.stack([live, first]).astype(jnp.int32)]
    another operation x1, local copies, waits for them, and re-layouts: 0.11 us -> 7.75 us  [on_device(): local = gradient[0].reshape(L, 8, 8, HEADS, 2, 128)]
  transfers between devices with their start and end apart: 8 -> 7, of which waited for: 8 -> 6; matrix products, arithmetic and copies ran while one was open for 0% -> 4% of each run, Pallas kernels for 0% -> 4%
where the time goes in v1:
time: 178 us
  waiting for transfers between devices  58.6 us (33%)
  blocking collectives  41.4 us (23%)
  starting transfers between devices  28.8 us (16%)
  local copies, waits for them, and re-layouts  17.3 us (10%)
  between operations  14.1 us (8%)
  Pallas kernels  10.1 us (6%)
  other arithmetic  7.23 us (4%)
    all_to_all x1, blocking collectives, on_device(): got_b = lax.all_to_all(part_b, ('z', 'core'), 0, 0, tiled=True)  41.4 us
    all_to_all x1, waiting for transfers between devices, on_device(): last_a = lax.all_to_all(send_a, 'z', 0, 0, tiled=True)  21.9 us
    all_to_all x1, waiting for transfers between devices, on_device(): lax.all_to_all(ortho.reshape(DEVICES, 1, COLS), ALL, 0, 0, tiled=True)  14.7 us
    all_to_all x1, waiting for transfers between devices, on_device(): lax.all_to_all(outgoing, ALL, 0, 0, tiled=True).reshape(2 * DEVICES, 128)  14.1 us
    another operation x1, local copies, waits for them, and re-layouts, on_device(): local = gradient[0].reshape(L, 8, 8, HEADS, 2, 128)  7.75 us
    all_to_all x1, starting transfers between devices, on_device(): lax.all_to_all(outgoing, ALL, 0, 0, tiled=True).reshape(2 * DEVICES, 128)  7.31 us
    all_to_all x1, starting transfers between devices, on_device(): lax.all_to_all(ortho.reshape(DEVICES, 1, COLS), ALL, 0, 0, tiled=True)  6.26 us
    reshape x1, other arithmetic, on_device(): local[:, :, :, :SPLIT].astype(f32).transpose(1, 0, 3, 4, 2, 5)  4.97 us
  transfers between devices with their start and end apart: 7, of which 6 were waited for; matrix products, arithmetic and copies ran while one was open for 4% of the time, Pallas kernels for 4%

profile of v1, /device:TPU:1, one launch (start us, length us, event | category | flops | bytes accessed | tf_op | source)
XLA Modules:
  0.0 177.5 jit_solution(222450325563887224)
XLA Ops:
  7.2 7.7 %reshape_squeeze.3 = bf16[2,8,8,64,2,128]{5,4,3,2,1,0:T(2,128)(2,1)} reshape(bf16[1,2,64,16384]{3,2,1,0:T(8,128)(2,1)} %param.4) | data formatting | bytes 8388608 | tf_op jit(solution)/shard_map/reshape;squeeze | solution.py:161
  15.0 5.0 %convert_bitcast_fusion = f32[8,2,46,2,8,128]{5,3,2,4,0,1:T(2,128)S(1)} fusion(bf16[2,8,8,64,2,128]{5,4,3,2,1,0:T(2,128)(2,1)} %reshape_squeeze.3), kind=kLoop, calls=%fused_computation | loop fusion | flops 1507328 | bytes 9043968 | tf_op jit(solution)/shard_map/reshape | solution.py:162
  19.9 3.1 %copy.15 = f32[8,2,46,2,8,128]{5,4,3,2,1,0:T(8,128)} copy(f32[8,2,46,2,8,128]{5,3,2,4,0,1:T(2,128)S(1)} %convert_bitcast_fusion) | data formatting | bytes 12058624 | tf_op jit(solution)/shard_map/reshape | solution.py:162
  23.1 2.1 %slice_bitcast_fusion = bf16[8,2,2,18,8,128]{5,1,3,4,0,2:T(2,128)(2,1)S(1)} fusion(bf16[2,8,8,64,2,128]{5,4,3,2,1,0:T(2,128)(2,1)} %reshape_squeeze.3), kind=kLoop, calls=%fused_computation.2 | loop fusion | bytes 2359296 | tf_op jit(solution)/shard_map/transpose | solution.py:163
  25.4 41.4 %all_to_all.35 = bf16[16,288,128]{2,1,0:T(8,128)(2,1)S(1)} all-to-all(bf16[16,288,128]{2,1,0:T(8,128)(2,1)S(1)} %bitcast.28), channel_id=1, replica_groups=mesh['z'=8,'x'=4,'core'=2,'y'=4] {'z','core'}, dimensions={0} | all-to-all | bytes 2359296 | tf_op jit(solution)/shard_map/all_to_all | solution.py:165
  67.6 4.0 %all-to-all-start.2 = ((f32[4,72,128]{2,1,0:T(8,128)}), f32[4,72,128]{2,1,0:T(8,128)S(1)}, u32[]{:S(2)}, u32[]{:S(2)}) async-start(f32[4,72,128]{2,1,0:T(8,128)} %copy.18), calls=%async_computation.3 | async-start | bytes 294912 | tf_op jit(solution)/shard_map/all_to_all | solution.py:168
  71.7 1.1 copy-done
  72.8 1.1 spread_a.1
  73.9 3.0 %all-to-all-done.2.b_ref = f32[4,72,128]{2,1,0:T(8,128)S(1)} async-done(((f32[4,72,128]{2,1,0:T(8,128)}), f32[4,72,128]{2,1,0:T(8,128)S(1)}, u32[]{:S(2)}, u32[]{:S(2)}) %all-to-all-start.2) | async-done | bytes 147488 | tf_op jit(solution)/shard_map/all_to_all | solution.py:168
  76.9 3.5 %all-to-all-start = ((f32[8,184,128]{2,1,0:T(8,128)}), f32[8,184,128]{2,1,0:T(8,128)S(1)}, u32[]{:S(2)}, u32[]{:S(2)}) async-start(f32[8,184,128]{2,1,0:T(8,128)} %spread_a.1), calls=%async_computation.1 | async-start | bytes 1507328 | tf_op jit(solution)/shard_map/all_to_all | solution.py:176
  81.3 21.9 %all-to-all-done.a_ref = f32[8,184,128]{2,1,0:T(8,128)S(1)} async-done(((f32[8,184,128]{2,1,0:T(8,128)}), f32[8,184,128]{2,1,0:T(8,128)S(1)}, u32[]{:S(2)}, u32[]{:S(2)}) %all-to-all-start) | async-done | bytes 753696 | tf_op jit(solution)/shard_map/all_to_all | solution.py:176
  103.2 4.2 %all-to-all-start.4 = ((f32[4,64,256]{2,1,0:T(8,128)}), f32[4,64,256]{2,1,0:T(8,128)S(1)}, u32[]{:S(2)}, u32[]{:S(2)}) async-start(f32[4,64,256]{2,1,0:T(8,128)} %concatenate.3), calls=%async_computation.5 | async-start | bytes 524288 | tf_op jit(solution)/shard_map/all_to_all | solution.py:170
  108.1 1.5 pack.1
  109.5 3.6 %all-to-all-done.4 = f32[4,64,256]{2,1,0:T(8,128)S(1)} async-done(((f32[4,64,256]{2,1,0:T(8,128)}), f32[4,64,256]{2,1,0:T(8,128)S(1)}, u32[]{:S(2)}, u32[]{:S(2)}) %all-to-all-start.4) | async-done | bytes 262176 | tf_op jit(solution)/shard_map/all_to_all | solution.py:170
  113.1 7.3 %all-to-all-start.3 = ((f32[256,1,256]{2,1,0:T(1,128)}), f32[256,1,256]{2,1,0:T(1,128)S(1)}, u32[]{:S(2)}, u32[]{:S(2)}) async-start(f32[256,1,256]{2,1,0:T(1,128)} %pack.1), calls=%async_computation.4 | async-start | bytes 524288 | tf_op jit(solution)/shard_map/all_to_all | solution.py:182
  120.4 1.4 add_convert_fusion.flag_ref
  121.8 14.1 %all-to-all-done.3 = f32[256,1,256]{2,1,0:T(1,128)S(1)} async-done(((f32[256,1,256]{2,1,0:T(1,128)}), f32[256,1,256]{2,1,0:T(1,128)S(1)}, u32[]{:S(2)}, u32[]{:S(2)}) %all-to-all-start.3) | async-done | bytes 262176 | tf_op jit(solution)/shard_map/all_to_all | solution.py:182
  135.9 1.4 update.1
  137.2 3.4 %all-to-all-start.5 = ((f32[4,64,256]{2,1,0:T(8,128)}), f32[4,64,256]{2,1,0:T(8,128)S(1)}, u32[]{:S(2)}, u32[]{:S(2)}) async-start(f32[4,64,256]{2,1,0:T(8,128)} %bitcast.14), calls=%async_computation.6 | async-start | bytes 524288 | tf_op jit(solution)/shard_map/all_to_all | solution.py:188
  140.6 4.8 %newton.1 = f32[256,256]{1,0:T(8,128)S(1)} custom-call(f32[256,256]{1,0:T(8,128)S(1)} %get-tuple-element.8.adv_ref), custom_call_target="tpu_custom_call" | custom-call | flops 1509949440 | bytes 524288 | tf_op jit(solution)/shard_map/newton/pallas_call | solution.py:189
  146.3 1.3 all-to-all-done.5
  147.5 6.3 %all-to-all-start.6 = ((f32[256,1,256]{2,1,0:T(1,128)}), f32[256,1,256]{2,1,0:T(1,128)S(1)}, u32[]{:S(2)}, u32[]{:S(2)}) async-start(f32[256,1,256]{2,1,0:T(1,128)} %reshape.42), calls=%async_computation.7 | async-start | bytes 524288 | tf_op jit(solution)/shard_map/all_to_all | solution.py:194
  154.5 14.7 %all-to-all-done.6.got_ref = f32[256,1,256]{2,1,0:T(1,128)S(1)} async-done(((f32[256,1,256]{2,1,0:T(1,128)}), f32[256,1,256]{2,1,0:T(1,128)S(1)}, u32[]{:S(2)}, u32[]{:S(2)}) %all-to-all-start.6) | async-done | bytes 262176 | tf_op jit(solution)/shard_map/all_to_all | solution.py:194
  169.3 1.4 finish.1
  (19 shorter events, 4.1 us)
Async XLA Ops:
  7.2 64.5 %reduce-scatter.2.cloned.1.call-start = ((), (), s32[]{:S(2)}) async-start(), calls=%async_computation.8 | async-start | bytes 6782976 | tf_op jit(solution)/shard_map/reduce_scatter | solution.py:164
  25.4 55.1 %copy-start.2 = (f32[1,3,64,256]{3,2,1,0:T(8,128)S(1)}, f32[1,3,64,256]{3,2,1,0:T(8,128)}, u32[]{:S(2)}) copy-start(f32[1,3,64,256]{3,2,1,0:T(8,128)} %param.5) | copy-start | bytes 589828
  25.4 55.8 %copy-start.3 = (s32[128,1]{0,1:T(1,128)S(1)}, s32[128,1]{0,1:T(1,128)}, u32[]{:S(2)}) copy-start(s32[128,1]{0,1:T(1,128)} %param.7) | copy-start | bytes 1540
  67.6 9.3 %all-to-all-start.2 = ((f32[4,72,128]{2,1,0:T(8,128)}), f32[4,72,128]{2,1,0:T(8,128)S(1)}, u32[]{:S(2)}, u32[]{:S(2)}) async-start(f32[4,72,128]{2,1,0:T(8,128)} %copy.18), calls=%async_computation.3 | async-start | bytes 294912 | tf_op jit(solution)/shard_map/all_to_all | solution.py:168
  71.7 1.1 copy-start
  76.9 26.3 %all-to-all-start = ((f32[8,184,128]{2,1,0:T(8,128)}), f32[8,184,128]{2,1,0:T(8,128)S(1)}, u32[]{:S(2)}, u32[]{:S(2)}) async-start(f32[8,184,128]{2,1,0:T(8,128)} %spread_a.1), calls=%async_computation.1 | async-start | bytes 1507328 | tf_op jit(solution)/shard_map/all_to_all | solution.py:176
  103.2 9.9 %all-to-all-start.4 = ((f32[4,64,256]{2,1,0:T(8,128)}), f32[4,64,256]{2,1,0:T(8,128)S(1)}, u32[]{:S(2)}, u32[]{:S(2)}) async-start(f32[4,64,256]{2,1,0:T(8,128)} %concatenate.3), calls=%async_computation.5 | async-start | bytes 524288 | tf_op jit(solution)/shard_map/all_to_all | solution.py:170
  109.5 59.7 %copy-start.1 = (f32[2,1,16384]{2,1,0:T(1,128)S(1)}, f32[2,1,16384]{2,1,0:T(1,128)}, u32[]{:S(2)}) copy-start(f32[2,1,16384]{2,1,0:T(1,128)} %weights_ref.1) | copy-start | bytes 393220
  113.1 22.8 %all-to-all-start.3 = ((f32[256,1,256]{2,1,0:T(1,128)}), f32[256,1,256]{2,1,0:T(1,128)S(1)}, u32[]{:S(2)}, u32[]{:S(2)}) async-start(f32[256,1,256]{2,1,0:T(1,128)} %pack.1), calls=%async_computation.4 | async-start | bytes 524288 | tf_op jit(solution)/shard_map/all_to_all | solution.py:182
  137.2 10.3 %all-to-all-start.5 = ((f32[4,64,256]{2,1,0:T(8,128)}), f32[4,64,256]{2,1,0:T(8,128)S(1)}, u32[]{:S(2)}, u32[]{:S(2)}) async-start(f32[4,64,256]{2,1,0:T(8,128)} %bitcast.14), calls=%async_computation.6 | async-start | bytes 524288 | tf_op jit(solution)/shard_map/all_to_all | solution.py:188
  147.5 21.7 %all-to-all-start.6 = ((f32[256,1,256]{2,1,0:T(1,128)}), f32[256,1,256]{2,1,0:T(1,128)S(1)}, u32[]{:S(2)}, u32[]{:S(2)}) async-start(f32[256,1,256]{2,1,0:T(1,128)} %reshape.42), calls=%async_computation.7 | async-start | bytes 524288 | tf_op jit(solution)/shard_map/all_to_all | solution.py:194
Sparse Core Ops, SparseCore 0:
  23.2 46.9 reduce-scatter.1

commit v2 on v1

v2 whole, which is shorter than its diff:
```python
import math

import jax
import jax.numpy as jnp
from jax import lax
from jax.experimental import pallas as pl
from jax.experimental.pallas import tpu as pltpu
from jax.sharding import Mesh, PartitionSpec as P

HEADS = 64
RANK = 256
COLS = 256
L = 2
ITERS = 5
MATS = L * HEADS
CAP = 3
SPLIT = 48
REST = HEADS - SPLIT
NA = L * SPLIT
NB = L * REST
HALF = SPLIT // 2
NH = NA // 2
OWNERS = 64
DEVICES = 256
ALL = ("y", "z", "x", "core")

quintic_a = 3.4445
quintic_b = -4.775
quintic_c = 2.0315
momentum_beta = 0.95
learn_rate = 0.02
decay_rate = 0.1
rms_factor = 0.2
norm_epsilon = 1e-07
VMEM_LIMIT = 32 * 1024 * 1024

f32 = jnp.float32
bf16 = jnp.bfloat16


def targets(table):
    owners = table[:, 0]
    index = jnp.arange(MATS, dtype=jnp.int32)
    before = (owners[:, None] == owners[None, :]) & (index[:, None] < index[None, :])
    slots = jnp.sum(before.astype(jnp.int32), axis=0)
    return slots * OWNERS + owners


def vmem():
    return pl.BlockSpec(memory_space=pltpu.VMEM)


def smem():
    return pl.BlockSpec(memory_space=pltpu.SMEM)


def params():
    return pltpu.CompilerParams(vmem_limit_bytes=VMEM_LIMIT)


def lanes_of(head, half):
    return pl.ds(pl.multiple_of(head * COLS + half * 128, 128), 128)


def rows_of(block, size):
    return pl.ds(pl.multiple_of(block * size, size), size)


def x_bits():
    x = lax.axis_index("x")
    second = x // 2
    return (x + second) % 2, second


def split_kernel(grad_ref, cross_ref, b_ref):
    other = 1 - lax.axis_index("core")

    @pl.loop(0, REST // 2)
    def _(pair):
        head = SPLIT + 2 * pair
        for layer in range(L):
            for half in range(2):
                one = grad_ref[layer, :, lanes_of(head, half)].astype(f32)
                two = grad_ref[layer, :, lanes_of(head + 1, half)].astype(f32)
                at = rows_of(layer * (REST // 2) + pair, 16)
                for tile in range(8):
                    rows = slice(tile * 8, tile * 8 + 8)
                    b_ref[tile * 2 + half, at, :] = jnp.concatenate([one[rows], two[rows]], axis=0).astype(bf16)

    @pl.loop(0, SPLIT)
    def _(head):
        for layer in range(L):
            cross_ref[layer * SPLIT + head] = grad_ref[layer, :, lanes_of(head, other)]


def first_kernel(grad_ref, got_ref, send1_ref, keep1_ref, send2_ref, keep2_ref):
    core = lax.axis_index("core")
    one, two = x_bits()

    def total(layer, head, rows):
        mine = grad_ref[layer, rows, lanes_of(head, core)].astype(f32)
        return mine + got_ref[layer * SPLIT + head, rows, :].astype(f32)

    @pl.loop(0, HALF)
    def _(head):
        for layer in range(L):
            at = layer * HALF + head
            send1_ref[at] = total(layer, head, rows_of(1 - one, 32))
            keep1_ref[at] = total(layer, head, rows_of(one, 32))
            for block in range(2):
                rows = slice(block * 16, block * 16 + 16)
                send2_ref[at, rows, :] = total(layer, head + HALF, rows_of(2 * block + 1 - two, 16))
                keep2_ref[at, rows, :] = total(layer, head + HALF, rows_of(2 * block + two, 16))


def second_kernel(keep1_ref, got1_ref, keep2_ref, got2_ref, send1_ref, stay1_ref, send2_ref, stay2_ref):
    one, two = x_bits()

    @pl.loop(0, NH)
    def _(at):
        for rows, out in ((rows_of(1 - two, 16), send1_ref), (rows_of(two, 16), stay1_ref)):
            out[at] = keep1_ref[at, rows, :] + got1_ref[at, rows, :]
        for rows, out in ((rows_of(1 - one, 16), send2_ref), (rows_of(one, 16), stay2_ref)):
            out[at] = keep2_ref[at, rows, :] + got2_ref[at, rows, :]


def third_kernel(stay1_ref, got1_ref, stay2_ref, got2_ref, out_ref, total):
    total[: NH * 16, :] = (stay1_ref[...] + got1_ref[...]).reshape(NH * 16, 128)
    total[NH * 16 :, :] = (stay2_ref[...] + got2_ref[...]).reshape(NH * 16, 128)
    for pair in range(8):
        for e in range(2):
            out_ref[pair, e * NA : (e + 1) * NA, :] = total[pl.ds(2 * pair + e, NA, stride=16), :]


def b_kernel(part_ref, mom_ref, own_ref, near_ref, far_ref, across_ref, mom1_ref, mom2_ref, mom3_ref, total):
    total[...] = part_ref[0].astype(f32)
    for source in range(1, 16):
        total[...] += part_ref[source].astype(f32)
    x, y = lax.axis_index("x"), lax.axis_index("y")
    for pair, out in ((x, own_ref), (x + 1 - 2 * (x % 2), near_ref), (3 - x, far_ref), ((x + 2) % 4, across_ref)):
        for e in range(2):
            out[e * NB : (e + 1) * NB, :] = total[pl.ds(2 * pair + e, NB, stride=8), :]
    for step, out in ((1, mom1_ref), (2, mom2_ref), (3, mom3_ref)):
        out[...] = mom_ref[jnp.minimum((y + step) % 4, CAP - 1)]


def pack_kernel(target_ref, a_ref, own_ref, near_ref, far_ref, across_ref, out_ref, sum_a, sum_b):
    sum_a[...] = jnp.sum(a_ref[...], axis=0)
    sum_b[...] = (own_ref[...] + near_ref[...]) + (far_ref[...] + across_ref[...])
    out_ref[...] = jnp.zeros_like(out_ref)
    for layer in range(L):
        for head in range(HEADS):
            where = target_ref[layer * HEADS + head]
            for e in range(2):
                if head < HALF:
                    row = sum_a[pl.ds(e * NA + layer * HALF + head, 1), :]
                elif head < SPLIT:
                    row = sum_a[pl.ds(e * NA + NH + layer * HALF + head - HALF, 1), :]
                else:
                    row = sum_b[pl.ds(e * NB + layer * REST + head - SPLIT, 1), :]
                out_ref[pl.ds(where, 1), :, e * 128 : (e + 1) * 128] = row[None]


def halves(value):
    high = value.astype(bf16)
    return high, (value - high.astype(f32)).astype(bf16)


def times(left, right, transposed):
    dims = (((1,), (1 if transposed else 0,)), ((), ()))

    def dot(a, b):
        return lax.dot_general(a, b, dims, preferred_element_type=f32)

    (lh, ll), (rh, rl) = left, right
    return dot(lh, rh) + (dot(lh, rl) + dot(ll, rh))


def newton(advance):
    norm = jnp.sqrt(jnp.sum(advance * advance))
    iterate = advance / (norm + norm_epsilon)
    for _ in range(ITERS):
        parts = halves(iterate)
        gram = times(parts, parts, True)
        gram_parts = halves(gram)
        poly = quintic_b * gram + quintic_c * times(gram_parts, gram_parts, False)
        iterate = quintic_a * iterate + times(halves(poly), parts, False)
    return iterate


def work_kernel(target_ref, got_ref, held_ref, mom1_ref, mom2_ref, mom3_ref, out_ref, own_ref, new1_ref, new2_ref, new3_ref, grad, fresh, adv):
    y = lax.axis_index("y")
    me = y * OWNERS + (lax.axis_index("z") * 4 + lax.axis_index("x")) * 2 + lax.axis_index("core")
    index = lax.broadcasted_iota(jnp.int32, (1, MATS), 1)
    kind = jnp.where(target_ref[...] == me, jnp.where(index % HEADS < SPLIT, 2, 1), 0)
    kind = jnp.max(kind)

    @pl.when(kind == 2)
    def _():
        for block in range(4):
            for x, (one, two) in enumerate(((0, 0), (1, 0), (1, 1), (0, 1))):
                for half in range(2):
                    for e in range(2):
                        grad[half, pl.ds(block * 64 + one * 32 + two * 16 + e, 8, stride=2), :] = got_ref[
                            pl.ds(2 * (block * 64 + x * 2 + half) + e, 8, stride=16), :
                        ]

    @pl.when(kind != 2)
    def _():
        for block in range(4):
            for half in range(2):
                for e in range(2):
                    grad[half, pl.ds(block * 64 + e, 32, stride=2), :] = got_ref[pl.ds(2 * (block * 64 + half) + e, 32, stride=4), :]

    live = kind > 0
    for step, mom_ref in enumerate((None, mom1_ref, mom2_ref, mom3_ref)):
        rows = rows_of((y + 4 - step) % 4, 64)
        mom = held_ref[jnp.minimum(y, CAP - 1)] if mom_ref is None else mom_ref[...]
        for half in range(2):
            lanes = slice(half * 128, (half + 1) * 128)
            g = jnp.where(live, grad[half, rows, :], 0.0)
            new = jnp.where(live, momentum_beta * mom[:, lanes] + g, 0.0)
            fresh[rows, lanes] = new
            adv[rows, lanes] = g + momentum_beta * new
    for step, out in enumerate((own_ref, new1_ref, new2_ref, new3_ref)):
        out[...] = fresh[rows_of((y + step) % 4, 64), :]
    ortho = newton(adv[...])
    for half in range(2):
        out_ref[pl.ds(half, RANK, stride=2), :] = ortho[:, half * 128 : (half + 1) * 128]


def finish_kernel(target_ref, got_ref, weights_ref, own_ref, new1_ref, new2_ref, new3_ref, mom_ref, step_ref, new_ref):
    y = lax.axis_index("y")
    for step, ref in enumerate((own_ref, new1_ref, new2_ref, new3_ref)):
        slot = (y + 4 - step) % 4

        @pl.when(slot < CAP)
        def _(slot=slot, ref=ref):
            mom_ref[slot] = ref[...]

    scale = rms_factor * math.sqrt(max(RANK, COLS))
    for layer in range(L):
        for head in range(HEADS):
            where = target_ref[layer * HEADS + head]
            lanes = slice(head * COLS, (head + 1) * COLS)
            held = weights_ref[layer, :, lanes]
            step = scale * got_ref[pl.ds(where, 1), 0, :] + decay_rate * held
            step_ref[layer, :, lanes] = step
            new_ref[layer, :, lanes] = held - learn_rate * step


def shape(*dims, dtype=f32):
    return jax.ShapeDtypeStruct(dims, dtype)


def call(kernel, outs, ins, scratch=(), flops=0, moved=1 << 22):
    many = isinstance(outs, tuple)
    return pl.pallas_call(
        kernel,
        out_shape=outs,
        in_specs=[smem() if kind == "s" else vmem() for kind in ins],
        out_specs=tuple(vmem() for _ in outs) if many else vmem(),
        scratch_shapes=[pltpu.VMEM(dims, f32) for dims in scratch],
        compiler_params=params(),
        cost_estimate=pl.CostEstimate(flops=flops, bytes_accessed=moved, transcendentals=0),
        name=kernel.__name__.removesuffix("_kernel"),
    )


NEAR = [(i, i ^ 1) for i in range(4)]
FAR = [(i, 3 - i) for i in range(4)]
ACROSS = [(i, (i + 2) % 4) for i in range(4)]


def along_y(values):
    return [
        lax.ppermute(value, "y", [(i, (i + step) % 4) for i in range(4)]) for step, value in enumerate(values, start=1)
    ]


def on_device(gradient, momentum, weights, table):
    target = targets(table)
    local = gradient[0]

    cross, part_b = call(split_kernel, (shape(NA, 64, 128, dtype=bf16), shape(16, NB * 8, 128, dtype=bf16)), "v")(local)
    crossed = lax.ppermute(cross, "core", [(0, 1), (1, 0)])
    got_b = lax.all_to_all(part_b, ("z", "core"), 0, 0, tiled=True)
    send1, keep1, send2, keep2 = call(first_kernel, (shape(NH, 32, 128),) * 4, "vv")(local, crossed)
    got1, got2 = lax.ppermute(send1, "x", NEAR), lax.ppermute(send2, "x", FAR)
    send1, stay1, send2, stay2 = call(second_kernel, (shape(NH, 16, 128),) * 4, "vvvv")(keep1, got1, keep2, got2)
    got1, got2 = lax.ppermute(send1, "x", FAR), lax.ppermute(send2, "x", NEAR)
    send_a = call(third_kernel, shape(8, 2 * NA, 128), "vvvv", [(NA * 16, 128)])(stay1, got1, stay2, got2)
    last_a = lax.all_to_all(send_a, "z", 0, 0, tiled=True)

    outs = (shape(2 * NB, 128),) * 4 + (shape(64, COLS),) * 3
    own, near, far, across, *moms = call(b_kernel, outs, "vv", [(NB * 8, 128)])(got_b, momentum[0])
    near, far, across = lax.ppermute(near, "x", NEAR), lax.ppermute(far, "x", FAR), lax.ppermute(across, "x", ACROSS)
    moms = along_y(moms)

    outgoing = call(pack_kernel, shape(DEVICES, 1, COLS), "svvvvv", [(2 * NA, 128), (2 * NB, 128)])(
        target, last_a, own, near, far, across
    )
    got = lax.all_to_all(outgoing, ALL, 0, 0, tiled=True).reshape(2 * DEVICES, 128)
    outs = (shape(2 * RANK, 128),) + (shape(64, COLS),) * 4
    scratch = [(2, RANK, 128), (RANK, COLS), (RANK, COLS)]
    ortho, fresh, *news = call(work_kernel, outs, "vvvvvv", scratch, 15 * 3 * 2 * 256**3)(
        target.reshape(1, MATS), got, momentum[0], *moms
    )
    returned = lax.all_to_all(ortho.reshape(DEVICES, 1, COLS), ALL, 0, 0, tiled=True)
    news = along_y(news)
    outs = (shape(CAP, 64, COLS), shape(L, 1, HEADS * COLS), shape(L, 1, HEADS * COLS))
    new_momentum, step_update, new_weights = call(finish_kernel, outs, "svvvvvv")(target, returned, weights, fresh, *news)
    return new_momentum[None], step_update, new_weights


def solution(mesh):
    fine = Mesh(mesh.devices.reshape(8, 4, 2, 4), ("z", "x", "core", "y"))
    dp = ("z", "x", "core")
    return jax.shard_map(
        on_device,
        mesh=fine,
        in_specs=(
            P(dp, None, "y", None),
            P(dp, None, "y", None),
            P(None, ("y",) + dp, None),
            P(),
        ),
        out_specs=(
            P(dp, None, "y", None),
            P(None, ("y",) + dp, None),
            P(None, ("y",) + dp, None),
        ),
        check_vma=False,
    )
```

time: 178 us -> 136 us (0.76)
  blocking collectives: 41.4 us -> 0 us
  starting transfers between devices: 28.8 us -> 50.5 us
  between operations: 14.1 us -> 0.72 us
  local copies, waits for them, and re-layouts: 17.3 us -> 5.36 us
  other arithmetic: 7.23 us -> 0.11 us
  waiting for transfers between devices: 58.6 us -> 65.2 us
  Pallas kernels: 10.1 us -> 13.6 us
    all_to_all x1 -> x0, blocking collectives: 41.4 us -> none  [on_device(): got_b = lax.all_to_all(part_b, ('z', 'core'), 0, 0, tiled=True)]
    ppermute x0 -> x14, waiting for transfers between devices: none -> 36.1 us  [the longest x2 18.2 us: on_device(): got1, got2 = (lax.ppermute(send1, 'x', NEAR), lax.ppermute(send2, 'x', FAR))]
    ppermute x0 -> x14, starting transfers between devices: none -> 21.7 us  [the longest x6 10.1 us: along_y(): lax.ppermute(value, 'y', [(i, (i + step) % 4) for i in range(4)])]
    all_to_all x3 -> x1, waiting for transfers between devices: 7.86 us -> 0.01 us  [on_device(): got_b = lax.all_to_all(part_b, ('z', 'core'), 0, 0, tiled=True)]
    another operation x1 -> x0, local copies, waits for them, and re-layouts: 7.75 us -> none  [on_device(): local = gradient[0].reshape(L, 8, 8, HEADS, 2, 128)]
    all_to_all x1, waiting for transfers between devices: 21.9 us -> 14.5 us  [on_device(): last_a = lax.all_to_all(send_a, 'z', 0, 0, tiled=True)]
    all_to_all x1, waiting for transfers between devices: 14.7 us -> 7.29 us  [on_device(): lax.all_to_all(ortho.reshape(DEVICES, 1, COLS), ALL, 0, 0, tiled=True)]
    all_to_all x1, waiting for transfers between devices: 14.1 us -> 7.29 us  [on_device(): lax.all_to_all(outgoing, ALL, 0, 0, tiled=True).reshape(2 * DEVICES, 128)]
  transfers between devices with their start and end apart: 7 -> 18, of which waited for: 6 -> 11; matrix products, arithmetic and copies ran while one was open for 4% -> 0% of each run, Pallas kernels for 4% -> 2%
where the time goes in v2:
time: 136 us; the launch traced here: 135 us
  waiting for transfers between devices  65.2 us (48%)
  starting transfers between devices  50.5 us (37%)
  Pallas kernels  13.6 us (10%)
  local copies, waits for them, and re-layouts  5.36 us (4%)
    ppermute x2, waiting for transfers between devices, on_device(): got1, got2 = (lax.ppermute(send1, 'x', NEAR), lax.ppermute(send2, 'x', FAR))  18.2 us
    all_to_all x1, waiting for transfers between devices, on_device(): last_a = lax.all_to_all(send_a, 'z', 0, 0, tiled=True)  14.5 us
    ppermute x6, starting transfers between devices, along_y(): lax.ppermute(value, 'y', [(i, (i + step) % 4) for i in range(4)])  10.1 us
    all_to_all x1, starting transfers between devices, on_device(): lax.all_to_all(outgoing, ALL, 0, 0, tiled=True).reshape(2 * DEVICES, 128)  9.66 us
    ppermute x2, waiting for transfers between devices, on_device(): got1, got2 = (lax.ppermute(send1, 'x', FAR), lax.ppermute(send2, 'x', NEAR))  9.13 us
    all_to_all x1, waiting for transfers between devices, on_device(): lax.all_to_all(outgoing, ALL, 0, 0, tiled=True).reshape(2 * DEVICES, 128)  7.29 us
    all_to_all x1, waiting for transfers between devices, on_device(): lax.all_to_all(ortho.reshape(DEVICES, 1, COLS), ALL, 0, 0, tiled=True)  7.29 us
    all_to_all x1, starting transfers between devices, on_device(): got_b = lax.all_to_all(part_b, ('z', 'core'), 0, 0, tiled=True)  6.86 us
  transfers between devices with their start and end apart: 18, of which 11 were waited for; matrix products, arithmetic and copies ran while one was open for 0% of the time, Pallas kernels for 2%

profile of v2, /device:TPU:1, one launch (start us, length us, event | category | flops | bytes accessed | tf_op | source)
XLA Modules:
  0.0 135.5 jit_solution(12987272842682809073)
XLA Ops:
  0.6 2.2 %copy-done = bf16[1,2,64,16384]{3,2,1,0:T(8,128)(2,1)S(1)} copy-done((bf16[1,2,64,16384]{3,2,1,0:T(8,128)(2,1)S(1)}, bf16[1,2,64,16384]{3,2,1,0:T(8,128)(2,1)}, u32[]{:S(2)}) %copy-start) | copy-done | bytes 4194328
  2.8 2.1 %split.1 = (bf16[96,64,128]{2,1,0:T(8,128)(2,1)}, bf16[16,256,128]{2,1,0:T(8,128)(2,1)S(1)}) custom-call(bf16[2,64,16384]{2,1,0:T(8,128)(2,1)S(1)} %bitcast.11), custom_call_target="tpu_custom_call" | custom-call | bytes 4194304 | tf_op jit(solution)/shard_map/split/pallas_call | solution.py:285
  5.9 3.2 %collective-permute-start = (bf16[96,64,128]{2,1,0:T(8,128)(2,1)}, bf16[96,64,128]{2,1,0:T(8,128)(2,1)S(1)}, u32[]{:S(2)}, u32[]{:S(2)}) collective-permute-start(bf16[96,64,128]{2,1,0:T(8,128)(2,1)} %get-tuple-element.28), channel_id=1, source_target_pairs={{0,4},{4,0},{1,5},{5,1},{2,6},{6,2},{3,7},{7,3},{8,12},{12,8},{9,1... | collective-permute-start | bytes 4718600 | tf_op jit(solution)/shard_map/ppermute | solution.py:286
  9.2 6.9 %all-to-all-start.1 = ((bf16[16,256,128]{2,1,0:T(8,128)(2,1)}), bf16[16,256,128]{2,1,0:T(8,128)(2,1)S(1)}, u32[]{:S(2)}, u32[]{:S(2)}) async-start(bf16[16,256,128]{2,1,0:T(8,128)(2,1)} %copy-done.2), calls=%async_computation.1 | async-start | bytes 2097152 | tf_op jit(solution)/shard_map/all_to_all | solution.py:287
  16.1 2.2 %copy-done.1 = bf16[1,2,64,16384]{3,2,1,0:T(8,128)(2,1)S(1)} copy-done((bf16[1,2,64,16384]{3,2,1,0:T(8,128)(2,1)S(1)}, bf16[1,2,64,16384]{3,2,1,0:T(8,128)(2,1)}, u32[]{:S(2)}) %copy-start.1) | copy-done | bytes 4194328
  20.3 1.8 %collective-permute-start.2 = (f32[48,32,128]{2,1,0:T(8,128)S(1)}, f32[48,32,128]{2,1,0:T(8,128)S(1)}, u32[]{:S(2)}, u32[]{:S(2)}) collective-permute-start(f32[48,32,128]{2,1,0:T(8,128)S(1)} %get-tuple-element.32), channel_id=1, source_target_pairs={{0,24},{8,16},{16,8},{24,0},{1,25},{9,17},{17,9},{25,1},{2,26},{10... | collective-permute-start | bytes 2359304 | tf_op jit(solution)/shard_map/ppermute | solution.py:289
  22.1 16.1 %collective-permute-done.1.got1_ref = f32[48,32,128]{2,1,0:T(8,128)S(1)} collective-permute-done((f32[48,32,128]{2,1,0:T(8,128)S(1)}, f32[48,32,128]{2,1,0:T(8,128)S(1)}, u32[]{:S(2)}, u32[]{:S(2)}) %collective-permute-start.1) | collective-permute-done | bytes 786464 | tf_op jit(solution)/shard_map/ppermute | solution.py:289
  38.1 2.1 %collective-permute-done.2.got2_ref = f32[48,32,128]{2,1,0:T(8,128)S(1)} collective-permute-done((f32[48,32,128]{2,1,0:T(8,128)S(1)}, f32[48,32,128]{2,1,0:T(8,128)S(1)}, u32[]{:S(2)}, u32[]{:S(2)}) %collective-permute-start.2) | collective-permute-done | bytes 786464 | tf_op jit(solution)/shard_map/ppermute | solution.py:289
  40.8 1.9 %collective-permute-start.3 = (f32[48,16,128]{2,1,0:T(8,128)S(1)}, f32[48,16,128]{2,1,0:T(8,128)S(1)}, u32[]{:S(2)}, u32[]{:S(2)}) collective-permute-start(f32[48,16,128]{2,1,0:T(8,128)S(1)} %get-tuple-element.34), channel_id=1, source_target_pairs={{0,24},{8,16},{16,8},{24,0},{1,25},{9,17},{17,9},{25,1},{2,26},{10... | collective-permute-start | bytes 1179656 | tf_op jit(solution)/shard_map/ppermute | solution.py:291
  42.7 8.8 %collective-permute-done.3.got1_ref = f32[48,16,128]{2,1,0:T(8,128)S(1)} collective-permute-done((f32[48,16,128]{2,1,0:T(8,128)S(1)}, f32[48,16,128]{2,1,0:T(8,128)S(1)}, u32[]{:S(2)}, u32[]{:S(2)}) %collective-permute-start.3) | collective-permute-done | bytes 393248 | tf_op jit(solution)/shard_map/ppermute | solution.py:291
  53.1 5.9 %all-to-all-start = ((f32[8,192,128]{2,1,0:T(8,128)}), f32[8,192,128]{2,1,0:T(8,128)S(1)}, u32[]{:S(2)}, u32[]{:S(2)}) async-start(f32[8,192,128]{2,1,0:T(8,128)} %third.1), calls=%async_computation | async-start | bytes 1572864 | tf_op jit(solution)/shard_map/all_to_all | solution.py:293
  61.0 1.7 %collective-permute-start.7 = (f32[64,128]{1,0:T(8,128)S(1)}, f32[64,128]{1,0:T(8,128)S(1)}, u32[]{:S(2)}, u32[]{:S(2)}) collective-permute-start(f32[64,128]{1,0:T(8,128)S(1)} %get-tuple-element.41), channel_id=1, source_target_pairs={{0,16},{8,24},{16,0},{24,8},{1,17},{9,25},{17,1},{25,9},{2,18},{10... | collective-permute-start | bytes 98312 | tf_op jit(solution)/shard_map/ppermute | solution.py:297
  63.6 1.6 %collective-permute-done.7.across_ref = f32[64,128]{1,0:T(8,128)S(1)} collective-permute-done((f32[64,128]{1,0:T(8,128)S(1)}, f32[64,128]{1,0:T(8,128)S(1)}, u32[]{:S(2)}, u32[]{:S(2)}) %collective-permute-start.7) | collective-permute-done | bytes 32800 | tf_op jit(solution)/shard_map/ppermute | solution.py:297
  65.2 14.5 %all-to-all-done.a_ref = f32[8,192,128]{2,1,0:T(8,128)S(1)} async-done(((f32[8,192,128]{2,1,0:T(8,128)}), f32[8,192,128]{2,1,0:T(8,128)S(1)}, u32[]{:S(2)}, u32[]{:S(2)}) %all-to-all-start) | async-done | bytes 786464 | tf_op jit(solution)/shard_map/all_to_all | solution.py:293
  81.2 9.7 %all-to-all-start.2 = ((f32[256,1,256]{2,1,0:T(1,128)}), f32[256,1,256]{2,1,0:T(1,128)S(1)}, u32[]{:S(2)}, u32[]{:S(2)}) async-start(f32[256,1,256]{2,1,0:T(1,128)} %pack.1), calls=%async_computation.2 | async-start | bytes 524288 | tf_op jit(solution)/shard_map/all_to_all | solution.py:303
  92.3 2.4 %collective-permute-start.9 = (f32[64,256]{1,0:T(8,128)S(1)}, f32[64,256]{1,0:T(8,128)S(1)}, u32[]{:S(2)}, u32[]{:S(2)}) collective-permute-start(f32[64,256]{1,0:T(8,128)S(1)} %get-tuple-element.43), channel_id=1, source_target_pairs={{0,2},{1,3},{2,0},{3,1},{4,6},{5,7},{6,4},{7,5},{8,10},{9,11},{10,... | collective-permute-start | bytes 196616 | tf_op jit(solution)/shard_map/ppermute | solution.py:277
  95.9 3.1 %collective-permute-done.9.mom2_ref = f32[64,256]{1,0:T(8,128)S(1)} collective-permute-done((f32[64,256]{1,0:T(8,128)S(1)}, f32[64,256]{1,0:T(8,128)S(1)}, u32[]{:S(2)}, u32[]{:S(2)}) %collective-permute-start.9) | collective-permute-done | bytes 65568 | tf_op jit(solution)/shard_map/ppermute | solution.py:277
  99.0 7.3 %all-to-all-done.2 = f32[256,1,256]{2,1,0:T(1,128)S(1)} async-done(((f32[256,1,256]{2,1,0:T(1,128)}), f32[256,1,256]{2,1,0:T(1,128)S(1)}, u32[]{:S(2)}, u32[]{:S(2)}) %all-to-all-start.2) | async-done | bytes 262176 | tf_op jit(solution)/shard_map/all_to_all | solution.py:303
  106.3 5.8 %work.1 = (f32[512,128]{1,0:T(8,128)}, f32[64,256]{1,0:T(8,128)S(1)}, f32[64,256]{1,0:T(8,128)S(1)}, f32[64,256]{1,0:T(8,128)S(1)}, f32[64,256]{1,0:T(8,128)S(1)}) custom-call(s32[1,128]{1,0:T(1,128)S(1)} %bitcast_add_fusion.target_ref, f32[512,128]{1,0:T(8,128)S(1)} %bitcast.13, f32[3,64,256]{2,1,0:T(8,128)S(1)} %bitcast.15, ...), custom_call_target="tpu_custom_call" | custom-call | flops 1509949440 | bytes 4194304 | tf_op jit(solution)/shard_map/work/pallas_call | solution.py:306
  112.1 6.4 %all-to-all-start.3 = ((f32[256,1,256]{2,1,0:T(1,128)}), f32[256,1,256]{2,1,0:T(1,128)S(1)}, u32[]{:S(2)}, u32[]{:S(2)}) async-start(f32[256,1,256]{2,1,0:T(1,128)} %bitcast.6), calls=%async_computation.3 | async-start | bytes 524288 | tf_op jit(solution)/shard_map/all_to_all | solution.py:309
  120.0 2.4 %collective-permute-start.12 = (f32[64,256]{1,0:T(8,128)S(1)}, f32[64,256]{1,0:T(8,128)S(1)}, u32[]{:S(2)}, u32[]{:S(2)}) collective-permute-start(f32[64,256]{1,0:T(8,128)S(1)} %get-tuple-element.48), channel_id=1, source_target_pairs={{0,2},{1,3},{2,0},{3,1},{4,6},{5,7},{6,4},{7,5},{8,10},{9,11},{10,... | collective-permute-start | bytes 196616 | tf_op jit(solution)/shard_map/ppermute | solution.py:277
  123.6 3.1 %collective-permute-done.12.new2_ref = f32[64,256]{1,0:T(8,128)S(1)} collective-permute-done((f32[64,256]{1,0:T(8,128)S(1)}, f32[64,256]{1,0:T(8,128)S(1)}, u32[]{:S(2)}, u32[]{:S(2)}) %collective-permute-start.12) | collective-permute-done | bytes 65568 | tf_op jit(solution)/shard_map/ppermute | solution.py:277
  126.7 7.3 %all-to-all-done.3.got_ref = f32[256,1,256]{2,1,0:T(1,128)S(1)} async-done(((f32[256,1,256]{2,1,0:T(1,128)}), f32[256,1,256]{2,1,0:T(1,128)S(1)}, u32[]{:S(2)}, u32[]{:S(2)}) %all-to-all-start.3) | async-done | bytes 262176 | tf_op jit(solution)/shard_map/all_to_all | solution.py:309
  134.0 1.5 %finish.1 = (f32[3,64,256]{2,1,0:T(8,128)}, f32[2,1,16384]{2,1,0:T(1,128)}, f32[2,1,16384]{2,1,0:T(1,128)}) custom-call(s32[128]{0:T(128)S(1)} %multiply_add_fusion.target_ref, f32[256,1,256]{2,1,0:T(1,128)S(1)} %all-to-all-done.3.got_ref, f32[2,1,16384]{2,1,0:T(1,128)S(1)} %copy-done.4, f32[64,256]{1,0:T(8,128)S(1)} %get-tuple-element.46.own_ref, ...), custom_call_target="tpu_custom_call" | custom-call | bytes 4194304 | tf_op jit(solution)/shard_map/finish/pallas_call | solution.py:312
  (35 shorter events, 14.8 us)
Async XLA Ops:
  0.6 2.2 %copy-start = (bf16[1,2,64,16384]{3,2,1,0:T(8,128)(2,1)S(1)}, bf16[1,2,64,16384]{3,2,1,0:T(8,128)(2,1)}, u32[]{:S(2)}) copy-start(bf16[1,2,64,16384]{3,2,1,0:T(8,128)(2,1)} %param.4) | copy-start | bytes 12582916
  5.0 1.0 copy-start.2
  5.9 10.1 %collective-permute-start = (bf16[96,64,128]{2,1,0:T(8,128)(2,1)}, bf16[96,64,128]{2,1,0:T(8,128)(2,1)S(1)}, u32[]{:S(2)}, u32[]{:S(2)}) collective-permute-start(bf16[96,64,128]{2,1,0:T(8,128)(2,1)} %get-tuple-element.28), channel_id=1, source_target_pairs={{0,4},{4,0},{1,5},{5,1},{2,6},{6,2},{3,7},{7,3},{8,12},{12,8},{9,1... | collective-permute-start | bytes 4718600 | tf_op jit(solution)/shard_map/ppermute | solution.py:286
  9.2 43.9 %all-to-all-start.1 = ((bf16[16,256,128]{2,1,0:T(8,128)(2,1)}), bf16[16,256,128]{2,1,0:T(8,128)(2,1)S(1)}, u32[]{:S(2)}, u32[]{:S(2)}) async-start(bf16[16,256,128]{2,1,0:T(8,128)(2,1)} %copy-done.2), calls=%async_computation.1 | async-start | bytes 2097152 | tf_op jit(solution)/shard_map/all_to_all | solution.py:287
  16.0 2.2 %copy-start.1 = (bf16[1,2,64,16384]{3,2,1,0:T(8,128)(2,1)S(1)}, bf16[1,2,64,16384]{3,2,1,0:T(8,128)(2,1)}, u32[]{:S(2)}) copy-start(bf16[1,2,64,16384]{3,2,1,0:T(8,128)(2,1)} %param.4) | copy-start | bytes 12582916
  18.9 19.2 %collective-permute-start.1 = (f32[48,32,128]{2,1,0:T(8,128)S(1)}, f32[48,32,128]{2,1,0:T(8,128)S(1)}, u32[]{:S(2)}, u32[]{:S(2)}) collective-permute-start(f32[48,32,128]{2,1,0:T(8,128)S(1)} %get-tuple-element.30), channel_id=1, source_target_pairs={{0,8},{8,0},{16,24},{24,16},{1,9},{9,1},{17,25},{25,17},{2,10},{10... | collective-permute-start | bytes 2359304 | tf_op jit(solution)/shard_map/ppermute | solution.py:289
  20.3 20.0 %collective-permute-start.2 = (f32[48,32,128]{2,1,0:T(8,128)S(1)}, f32[48,32,128]{2,1,0:T(8,128)S(1)}, u32[]{:S(2)}, u32[]{:S(2)}) collective-permute-start(f32[48,32,128]{2,1,0:T(8,128)S(1)} %get-tuple-element.32), channel_id=1, source_target_pairs={{0,24},{8,16},{16,8},{24,0},{1,25},{9,17},{17,9},{25,1},{2,26},{10... | collective-permute-start | bytes 2359304 | tf_op jit(solution)/shard_map/ppermute | solution.py:289
  40.8 10.7 %collective-permute-start.3 = (f32[48,16,128]{2,1,0:T(8,128)S(1)}, f32[48,16,128]{2,1,0:T(8,128)S(1)}, u32[]{:S(2)}, u32[]{:S(2)}) collective-permute-start(f32[48,16,128]{2,1,0:T(8,128)S(1)} %get-tuple-element.34), channel_id=1, source_target_pairs={{0,24},{8,16},{16,8},{24,0},{1,25},{9,17},{17,9},{25,1},{2,26},{10... | collective-permute-start | bytes 1179656 | tf_op jit(solution)/shard_map/ppermute | solution.py:291
  42.7 9.1 %collective-permute-start.4 = (f32[48,16,128]{2,1,0:T(8,128)S(1)}, f32[48,16,128]{2,1,0:T(8,128)S(1)}, u32[]{:S(2)}, u32[]{:S(2)}) collective-permute-start(f32[48,16,128]{2,1,0:T(8,128)S(1)} %get-tuple-element.36), channel_id=1, source_target_pairs={{0,8},{8,0},{16,24},{24,16},{1,9},{9,1},{17,25},{25,17},{2,10},{10... | collective-permute-start | bytes 1179656 | tf_op jit(solution)/shard_map/ppermute | solution.py:291
  51.8 7.1 %copy-start.5 = (s32[128,1]{0,1:T(1,128)S(1)}, s32[128,1]{0,1:T(1,128)}, u32[]{:S(2)}) copy-start(s32[128,1]{0,1:T(1,128)} %param.7) | copy-start | bytes 1540
  51.8 7.2 %copy-start.3 = (f32[1,3,64,256]{3,2,1,0:T(8,128)S(1)}, f32[1,3,64,256]{3,2,1,0:T(8,128)}, u32[]{:S(2)}) copy-start(f32[1,3,64,256]{3,2,1,0:T(8,128)} %param.5) | copy-start | bytes 589828
  53.1 26.6 %all-to-all-start = ((f32[8,192,128]{2,1,0:T(8,128)}), f32[8,192,128]{2,1,0:T(8,128)S(1)}, u32[]{:S(2)}, u32[]{:S(2)}) async-start(f32[8,192,128]{2,1,0:T(8,128)} %third.1), calls=%async_computation | async-start | bytes 1572864 | tf_op jit(solution)/shard_map/all_to_all | solution.py:293
  59.3 3.3 %collective-permute-start.5 = (f32[64,128]{1,0:T(8,128)S(1)}, f32[64,128]{1,0:T(8,128)S(1)}, u32[]{:S(2)}, u32[]{:S(2)}) collective-permute-start(f32[64,128]{1,0:T(8,128)S(1)} %get-tuple-element.39), channel_id=1, source_target_pairs={{0,8},{8,0},{16,24},{24,16},{1,9},{9,1},{17,25},{25,17},{2,10},{10... | collective-permute-start | bytes 98312 | tf_op jit(solution)/shard_map/ppermute | solution.py:297
  59.7 4.0 %collective-permute-start.6 = (f32[64,128]{1,0:T(8,128)S(1)}, f32[64,128]{1,0:T(8,128)S(1)}, u32[]{:S(2)}, u32[]{:S(2)}) collective-permute-start(f32[64,128]{1,0:T(8,128)S(1)} %get-tuple-element.40), channel_id=1, source_target_pairs={{0,24},{8,16},{16,8},{24,0},{1,25},{9,17},{17,9},{25,1},{2,26},{10... | collective-permute-start | bytes 98312 | tf_op jit(solution)/shard_map/ppermute | solution.py:297
  61.0 4.3 %collective-permute-start.7 = (f32[64,128]{1,0:T(8,128)S(1)}, f32[64,128]{1,0:T(8,128)S(1)}, u32[]{:S(2)}, u32[]{:S(2)}) collective-permute-start(f32[64,128]{1,0:T(8,128)S(1)} %get-tuple-element.41), channel_id=1, source_target_pairs={{0,16},{8,24},{16,0},{24,8},{1,17},{9,25},{17,1},{25,9},{2,18},{10... | collective-permute-start | bytes 98312 | tf_op jit(solution)/shard_map/ppermute | solution.py:297
  81.2 25.1 %all-to-all-start.2 = ((f32[256,1,256]{2,1,0:T(1,128)}), f32[256,1,256]{2,1,0:T(1,128)S(1)}, u32[]{:S(2)}, u32[]{:S(2)}) async-start(f32[256,1,256]{2,1,0:T(1,128)} %pack.1), calls=%async_computation.2 | async-start | bytes 524288 | tf_op jit(solution)/shard_map/all_to_all | solution.py:303
  90.8 5.1 %collective-permute-start.8 = (f32[64,256]{1,0:T(8,128)S(1)}, f32[64,256]{1,0:T(8,128)S(1)}, u32[]{:S(2)}, u32[]{:S(2)}) collective-permute-start(f32[64,256]{1,0:T(8,128)S(1)} %get-tuple-element.42), channel_id=1, source_target_pairs={{0,1},{1,2},{2,3},{3,0},{4,5},{5,6},{6,7},{7,4},{8,9},{9,10},{10,1... | collective-permute-start | bytes 196616 | tf_op jit(solution)/shard_map/ppermute | solution.py:277
  92.3 6.7 %collective-permute-start.9 = (f32[64,256]{1,0:T(8,128)S(1)}, f32[64,256]{1,0:T(8,128)S(1)}, u32[]{:S(2)}, u32[]{:S(2)}) collective-permute-start(f32[64,256]{1,0:T(8,128)S(1)} %get-tuple-element.43), channel_id=1, source_target_pairs={{0,2},{1,3},{2,0},{3,1},{4,6},{5,7},{6,4},{7,5},{8,10},{9,11},{10,... | collective-permute-start | bytes 196616 | tf_op jit(solution)/shard_map/ppermute | solution.py:277
  94.7 4.2 %collective-permute-start.10 = (f32[64,256]{1,0:T(8,128)S(1)}, f32[64,256]{1,0:T(8,128)S(1)}, u32[]{:S(2)}, u32[]{:S(2)}) collective-permute-start(f32[64,256]{1,0:T(8,128)S(1)} %get-tuple-element.44), channel_id=1, source_target_pairs={{0,3},{1,0},{2,1},{3,2},{4,7},{5,4},{6,5},{7,6},{8,11},{9,8},{10,9... | collective-permute-start | bytes 196616 | tf_op jit(solution)/shard_map/ppermute | solution.py:277
  106.3 27.7 %copy-start.4 = (f32[2,1,16384]{2,1,0:T(1,128)S(1)}, f32[2,1,16384]{2,1,0:T(1,128)}, u32[]{:S(2)}) copy-start(f32[2,1,16384]{2,1,0:T(1,128)} %weights_ref.1) | copy-start | bytes 393220
  112.1 21.9 %all-to-all-start.3 = ((f32[256,1,256]{2,1,0:T(1,128)}), f32[256,1,256]{2,1,0:T(1,128)S(1)}, u32[]{:S(2)}, u32[]{:S(2)}) async-start(f32[256,1,256]{2,1,0:T(1,128)} %bitcast.6), calls=%async_computation.3 | async-start | bytes 524288 | tf_op jit(solution)/shard_map/all_to_all | solution.py:309
  118.5 5.0 %collective-permute-start.11 = (f32[64,256]{1,0:T(8,128)S(1)}, f32[64,256]{1,0:T(8,128)S(1)}, u32[]{:S(2)}, u32[]{:S(2)}) collective-permute-start(f32[64,256]{1,0:T(8,128)S(1)} %get-tuple-element.47), channel_id=1, source_target_pairs={{0,1},{1,2},{2,3},{3,0},{4,5},{5,6},{6,7},{7,4},{8,9},{9,10},{10,1... | collective-permute-start | bytes 196616 | tf_op jit(solution)/shard_map/ppermute | solution.py:277
  120.0 6.7 %collective-permute-start.12 = (f32[64,256]{1,0:T(8,128)S(1)}, f32[64,256]{1,0:T(8,128)S(1)}, u32[]{:S(2)}, u32[]{:S(2)}) collective-permute-start(f32[64,256]{1,0:T(8,128)S(1)} %get-tuple-element.48), channel_id=1, source_target_pairs={{0,2},{1,3},{2,0},{3,1},{4,6},{5,7},{6,4},{7,5},{8,10},{9,11},{10,... | collective-permute-start | bytes 196616 | tf_op jit(solution)/shard_map/ppermute | solution.py:277
  122.4 4.2 %collective-permute-start.13 = (f32[64,256]{1,0:T(8,128)S(1)}, f32[64,256]{1,0:T(8,128)S(1)}, u32[]{:S(2)}, u32[]{:S(2)}) collective-permute-start(f32[64,256]{1,0:T(8,128)S(1)} %get-tuple-element.49), channel_id=1, source_target_pairs={{0,3},{1,0},{2,1},{3,2},{4,7},{5,4},{6,5},{7,6},{8,11},{9,8},{10,9... | collective-permute-start | bytes 196616 | tf_op jit(solution)/shard_map/ppermute | solution.py:277

commit v3 on v2

v3 whole, which is shorter than its diff:
```python
import math

import jax
import jax.numpy as jnp
from jax import lax
from jax.experimental import pallas as pl
from jax.experimental.pallas import tpu as pltpu
from jax.sharding import Mesh, PartitionSpec as P

HEADS = 64
RANK = 256
COLS = 256
L = 2
ITERS = 5
MATS = L * HEADS
CAP = 3
GROUP = HEADS // 4
NG = L * GROUP
OWNERS = 64
DEVICES = 256
ALL = ("y", "z", "x", "core")

quintic_a = 3.4445
quintic_b = -4.775
quintic_c = 2.0315
momentum_beta = 0.95
learn_rate = 0.02
decay_rate = 0.1
rms_factor = 0.2
norm_epsilon = 1e-07
VMEM_LIMIT = 32 * 1024 * 1024

f32 = jnp.float32
bf16 = jnp.bfloat16


def targets(table):
    owners = table[:, 0]
    index = jnp.arange(MATS, dtype=jnp.int32)
    before = (owners[:, None] == owners[None, :]) & (index[:, None] < index[None, :])
    slots = jnp.sum(before.astype(jnp.int32), axis=0)
    return slots * OWNERS + owners


def params():
    return pltpu.CompilerParams(vmem_limit_bytes=VMEM_LIMIT)


def lanes_of(head, half):
    return pl.ds(pl.multiple_of(head * COLS + half * 128, 128), 128)


def rows_of(block, size):
    return pl.ds(pl.multiple_of(block * size, size), size)


def bits():
    x = lax.axis_index("x")
    second = x // 2
    return (x + second) % 2, second, lax.axis_index("z") % 2


def cross_kernel(grad_ref, cross_ref):
    other = 1 - lax.axis_index("core")

    @pl.loop(0, HEADS)
    def _(head):
        for layer in range(L):
            cross_ref[layer * HEADS + head] = grad_ref[layer, :, lanes_of(head, other)]


def first_kernel(grad_ref, got_ref, mom_ref, *refs):
    send1, keep1, send2, keep2, send3, keep3, send4, keep4, mom1, mom2, mom3 = refs
    core = lax.axis_index("core")
    one, two, three = bits()

    def total(layer, head, rows):
        mine = grad_ref[layer, rows, lanes_of(head, core)].astype(f32)
        return mine + got_ref[layer * HEADS + head, rows, :].astype(f32)

    @pl.loop(0, GROUP)
    def _(head):
        for layer in range(L):
            at = layer * GROUP + head
            send1[at] = total(layer, head, rows_of(1 - one, 32))
            keep1[at] = total(layer, head, rows_of(one, 32))
            for block in range(2):
                rows = slice(block * 16, block * 16 + 16)
                send2[at, rows, :] = total(layer, GROUP + head, rows_of(2 * block + 1 - two, 16))
                keep2[at, rows, :] = total(layer, GROUP + head, rows_of(2 * block + two, 16))
            for group, send, keep in ((2, send3, keep3), (3, send4, keep4)):
                for block in range(4):
                    rows = slice(block * 8, block * 8 + 8)
                    both = total(layer, group * GROUP + head, slice(block * 16, block * 16 + 16))
                    send[at, rows, :] = jnp.where(three == 0, both[8:], both[:8])
                    keep[at, rows, :] = jnp.where(three == 0, both[:8], both[8:])

    y = lax.axis_index("y")
    for step, out in ((1, mom1), (2, mom2), (3, mom3)):
        out[...] = mom_ref[jnp.minimum((y + step) % 4, CAP - 1)]


def second_kernel(*refs):
    one, two, three = bits()
    keeps, gots, sends, stays = refs[0:4], refs[4:8], refs[8:12], refs[12:16]

    @pl.loop(0, NG)
    def _(at):
        for group, bit in ((0, three), (1, three), (3, two)):
            for block in range(2):
                rows = slice(block * 8, block * 8 + 8)
                for value, outs in ((1 - bit, sends), (bit, stays)):
                    here = rows_of(2 * block + value, 8)
                    outs[group][at, rows, :] = keeps[group][at, here, :] + gots[group][at, here, :]
        for value, outs in ((1 - one, sends), (one, stays)):
            here = rows_of(value, 16)
            outs[2][at] = keeps[2][at, here, :] + gots[2][at, here, :]


def third_kernel(*refs):
    one, two, _ = bits()
    stays, gots, (send_far, keep_far, send_near, keep_near) = refs[0:4], refs[4:8], refs[8:12]

    @pl.loop(0, NG)
    def _(at):
        for group, bit, send, keep in ((0, two, send_far, keep_far), (2, two, send_far, keep_far), (1, one, send_near, keep_near), (3, one, send_near, keep_near)):
            to = (group // 2) * NG + at
            for value, out in ((1 - bit, send), (bit, keep)):
                here = rows_of(value, 8)
                out[to] = stays[group][at, here, :] + gots[group][at, here, :]


def pack_kernel(target_ref, far_ref, got_far_ref, near_ref, got_near_ref, out_ref):
    out_ref[...] = jnp.zeros_like(out_ref)
    for layer in range(L):
        for head in range(HEADS):
            where = target_ref[layer * HEADS + head]
            group = head // GROUP
            at = (group // 2) * NG + layer * GROUP + head % GROUP
            kept, got = (far_ref, got_far_ref) if group % 2 == 0 else (near_ref, got_near_ref)
            out_ref[where] = kept[at] + got[at]


def halves(value):
    high = value.astype(bf16)
    return high, (value - high.astype(f32)).astype(bf16)


def times(left, right, transposed):
    dims = (((1,), (1 if transposed else 0,)), ((), ()))

    def dot(a, b):
        return lax.dot_general(a, b, dims, preferred_element_type=f32)

    (lh, ll), (rh, rl) = left, right
    return dot(lh, rh) + (dot(lh, rl) + dot(ll, rh))


def newton(advance):
    norm = jnp.sqrt(jnp.sum(advance * advance))
    iterate = advance / (norm + norm_epsilon)
    for _ in range(ITERS):
        parts = halves(iterate)
        gram = times(parts, parts, True)
        gram_parts = halves(gram)
        poly = quintic_b * gram + quintic_c * times(gram_parts, gram_parts, False)
        iterate = quintic_a * iterate + times(halves(poly), parts, False)
    return iterate


def work_kernel(target_ref, got_ref, held_ref, mom1_ref, mom2_ref, mom3_ref, out_ref, own_ref, new1_ref, new2_ref, new3_ref, fresh, adv):
    y = lax.axis_index("y")
    me = y * OWNERS + (lax.axis_index("z") * 4 + lax.axis_index("x")) * 2 + lax.axis_index("core")
    live = jnp.max(jnp.where(target_ref[...] == me, 1, 0)) > 0
    for step, mom_ref in enumerate((None, mom1_ref, mom2_ref, mom3_ref)):
        block = (y + 4 - step) % 4
        for x, (one, two) in enumerate(((0, 0), (1, 0), (1, 1), (0, 1))):
            for three in range(2):
                tile = 4 * one + 2 * two + three
                for half in range(2):
                    lanes = slice(half * 128, (half + 1) * 128)
                    parts = [got_ref[block * 64 + (z * 4 + x) * 2 + half] for z in range(three, 8, 2)]
                    g = jnp.where(live, (parts[0] + parts[1]) + (parts[2] + parts[3]), 0.0)
                    if mom_ref is None:
                        mom = held_ref[jnp.minimum(y, CAP - 1), tile * 8 : tile * 8 + 8, lanes]
                    else:
                        mom = mom_ref[tile * 8 : tile * 8 + 8, lanes]
                    new = jnp.where(live, momentum_beta * mom + g, 0.0)
                    rows = rows_of(block * 8 + tile, 8)
                    fresh[rows, lanes] = new
                    adv[rows, lanes] = g + momentum_beta * new
    for step, out in enumerate((own_ref, new1_ref, new2_ref, new3_ref)):
        out[...] = fresh[rows_of((y + step) % 4, 64), :]
    ortho = newton(adv[...])
    for half in range(2):
        out_ref[pl.ds(half, RANK, stride=2), :] = ortho[:, half * 128 : (half + 1) * 128]


def finish_kernel(target_ref, got_ref, weights_ref, own_ref, new1_ref, new2_ref, new3_ref, mom_ref, step_ref, new_ref):
    y = lax.axis_index("y")
    for step, ref in enumerate((own_ref, new1_ref, new2_ref, new3_ref)):
        slot = (y + 4 - step) % 4

        @pl.when(slot < CAP)
        def _(slot=slot, ref=ref):
            mom_ref[slot] = ref[...]

    scale = rms_factor * math.sqrt(max(RANK, COLS))
    for layer in range(L):
        for head in range(HEADS):
            where = target_ref[layer * HEADS + head]
            lanes = slice(head * COLS, (head + 1) * COLS)
            held = weights_ref[layer, :, lanes]
            step = scale * got_ref[pl.ds(where, 1), 0, :] + decay_rate * held
            step_ref[layer, :, lanes] = step
            new_ref[layer, :, lanes] = held - learn_rate * step


def shape(*dims, dtype=f32):
    return jax.ShapeDtypeStruct(dims, dtype)


def call(kernel, outs, ins, scratch=(), flops=0, moved=1 << 22):
    many = isinstance(outs, tuple)
    out_spec = pl.BlockSpec(memory_space=pltpu.VMEM)
    return pl.pallas_call(
        kernel,
        out_shape=outs,
        in_specs=[pl.BlockSpec(memory_space=pltpu.SMEM if kind == "s" else pltpu.VMEM) for kind in ins],
        out_specs=tuple(out_spec for _ in outs) if many else out_spec,
        scratch_shapes=[pltpu.VMEM(dims, f32) for dims in scratch],
        compiler_params=params(),
        cost_estimate=pl.CostEstimate(flops=flops, bytes_accessed=moved, transcendentals=0),
        name=kernel.__name__.removesuffix("_kernel"),
    )


NEAR = [(i, i ^ 1) for i in range(4)]
FAR = [(i, 3 - i) for i in range(4)]
PAIR = [(i, i ^ 1) for i in range(8)]
LINK = [(i, (i + 1 if i % 2 else i - 1) % 8) for i in range(8)]


def along_y(values):
    return [
        lax.ppermute(value, "y", [(i, (i + step) % 4) for i in range(4)]) for step, value in enumerate(values, start=1)
    ]


def on_device(gradient, momentum, weights, table):
    target = targets(table)
    local = gradient[0]

    cross = call(cross_kernel, shape(MATS, 64, 128, dtype=bf16), "v")(local)
    crossed = lax.ppermute(cross, "core", [(0, 1), (1, 0)])
    outs = (shape(NG, 32, 128),) * 8 + (shape(64, COLS),) * 3
    *parts, mom1, mom2, mom3 = call(first_kernel, outs, "vvv")(local, crossed, momentum[0])
    sends, keeps = parts[0::2], parts[1::2]
    moves = (("x", NEAR), ("x", FAR), ("z", PAIR), ("z", LINK))
    gots = [lax.ppermute(value, *move) for value, move in zip(sends, moves)]
    moms = along_y((mom1, mom2, mom3))

    parts = call(second_kernel, (shape(NG, 16, 128),) * 8, "v" * 8)(*keeps, *gots)
    sends, stays = parts[:4], parts[4:]
    moves = (("z", PAIR), ("z", LINK), ("x", NEAR), ("x", FAR))
    gots = [lax.ppermute(value, *move) for value, move in zip(sends, moves)]

    send_far, keep_far, send_near, keep_near = call(third_kernel, (shape(2 * NG, 8, 128),) * 4, "v" * 8)(*stays, *gots)
    got_far, got_near = lax.ppermute(send_far, "x", FAR), lax.ppermute(send_near, "x", NEAR)

    outgoing = call(pack_kernel, shape(DEVICES, 8, 128), "svvvv")(target, keep_far, got_far, keep_near, got_near)
    got = lax.all_to_all(outgoing, ALL, 0, 0, tiled=True)
    outs = (shape(2 * RANK, 128),) + (shape(64, COLS),) * 4
    ortho, fresh, *news = call(work_kernel, outs, "vvvvvv", [(RANK, COLS), (RANK, COLS)], 15 * 3 * 2 * 256**3)(
        target.reshape(1, MATS), got, momentum[0], *moms
    )
    returned = lax.all_to_all(ortho.reshape(DEVICES, 1, COLS), ALL, 0, 0, tiled=True)
    news = along_y(news)
    outs = (shape(CAP, 64, COLS), shape(L, 1, HEADS * COLS), shape(L, 1, HEADS * COLS))
    new_momentum, step_update, new_weights = call(finish_kernel, outs, "svvvvvv")(target, returned, weights, fresh, *news)
    return new_momentum[None], step_update, new_weights


def solution(mesh):
    fine = Mesh(mesh.devices.reshape(8, 4, 2, 4), ("z", "x", "core", "y"))
    dp = ("z", "x", "core")
    return jax.shard_map(
        on_device,
        mesh=fine,
        in_specs=(
            P(dp, None, "y", None),
            P(dp, None, "y", None),
            P(None, ("y",) + dp, None),
            P(),
        ),
        out_specs=(
            P(dp, None, "y", None),
            P(None, ("y",) + dp, None),
            P(None, ("y",) + dp, None),
        ),
        check_vma=False,
    )
```

time: 136 us -> 123 us (0.904)
  starting transfers between devices: 50.5 us -> 45 us
  local copies, waits for them, and re-layouts: 5.36 us -> 2.19 us
  waiting for transfers between devices: 65.2 us -> 62.5 us
  Pallas kernels: 13.6 us -> 12.1 us
    all_to_all x3 -> x1, starting transfers between devices: 22.4 us -> 12.7 us  [on_device(): got = lax.all_to_all(outgoing, ALL, 0, 0, tiled=True)]
    ppermute x7 -> x10, waiting for transfers between devices: 29.9 us -> 22.3 us  [the longest x8 16.9 us: on_device(): gots = [lax.ppermute(value, *move) for value, move in zip(sends, moves)]]
    ppermute x7 -> x10, starting transfers between devices: 8.38 us -> 12.5 us  [the longest x8 11.4 us: on_device(): gots = [lax.ppermute(value, *move) for value, move in zip(sends, moves)]]
    ppermute x1, waiting for transfers between devices: 0.01 us -> 3.79 us  [on_device(): crossed = lax.ppermute(cross, 'core', [(0, 1), (1, 0)])]
    unnamed x12 -> x8, local copies, waits for them, and re-layouts: 5.36 us -> 2.19 us
    pallas_call x7 -> x6, Pallas kernels: 12.1 us -> 10.6 us  [the longest x1 5.74 us: on_device(): call(work_kernel, outs, 'vvvvvv', [(RANK, COLS), (RANK, COLS)], 15 * 3 *...]
    all_to_all x3 -> x1, waiting for transfers between devices: 21.8 us -> 21.7 us  [on_device(): got = lax.all_to_all(outgoing, ALL, 0, 0, tiled=True)]
  transfers between devices with their start and end apart: 18 -> 19, of which waited for: 11 -> 14; matrix products, arithmetic and copies ran while one was open for 0% -> 0% of each run, Pallas kernels for 2% -> 0%
where the time goes in v3:
time: 123 us
  waiting for transfers between devices  62.5 us (51%)
  starting transfers between devices  45 us (37%)
  Pallas kernels  12.1 us (10%)
  local copies, waits for them, and re-layouts  2.19 us (2%)
    all_to_all x1, waiting for transfers between devices, on_device(): got = lax.all_to_all(outgoing, ALL, 0, 0, tiled=True)  21.7 us
    ppermute x8, waiting for transfers between devices, on_device(): gots = [lax.ppermute(value, *move) for value, move in zip(sends, moves)]  16.9 us
    all_to_all x1, starting transfers between devices, on_device(): got = lax.all_to_all(outgoing, ALL, 0, 0, tiled=True)  12.7 us
    ppermute x8, starting transfers between devices, on_device(): gots = [lax.ppermute(value, *move) for value, move in zip(sends, moves)]  11.4 us
    ppermute x6, starting transfers between devices, along_y(): lax.ppermute(value, 'y', [(i, (i + step) % 4) for i in range(4)])  10.1 us
    ppermute x6, waiting for transfers between devices, along_y(): lax.ppermute(value, 'y', [(i, (i + step) % 4) for i in range(4)])  7.44 us
    all_to_all x1, waiting for transfers between devices, on_device(): lax.all_to_all(ortho.reshape(DEVICES, 1, COLS), ALL, 0, 0, tiled=True)  7.29 us
    all_to_all x1, starting transfers between devices, on_device(): lax.all_to_all(ortho.reshape(DEVICES, 1, COLS), ALL, 0, 0, tiled=True)  6.29 us
  transfers between devices with their start and end apart: 19, of which 14 were waited for; matrix products, arithmetic and copies ran while one was open for 0% of the time, Pallas kernels for 0%

profile of v3, /device:TPU:1, one launch (start us, length us, event | category | flops | bytes accessed | tf_op | source)
XLA Modules:
  0.0 122.6 jit_solution(2316706334573836293)
XLA Ops:
  0.6 2.2 %copy-done = bf16[1,2,64,16384]{3,2,1,0:T(8,128)(2,1)S(1)} copy-done((bf16[1,2,64,16384]{3,2,1,0:T(8,128)(2,1)S(1)}, bf16[1,2,64,16384]{3,2,1,0:T(8,128)(2,1)}, u32[]{:S(2)}) %copy-start) | copy-done | bytes 4194328
  3.6 3.3 %collective-permute-start = (bf16[128,64,128]{2,1,0:T(8,128)(2,1)S(1)}, bf16[128,64,128]{2,1,0:T(8,128)(2,1)S(1)}, u32[]{:S(2)}, u32[]{:S(2)}) collective-permute-start(bf16[128,64,128]{2,1,0:T(8,128)(2,1)S(1)} %cross.1), channel_id=1, source_target_pairs={{0,4},{4,0},{1,5},{5,1},{2,6},{6,2},{3,7},{7,3},{8,12},{12,8},{9,1... | collective-permute-start | bytes 6291464 | tf_op jit(solution)/shard_map/ppermute | solution.py:255
  6.9 3.8 %collective-permute-done.got_ref = bf16[128,64,128]{2,1,0:T(8,128)(2,1)S(1)} collective-permute-done((bf16[128,64,128]{2,1,0:T(8,128)(2,1)S(1)}, bf16[128,64,128]{2,1,0:T(8,128)(2,1)S(1)}, u32[]{:S(2)}, u32[]{:S(2)}) %collective-permute-start) | collective-permute-done | bytes 2097184 | tf_op jit(solution)/shard_map/ppermute | solution.py:255
  12.9 1.6 %collective-permute-start.3 = (f32[32,32,128]{2,1,0:T(8,128)S(1)}, f32[32,32,128]{2,1,0:T(8,128)S(1)}, u32[]{:S(2)}, u32[]{:S(2)}) collective-permute-start(f32[32,32,128]{2,1,0:T(8,128)S(1)} %get-tuple-element.40), channel_id=1, source_target_pairs={{0,32},{32,0},{64,96},{96,64},{128,160},{160,128},{192,224},{224,1... | collective-permute-start | bytes 1572872 | tf_op jit(solution)/shard_map/ppermute | solution.py:260
  14.6 4.7 %collective-permute-start.4 = (f32[32,32,128]{2,1,0:T(8,128)S(1)}, f32[32,32,128]{2,1,0:T(8,128)S(1)}, u32[]{:S(2)}, u32[]{:S(2)}) collective-permute-start(f32[32,32,128]{2,1,0:T(8,128)S(1)} %get-tuple-element.41), channel_id=1, source_target_pairs={{0,224},{32,64},{64,32},{96,128},{128,96},{160,192},{192,160},{224... | collective-permute-start | bytes 1572872 | tf_op jit(solution)/shard_map/ppermute | solution.py:260
  19.2 5.5 %collective-permute-done.1.refs_4_ = f32[32,32,128]{2,1,0:T(8,128)S(1)} collective-permute-done((f32[32,32,128]{2,1,0:T(8,128)S(1)}, f32[32,32,128]{2,1,0:T(8,128)S(1)}, u32[]{:S(2)}, u32[]{:S(2)}) %collective-permute-start.1) | collective-permute-done | bytes 524320 | tf_op jit(solution)/shard_map/ppermute | solution.py:260
  26.1 4.2 %collective-permute-done.4.refs_7_ = f32[32,32,128]{2,1,0:T(8,128)S(1)} collective-permute-done((f32[32,32,128]{2,1,0:T(8,128)S(1)}, f32[32,32,128]{2,1,0:T(8,128)S(1)}, u32[]{:S(2)}, u32[]{:S(2)}) %collective-permute-start.4) | collective-permute-done | bytes 524320 | tf_op jit(solution)/shard_map/ppermute | solution.py:260
  31.3 2.5 %collective-permute-start.6 = (f32[32,16,128]{2,1,0:T(8,128)S(1)}, f32[32,16,128]{2,1,0:T(8,128)S(1)}, u32[]{:S(2)}, u32[]{:S(2)}) collective-permute-start(f32[32,16,128]{2,1,0:T(8,128)S(1)} %get-tuple-element.47), channel_id=1, source_target_pairs={{0,224},{32,64},{64,32},{96,128},{128,96},{160,192},{192,160},{224... | collective-permute-start | bytes 786440 | tf_op jit(solution)/shard_map/ppermute | solution.py:266
  34.9 2.3 %collective-permute-done.5.refs_4_ = f32[32,16,128]{2,1,0:T(8,128)S(1)} collective-permute-done((f32[32,16,128]{2,1,0:T(8,128)S(1)}, f32[32,16,128]{2,1,0:T(8,128)S(1)}, u32[]{:S(2)}, u32[]{:S(2)}) %collective-permute-start.5) | collective-permute-done | bytes 262176 | tf_op jit(solution)/shard_map/ppermute | solution.py:266
  39.3 1.5 %collective-permute-done.8.refs_7_ = f32[32,16,128]{2,1,0:T(8,128)S(1)} collective-permute-done((f32[32,16,128]{2,1,0:T(8,128)S(1)}, f32[32,16,128]{2,1,0:T(8,128)S(1)}, u32[]{:S(2)}, u32[]{:S(2)}) %collective-permute-start.8) | collective-permute-done | bytes 262176 | tf_op jit(solution)/shard_map/ppermute | solution.py:266
  42.6 4.1 %collective-permute-done.10.got_near_ref = f32[64,8,128]{2,1,0:T(8,128)S(1)} collective-permute-done((f32[64,8,128]{2,1,0:T(8,128)S(1)}, f32[64,8,128]{2,1,0:T(8,128)S(1)}, u32[]{:S(2)}, u32[]{:S(2)}) %collective-permute-start.10) | collective-permute-done | bytes 262176 | tf_op jit(solution)/shard_map/ppermute | solution.py:269
  48.0 1.7 %pack.1 = f32[256,8,128]{2,1,0:T(8,128)} custom-call(s32[128]{0:T(128)S(1)} %multiply_add_fusion.target_ref, f32[64,8,128]{2,1,0:T(8,128)S(1)} %get-tuple-element.50.far_ref, f32[64,8,128]{2,1,0:T(8,128)S(1)} %collective-permute-done.9.got_far_ref, f32[64,8,128]{2,1,0:T(8,128)S(1)} %get-tuple-element.52.near_ref, ...), custom_call_target="tpu_custom_call" | custom-call | bytes 4194304 | tf_op jit(solution)/shard_map/pack/pallas_call | solution.py:271
  49.8 12.7 %all-to-all-start = ((f32[256,8,128]{2,1,0:T(8,128)}), f32[256,8,128]{2,1,0:T(8,128)S(1)}, u32[]{:S(2)}, u32[]{:S(2)}) async-start(f32[256,8,128]{2,1,0:T(8,128)} %pack.1), calls=%async_computation | async-start | bytes 2097152 | tf_op jit(solution)/shard_map/all_to_all | solution.py:272
  62.5 1.5 %collective-permute-start.11 = (f32[64,256]{1,0:T(8,128)S(1)}, f32[64,256]{1,0:T(8,128)S(1)}, u32[]{:S(2)}, u32[]{:S(2)}) collective-permute-start(f32[64,256]{1,0:T(8,128)S(1)} %get-tuple-element.54), channel_id=1, source_target_pairs={{0,1},{1,2},{2,3},{3,0},{4,5},{5,6},{6,7},{7,4},{8,9},{9,10},{10,1... | collective-permute-start | bytes 196616 | tf_op jit(solution)/shard_map/ppermute | solution.py:246
  64.0 2.4 %collective-permute-start.12 = (f32[64,256]{1,0:T(8,128)S(1)}, f32[64,256]{1,0:T(8,128)S(1)}, u32[]{:S(2)}, u32[]{:S(2)}) collective-permute-start(f32[64,256]{1,0:T(8,128)S(1)} %get-tuple-element.55), channel_id=1, source_target_pairs={{0,2},{1,3},{2,0},{3,1},{4,6},{5,7},{6,4},{7,5},{8,10},{9,11},{10,... | collective-permute-start | bytes 196616 | tf_op jit(solution)/shard_map/ppermute | solution.py:246
  67.6 4.3 %collective-permute-done.12.mom2_ref = f32[64,256]{1,0:T(8,128)S(1)} collective-permute-done((f32[64,256]{1,0:T(8,128)S(1)}, f32[64,256]{1,0:T(8,128)S(1)}, u32[]{:S(2)}, u32[]{:S(2)}) %collective-permute-start.12) | collective-permute-done | bytes 65568 | tf_op jit(solution)/shard_map/ppermute | solution.py:246
  71.9 21.7 %all-to-all-done.got_ref = f32[256,8,128]{2,1,0:T(8,128)S(1)} async-done(((f32[256,8,128]{2,1,0:T(8,128)}), f32[256,8,128]{2,1,0:T(8,128)S(1)}, u32[]{:S(2)}, u32[]{:S(2)}) %all-to-all-start) | async-done | bytes 1048608 | tf_op jit(solution)/shard_map/all_to_all | solution.py:272
  93.6 5.7 %work.1 = (f32[512,128]{1,0:T(8,128)}, f32[64,256]{1,0:T(8,128)S(1)}, f32[64,256]{1,0:T(8,128)S(1)}, f32[64,256]{1,0:T(8,128)S(1)}, f32[64,256]{1,0:T(8,128)S(1)}) custom-call(s32[1,128]{1,0:T(1,128)S(1)} %bitcast_add_fusion.target_ref, f32[256,8,128]{2,1,0:T(8,128)S(1)} %all-to-all-done.got_ref, f32[3,64,256]{2,1,0:T(8,128)S(1)} %bitcast.13, ...), custom_call_target="tpu_custom_call" | custom-call | flops 1509949440 | bytes 4194304 | tf_op jit(solution)/shard_map/work/pallas_call | solution.py:274
  99.3 6.3 %all-to-all-start.1 = ((f32[256,1,256]{2,1,0:T(1,128)}), f32[256,1,256]{2,1,0:T(1,128)S(1)}, u32[]{:S(2)}, u32[]{:S(2)}) async-start(f32[256,1,256]{2,1,0:T(1,128)} %bitcast.5), calls=%async_computation.1 | async-start | bytes 524288 | tf_op jit(solution)/shard_map/all_to_all | solution.py:277
  105.6 1.5 %collective-permute-start.14 = (f32[64,256]{1,0:T(8,128)S(1)}, f32[64,256]{1,0:T(8,128)S(1)}, u32[]{:S(2)}, u32[]{:S(2)}) collective-permute-start(f32[64,256]{1,0:T(8,128)S(1)} %get-tuple-element.59), channel_id=1, source_target_pairs={{0,1},{1,2},{2,3},{3,0},{4,5},{5,6},{6,7},{7,4},{8,9},{9,10},{10,1... | collective-permute-start | bytes 196616 | tf_op jit(solution)/shard_map/ppermute | solution.py:246
  107.1 2.4 %collective-permute-start.15 = (f32[64,256]{1,0:T(8,128)S(1)}, f32[64,256]{1,0:T(8,128)S(1)}, u32[]{:S(2)}, u32[]{:S(2)}) collective-permute-start(f32[64,256]{1,0:T(8,128)S(1)} %get-tuple-element.60), channel_id=1, source_target_pairs={{0,2},{1,3},{2,0},{3,1},{4,6},{5,7},{6,4},{7,5},{8,10},{9,11},{10,... | collective-permute-start | bytes 196616 | tf_op jit(solution)/shard_map/ppermute | solution.py:246
  110.7 3.1 %collective-permute-done.15.new2_ref = f32[64,256]{1,0:T(8,128)S(1)} collective-permute-done((f32[64,256]{1,0:T(8,128)S(1)}, f32[64,256]{1,0:T(8,128)S(1)}, u32[]{:S(2)}, u32[]{:S(2)}) %collective-permute-start.15) | collective-permute-done | bytes 65568 | tf_op jit(solution)/shard_map/ppermute | solution.py:246
  113.8 7.3 %all-to-all-done.1.got_ref = f32[256,1,256]{2,1,0:T(1,128)S(1)} async-done(((f32[256,1,256]{2,1,0:T(1,128)}), f32[256,1,256]{2,1,0:T(1,128)S(1)}, u32[]{:S(2)}, u32[]{:S(2)}) %all-to-all-start.1) | async-done | bytes 262176 | tf_op jit(solution)/shard_map/all_to_all | solution.py:277
  121.1 1.5 %finish.1 = (f32[3,64,256]{2,1,0:T(8,128)}, f32[2,1,16384]{2,1,0:T(1,128)}, f32[2,1,16384]{2,1,0:T(1,128)}) custom-call(s32[128]{0:T(128)S(1)} %multiply_add_fusion.target_ref, f32[256,1,256]{2,1,0:T(1,128)S(1)} %all-to-all-done.1.got_ref, f32[2,1,16384]{2,1,0:T(1,128)S(1)} %copy-done.2, f32[64,256]{1,0:T(8,128)S(1)} %get-tuple-element.58.own_ref, ...), custom_call_target="tpu_custom_call" | custom-call | bytes 4194304 | tf_op jit(solution)/shard_map/finish/pallas_call | solution.py:280
  (32 shorter events, 13.9 us)
Async XLA Ops:
  0.6 2.2 %copy-start = (bf16[1,2,64,16384]{3,2,1,0:T(8,128)(2,1)S(1)}, bf16[1,2,64,16384]{3,2,1,0:T(8,128)(2,1)}, u32[]{:S(2)}) copy-start(bf16[1,2,64,16384]{3,2,1,0:T(8,128)(2,1)} %param.4) | copy-start | bytes 12582916
  2.8 7.9 %copy-start.1 = (f32[1,3,64,256]{3,2,1,0:T(8,128)S(1)}, f32[1,3,64,256]{3,2,1,0:T(8,128)}, u32[]{:S(2)}) copy-start(f32[1,3,64,256]{3,2,1,0:T(8,128)} %param.5) | copy-start | bytes 589828
  3.6 7.1 %collective-permute-start = (bf16[128,64,128]{2,1,0:T(8,128)(2,1)S(1)}, bf16[128,64,128]{2,1,0:T(8,128)(2,1)S(1)}, u32[]{:S(2)}, u32[]{:S(2)}) collective-permute-start(bf16[128,64,128]{2,1,0:T(8,128)(2,1)S(1)} %cross.1), channel_id=1, source_target_pairs={{0,4},{4,0},{1,5},{5,1},{2,6},{6,2},{3,7},{7,3},{8,12},{12,8},{9,1... | collective-permute-start | bytes 6291464 | tf_op jit(solution)/shard_map/ppermute | solution.py:255
  11.5 13.2 %collective-permute-start.1 = (f32[32,32,128]{2,1,0:T(8,128)S(1)}, f32[32,32,128]{2,1,0:T(8,128)S(1)}, u32[]{:S(2)}, u32[]{:S(2)}) collective-permute-start(f32[32,32,128]{2,1,0:T(8,128)S(1)} %get-tuple-element.38), channel_id=1, source_target_pairs={{0,8},{8,0},{16,24},{24,16},{1,9},{9,1},{17,25},{25,17},{2,10},{10... | collective-permute-start | bytes 1572872 | tf_op jit(solution)/shard_map/ppermute | solution.py:260
  11.6 14.4 %collective-permute-start.2 = (f32[32,32,128]{2,1,0:T(8,128)S(1)}, f32[32,32,128]{2,1,0:T(8,128)S(1)}, u32[]{:S(2)}, u32[]{:S(2)}) collective-permute-start(f32[32,32,128]{2,1,0:T(8,128)S(1)} %get-tuple-element.39), channel_id=1, source_target_pairs={{0,24},{8,16},{16,8},{24,0},{1,25},{9,17},{17,9},{25,1},{2,26},{10... | collective-permute-start | bytes 1572872 | tf_op jit(solution)/shard_map/ppermute | solution.py:260
  12.9 13.2 %collective-permute-start.3 = (f32[32,32,128]{2,1,0:T(8,128)S(1)}, f32[32,32,128]{2,1,0:T(8,128)S(1)}, u32[]{:S(2)}, u32[]{:S(2)}) collective-permute-start(f32[32,32,128]{2,1,0:T(8,128)S(1)} %get-tuple-element.40), channel_id=1, source_target_pairs={{0,32},{32,0},{64,96},{96,64},{128,160},{160,128},{192,224},{224,1... | collective-permute-start | bytes 1572872 | tf_op jit(solution)/shard_map/ppermute | solution.py:260
  14.6 15.7 %collective-permute-start.4 = (f32[32,32,128]{2,1,0:T(8,128)S(1)}, f32[32,32,128]{2,1,0:T(8,128)S(1)}, u32[]{:S(2)}, u32[]{:S(2)}) collective-permute-start(f32[32,32,128]{2,1,0:T(8,128)S(1)} %get-tuple-element.41), channel_id=1, source_target_pairs={{0,224},{32,64},{64,32},{96,128},{128,96},{160,192},{192,160},{224... | collective-permute-start | bytes 1572872 | tf_op jit(solution)/shard_map/ppermute | solution.py:260
  31.2 11.4 %copy-start.3 = (s32[128,1]{0,1:T(1,128)S(1)}, s32[128,1]{0,1:T(1,128)}, u32[]{:S(2)}) copy-start(s32[128,1]{0,1:T(1,128)} %param.7) | copy-start | bytes 1540
  31.2 6.0 %collective-permute-start.5 = (f32[32,16,128]{2,1,0:T(8,128)S(1)}, f32[32,16,128]{2,1,0:T(8,128)S(1)}, u32[]{:S(2)}, u32[]{:S(2)}) collective-permute-start(f32[32,16,128]{2,1,0:T(8,128)S(1)} %get-tuple-element.46), channel_id=1, source_target_pairs={{0,32},{32,0},{64,96},{96,64},{128,160},{160,128},{192,224},{224,1... | collective-permute-start | bytes 786440 | tf_op jit(solution)/shard_map/ppermute | solution.py:266
  31.3 7.2 %collective-permute-start.6 = (f32[32,16,128]{2,1,0:T(8,128)S(1)}, f32[32,16,128]{2,1,0:T(8,128)S(1)}, u32[]{:S(2)}, u32[]{:S(2)}) collective-permute-start(f32[32,16,128]{2,1,0:T(8,128)S(1)} %get-tuple-element.47), channel_id=1, source_target_pairs={{0,224},{32,64},{64,32},{96,128},{128,96},{160,192},{192,160},{224... | collective-permute-start | bytes 786440 | tf_op jit(solution)/shard_map/ppermute | solution.py:266
  33.7 5.5 %collective-permute-start.7 = (f32[32,16,128]{2,1,0:T(8,128)S(1)}, f32[32,16,128]{2,1,0:T(8,128)S(1)}, u32[]{:S(2)}, u32[]{:S(2)}) collective-permute-start(f32[32,16,128]{2,1,0:T(8,128)S(1)} %get-tuple-element.48), channel_id=1, source_target_pairs={{0,8},{8,0},{16,24},{24,16},{1,9},{9,1},{17,25},{25,17},{2,10},{10... | collective-permute-start | bytes 786440 | tf_op jit(solution)/shard_map/ppermute | solution.py:266
  34.0 6.7 %collective-permute-start.8 = (f32[32,16,128]{2,1,0:T(8,128)S(1)}, f32[32,16,128]{2,1,0:T(8,128)S(1)}, u32[]{:S(2)}, u32[]{:S(2)}) collective-permute-start(f32[32,16,128]{2,1,0:T(8,128)S(1)} %get-tuple-element.49), channel_id=1, source_target_pairs={{0,24},{8,16},{16,8},{24,0},{1,25},{9,17},{17,9},{25,1},{2,26},{10... | collective-permute-start | bytes 786440 | tf_op jit(solution)/shard_map/ppermute | solution.py:266
  41.4 5.3 %collective-permute-start.10 = (f32[64,8,128]{2,1,0:T(8,128)S(1)}, f32[64,8,128]{2,1,0:T(8,128)S(1)}, u32[]{:S(2)}, u32[]{:S(2)}) collective-permute-start(f32[64,8,128]{2,1,0:T(8,128)S(1)} %get-tuple-element.53), channel_id=1, source_target_pairs={{0,8},{8,0},{16,24},{24,16},{1,9},{9,1},{17,25},{25,17},{2,10},{10... | collective-permute-start | bytes 786440 | tf_op jit(solution)/shard_map/ppermute | solution.py:269
  41.5 6.5 %collective-permute-start.9 = (f32[64,8,128]{2,1,0:T(8,128)S(1)}, f32[64,8,128]{2,1,0:T(8,128)S(1)}, u32[]{:S(2)}, u32[]{:S(2)}) collective-permute-start(f32[64,8,128]{2,1,0:T(8,128)S(1)} %get-tuple-element.51), channel_id=1, source_target_pairs={{0,24},{8,16},{16,8},{24,0},{1,25},{9,17},{17,9},{25,1},{2,26},{10... | collective-permute-start | bytes 786440 | tf_op jit(solution)/shard_map/ppermute | solution.py:269
  49.8 43.8 %all-to-all-start = ((f32[256,8,128]{2,1,0:T(8,128)}), f32[256,8,128]{2,1,0:T(8,128)S(1)}, u32[]{:S(2)}, u32[]{:S(2)}) async-start(f32[256,8,128]{2,1,0:T(8,128)} %pack.1), calls=%async_computation | async-start | bytes 2097152 | tf_op jit(solution)/shard_map/all_to_all | solution.py:272
  62.5 5.1 %collective-permute-start.11 = (f32[64,256]{1,0:T(8,128)S(1)}, f32[64,256]{1,0:T(8,128)S(1)}, u32[]{:S(2)}, u32[]{:S(2)}) collective-permute-start(f32[64,256]{1,0:T(8,128)S(1)} %get-tuple-element.54), channel_id=1, source_target_pairs={{0,1},{1,2},{2,3},{3,0},{4,5},{5,6},{6,7},{7,4},{8,9},{9,10},{10,1... | collective-permute-start | bytes 196616 | tf_op jit(solution)/shard_map/ppermute | solution.py:246
  64.0 7.9 %collective-permute-start.12 = (f32[64,256]{1,0:T(8,128)S(1)}, f32[64,256]{1,0:T(8,128)S(1)}, u32[]{:S(2)}, u32[]{:S(2)}) collective-permute-start(f32[64,256]{1,0:T(8,128)S(1)} %get-tuple-element.55), channel_id=1, source_target_pairs={{0,2},{1,3},{2,0},{3,1},{4,6},{5,7},{6,4},{7,5},{8,10},{9,11},{10,... | collective-permute-start | bytes 196616 | tf_op jit(solution)/shard_map/ppermute | solution.py:246
  66.4 5.5 %collective-permute-start.13 = (f32[64,256]{1,0:T(8,128)S(1)}, f32[64,256]{1,0:T(8,128)S(1)}, u32[]{:S(2)}, u32[]{:S(2)}) collective-permute-start(f32[64,256]{1,0:T(8,128)S(1)} %get-tuple-element.56), channel_id=1, source_target_pairs={{0,3},{1,0},{2,1},{3,2},{4,7},{5,4},{6,5},{7,6},{8,11},{9,8},{10,9... | collective-permute-start | bytes 196616 | tf_op jit(solution)/shard_map/ppermute | solution.py:246
  67.5 53.5 %copy-start.2 = (f32[2,1,16384]{2,1,0:T(1,128)S(1)}, f32[2,1,16384]{2,1,0:T(1,128)}, u32[]{:S(2)}) copy-start(f32[2,1,16384]{2,1,0:T(1,128)} %weights_ref.1) | copy-start | bytes 393220
  99.3 21.7 %all-to-all-start.1 = ((f32[256,1,256]{2,1,0:T(1,128)}), f32[256,1,256]{2,1,0:T(1,128)S(1)}, u32[]{:S(2)}, u32[]{:S(2)}) async-start(f32[256,1,256]{2,1,0:T(1,128)} %bitcast.5), calls=%async_computation.1 | async-start | bytes 524288 | tf_op jit(solution)/shard_map/all_to_all | solution.py:277
  105.6 5.0 %collective-permute-start.14 = (f32[64,256]{1,0:T(8,128)S(1)}, f32[64,256]{1,0:T(8,128)S(1)}, u32[]{:S(2)}, u32[]{:S(2)}) collective-permute-start(f32[64,256]{1,0:T(8,128)S(1)} %get-tuple-element.59), channel_id=1, source_target_pairs={{0,1},{1,2},{2,3},{3,0},{4,5},{5,6},{6,7},{7,4},{8,9},{9,10},{10,1... | collective-permute-start | bytes 196616 | tf_op jit(solution)/shard_map/ppermute | solution.py:246
  107.1 6.7 %collective-permute-start.15 = (f32[64,256]{1,0:T(8,128)S(1)}, f32[64,256]{1,0:T(8,128)S(1)}, u32[]{:S(2)}, u32[]{:S(2)}) collective-permute-start(f32[64,256]{1,0:T(8,128)S(1)} %get-tuple-element.60), channel_id=1, source_target_pairs={{0,2},{1,3},{2,0},{3,1},{4,6},{5,7},{6,4},{7,5},{8,10},{9,11},{10,... | collective-permute-start | bytes 196616 | tf_op jit(solution)/shard_map/ppermute | solution.py:246
  109.5 4.2 %collective-permute-start.16 = (f32[64,256]{1,0:T(8,128)S(1)}, f32[64,256]{1,0:T(8,128)S(1)}, u32[]{:S(2)}, u32[]{:S(2)}) collective-permute-start(f32[64,256]{1,0:T(8,128)S(1)} %get-tuple-element.61), channel_id=1, source_target_pairs={{0,3},{1,0},{2,1},{3,2},{4,7},{5,4},{6,5},{7,6},{8,11},{9,8},{10,9... | collective-permute-start | bytes 196616 | tf_op jit(solution)/shard_map/ppermute | solution.py:246

commit v4 on v3

v4 whole, which is shorter than its diff:
```python
import functools
import math

import jax
import jax.numpy as jnp
from jax import lax
from jax.experimental import pallas as pl
from jax.experimental.pallas import tpu as pltpu
from jax.sharding import Mesh, PartitionSpec as P

HEADS = 64
RANK = 256
COLS = 256
L = 2
ITERS = 5
MATS = L * HEADS
CAP = 3
SIZE = HEADS // 2
COUNT = L * SIZE
OWNERS = 64
DEVICES = 256
ALL = ("y", "z", "x", "core")

quintic_a = 3.4445
quintic_b = -4.775
quintic_c = 2.0315
momentum_beta = 0.95
learn_rate = 0.02
decay_rate = 0.1
rms_factor = 0.2
norm_epsilon = 1e-07
VMEM_LIMIT = 32 * 1024 * 1024

f32 = jnp.float32
bf16 = jnp.bfloat16


def targets(table):
    owners = table[:, 0]
    index = jnp.arange(MATS, dtype=jnp.int32)
    before = (owners[:, None] == owners[None, :]) & (index[:, None] < index[None, :])
    slots = jnp.sum(before.astype(jnp.int32), axis=0)
    return slots * OWNERS + owners


def params():
    return pltpu.CompilerParams(vmem_limit_bytes=VMEM_LIMIT)


def lanes_of(head, half):
    return pl.ds(pl.multiple_of(head * COLS + half * 128, 128), 128)


def rows_of(block, size):
    return pl.ds(pl.multiple_of(block * size, size), size)


def bits():
    x = lax.axis_index("x")
    second = x // 2
    return (x + second) % 2, second, lax.axis_index("z") % 2


def middle_bit(group):
    one, two, three = bits()
    return jnp.where(lax.axis_index("core") == 0, three, two if group else one)


def rows_kernel(first, size, mine, grad_ref, out_ref, sems):
    core = lax.axis_index("core")
    rows = rows_of(core if mine else 1 - core, 32)
    lanes = slice(first * COLS, (first + size) * COLS)
    copies = [pltpu.make_async_copy(grad_ref.at[layer, rows, lanes], out_ref.at[layer], sems.at[layer]) for layer in range(L)]
    for copy in copies:
        copy.start()
    for copy in copies:
        copy.wait()


def total(own_ref, got_ref, layer, rows, lanes):
    return own_ref[layer, rows, lanes].astype(f32) + got_ref[layer, rows, lanes].astype(f32)


def first_kernel(group, own_ref, got_ref, send, keep):
    one, two, three = bits()

    @pl.when(lax.axis_index("core") == 0)
    def _():
        @pl.loop(0, SIZE, unroll=2)
        def _(head):
            for layer in range(L):
                at = layer * SIZE + head
                for value, out in ((1 - (two if group else one), send), ((two if group else one), keep)):
                    for block in range(2):
                        if group:
                            both = total(own_ref, got_ref, layer, slice(block * 16, block * 16 + 16), lanes_of(head, value))
                        else:
                            both = total(own_ref, got_ref, layer, rows_of(value, 16), lanes_of(head, block))
                        out[at, 2 * block] = both[:8]
                        out[at, 2 * block + 1] = both[8:]

    @pl.when(lax.axis_index("core") == 1)
    def _():
        @pl.loop(0, SIZE, unroll=2)
        def _(head):
            for layer in range(L):
                at = layer * SIZE + head
                for row in range(2):
                    for lane in range(2):
                        both = total(own_ref, got_ref, layer, slice(row * 16, row * 16 + 16), lanes_of(head, lane))
                        tile = 2 * row + lane if group else 2 * lane + row
                        send[at, tile] = jnp.where(three == 0, both[8:], both[:8])
                        keep[at, tile] = jnp.where(three == 0, both[:8], both[8:])


def second_kernel(group, kept, got, send, keep):
    bit = middle_bit(group)

    @pl.loop(0, COUNT, unroll=4)
    def _(at):
        for block in range(2):
            for tile, out in ((2 * block + 1 - bit, send), (2 * block + bit, keep)):
                out[at, block] = kept[at, tile] + got[at, tile]


def third_kernel(group, kept, got, send, keep):
    one, two, _ = bits()
    bit = one if group else two

    @pl.loop(0, COUNT, unroll=4)
    def _(at):
        send[at] = kept[at, 1 - bit] + got[at, 1 - bit]
        keep[at] = kept[at, bit] + got[at, bit]


def slots_kernel(mom_ref, *outs):
    y = lax.axis_index("y")
    for step, out in enumerate(outs, start=1):
        out[...] = mom_ref[jnp.minimum((y + step) % 4, CAP - 1)]


def pack_kernel(target_ref, a_ref, got_a_ref, b_ref, got_b_ref, out_ref):
    for layer in range(L):
        for head in range(HEADS):
            where = target_ref[layer * HEADS + head]
            at = layer * SIZE + head % SIZE
            kept, got = (b_ref, got_b_ref) if head >= SIZE else (a_ref, got_a_ref)
            out_ref[where] = kept[at] + got[at]


def halves(value):
    high = value.astype(bf16)
    return high, (value - high.astype(f32)).astype(bf16)


def times(left, right, transposed):
    dims = (((1,), (1 if transposed else 0,)), ((), ()))

    def dot(a, b):
        return lax.dot_general(a, b, dims, preferred_element_type=f32)

    (lh, ll), (rh, rl) = left, right
    return dot(lh, rh) + (dot(lh, rl) + dot(ll, rh))


def newton(advance):
    norm = jnp.sqrt(jnp.sum(advance * advance))
    iterate = advance / (norm + norm_epsilon)
    for _ in range(ITERS):
        parts = halves(iterate)
        gram = times(parts, parts, True)
        gram_parts = halves(gram)
        poly = quintic_b * gram + quintic_c * times(gram_parts, gram_parts, False)
        iterate = quintic_a * iterate + times(halves(poly), parts, False)
    return iterate


def work_kernel(target_ref, got_ref, held_ref, mom1_ref, mom2_ref, mom3_ref, out_ref, own_ref, new1_ref, new2_ref, new3_ref, fresh, adv):
    y = lax.axis_index("y")
    me = y * OWNERS + (lax.axis_index("z") * 4 + lax.axis_index("x")) * 2 + lax.axis_index("core")
    live = jnp.max(jnp.where(target_ref[...] == me, 1, 0)) > 0
    for step, mom_ref in enumerate((None, mom1_ref, mom2_ref, mom3_ref)):
        block = (y + 4 - step) % 4
        for x, (one, two) in enumerate(((0, 0), (1, 0), (1, 1), (0, 1))):
            lanes = slice(two * 128, (two + 1) * 128)
            for core in range(2):
                for three in range(2):
                    tile = 4 * core + 2 * one + three
                    parts = [got_ref[block * 64 + (z * 4 + x) * 2 + core] for z in range(three, 8, 2)]
                    g = jnp.where(live, (parts[0] + parts[1]) + (parts[2] + parts[3]), 0.0)
                    if mom_ref is None:
                        mom = held_ref[jnp.minimum(y, CAP - 1), tile * 8 : tile * 8 + 8, lanes]
                    else:
                        mom = mom_ref[tile * 8 : tile * 8 + 8, lanes]
                    new = jnp.where(live, momentum_beta * mom + g, 0.0)
                    rows = rows_of(block * 8 + tile, 8)
                    fresh[rows, lanes] = new
                    adv[rows, lanes] = g + momentum_beta * new
    for step, out in enumerate((own_ref, new1_ref, new2_ref, new3_ref)):
        out[...] = fresh[rows_of((y + step) % 4, 64), :]
    ortho = newton(adv[...])
    for half in range(2):
        out_ref[pl.ds(half, RANK, stride=2), :] = ortho[:, half * 128 : (half + 1) * 128]


def finish_kernel(target_ref, got_ref, weights_ref, own_ref, new1_ref, new2_ref, new3_ref, mom_ref, step_ref, new_ref):
    y = lax.axis_index("y")
    for step, ref in enumerate((own_ref, new1_ref, new2_ref, new3_ref)):
        slot = (y + 4 - step) % 4

        @pl.when(slot < CAP)
        def _(slot=slot, ref=ref):
            mom_ref[slot] = ref[...]

    scale = rms_factor * math.sqrt(max(RANK, COLS))
    for layer in range(L):
        for head in range(HEADS):
            where = target_ref[layer * HEADS + head]
            lanes = slice(head * COLS, (head + 1) * COLS)
            held = weights_ref[layer, :, lanes]
            step = scale * got_ref[pl.ds(where, 1), 0, :] + decay_rate * held
            step_ref[layer, :, lanes] = step
            new_ref[layer, :, lanes] = held - learn_rate * step


def shape(*dims, dtype=f32):
    return jax.ShapeDtypeStruct(dims, dtype)


def call(kernel, outs, ins, scratch=(), flops=0, moved=1 << 22):
    many = isinstance(outs, tuple)
    out_spec = pl.BlockSpec(memory_space=pltpu.VMEM)
    return pl.pallas_call(
        kernel,
        out_shape=outs,
        in_specs=[pl.BlockSpec(memory_space=pltpu.SMEM if kind == "s" else pltpu.VMEM) for kind in ins],
        out_specs=tuple(out_spec for _ in outs) if many else out_spec,
        scratch_shapes=[pltpu.VMEM(dims, f32) for dims in scratch],
        compiler_params=params(),
        cost_estimate=pl.CostEstimate(flops=flops, bytes_accessed=moved, transcendentals=0),
        name=getattr(kernel, "func", kernel).__name__.removesuffix("_kernel"),
    )


def rows_of_heads(gradient, first, size, mine):
    return pl.pallas_call(
        functools.partial(rows_kernel, first, size, mine),
        out_shape=shape(L, 32, size * COLS, dtype=bf16),
        in_specs=[pl.BlockSpec(memory_space=pltpu.HBM)],
        out_specs=pl.BlockSpec(memory_space=pltpu.VMEM),
        scratch_shapes=[pltpu.SemaphoreType.DMA((L,))],
        compiler_params=params(),
        cost_estimate=pl.CostEstimate(flops=0, bytes_accessed=1 << 22, transcendentals=0),
        name="own" if mine else "cross",
    )(pltpu.with_memory_space_constraint(gradient, pltpu.HBM))


def route(moves):
    pairs = []
    for z in range(8):
        for x in range(4):
            for core, move in enumerate(moves):
                to_z, to_x = move(z, x)
                pairs.append(((z * 4 + x) * 2 + core, (to_z * 4 + to_x) * 2 + core))
    return pairs


def near(z, x):
    return z, x ^ 1


def far(z, x):
    return z, 3 - x


def pair(z, x):
    return z ^ 1, x


def link(z, x):
    return (z + 1 if z % 2 else z - 1) % 8, x


ROUTES = (
    (route((near, pair)), route((pair, near)), route((far, far))),
    (route((far, link)), route((link, far)), route((near, near))),
)


def along_y(values):
    return [
        lax.ppermute(value, "y", [(i, (i + step) % 4) for i in range(4)]) for step, value in enumerate(values, start=1)
    ]


def on_device(gradient, momentum, weights, table):
    target = targets(table)
    local = gradient[0]

    groups = range(2)
    dp = ("z", "x", "core")
    crossed = [lax.ppermute(rows_of_heads(local, group * SIZE, SIZE, False), "core", [(0, 1), (1, 0)]) for group in groups]
    own = [rows_of_heads(local, group * SIZE, SIZE, True) for group in groups]
    parts = [(own[group], crossed[group]) for group in groups]
    for step, (kernel, dims) in enumerate(((first_kernel, (4, 8, 128)), (second_kernel, (2, 8, 128)), (third_kernel, (8, 128)))):
        pieces = [call(functools.partial(kernel, group), (shape(COUNT, *dims),) * 2, "vv")(*parts[group]) for group in groups]
        parts = [(keep, lax.ppermute(send, dp, ROUTES[group][step])) for group, (send, keep) in enumerate(pieces)]
    moms = along_y(call(slots_kernel, (shape(64, COLS),) * 3, "v")(momentum[0]))

    outgoing = call(pack_kernel, shape(DEVICES, 8, 128), "svvvv")(target, *parts[0], *parts[1])
    got = lax.all_to_all(outgoing, ALL, 0, 0, tiled=True)
    outs = (shape(2 * RANK, 128),) + (shape(64, COLS),) * 4
    ortho, fresh, *news = call(work_kernel, outs, "vvvvvv", [(RANK, COLS), (RANK, COLS)], 15 * 3 * 2 * 256**3)(
        target.reshape(1, MATS), got, momentum[0], *moms
    )
    returned = lax.all_to_all(ortho.reshape(DEVICES, 1, COLS), ALL, 0, 0, tiled=True)
    news = along_y(news)
    outs = (shape(CAP, 64, COLS), shape(L, 1, HEADS * COLS), shape(L, 1, HEADS * COLS))
    new_momentum, step_update, new_weights = call(finish_kernel, outs, "svvvvvv")(target, returned, weights, fresh, *news)
    return new_momentum[None], step_update, new_weights


def solution(mesh):
    fine = Mesh(mesh.devices.reshape(8, 4, 2, 4), ("z", "x", "core", "y"))
    dp = ("z", "x", "core")
    return jax.shard_map(
        on_device,
        mesh=fine,
        in_specs=(
            P(dp, None, "y", None),
            P(dp, None, "y", None),
            P(None, ("y",) + dp, None),
            P(),
        ),
        out_specs=(
            P(dp, None, "y", None),
            P(None, ("y",) + dp, None),
            P(None, ("y",) + dp, None),
        ),
        check_vma=False,
    )
```

time: 123 us -> 118 us (0.959)
  waiting for transfers between devices: 62.5 us -> 58.6 us
  Pallas kernels: 12.1 us -> 15.9 us
  starting transfers between devices: 45 us -> 42.5 us
  local copies, waits for them, and re-layouts: 2.19 us -> 0.01 us
    ppermute x11 -> x8, waiting for transfers between devices: 26.1 us -> 21.6 us  [the longest x6 21.6 us: on_device(): lax.ppermute(send, dp, ROUTES[group][step])]
    pallas_call x4 -> x11, Pallas kernels: 3.11 us -> 6.98 us  [the longest x4 4.87 us: rows_of_heads(): pl.pallas_call(functools.partial(rows_kernel, first, size, mine), out_sha...]
    unnamed x8 -> x6, local copies, waits for them, and re-layouts: 2.19 us -> 0.01 us
    ppermute x11 -> x8, starting transfers between devices: 15.9 us -> 13.9 us  [the longest x6 10.5 us: on_device(): lax.ppermute(send, dp, ROUTES[group][step])]
  transfers between devices with their start and end apart: 19 -> 16, of which waited for: 14 -> 12; matrix products, arithmetic and copies ran while one was open for 0% -> 0% of each run, Pallas kernels for 0% -> 5%
where the time goes in v4:
time: 118 us
  waiting for transfers between devices  58.6 us (50%)
  starting transfers between devices  42.5 us (36%)
  Pallas kernels  15.9 us (13%)
    all_to_all x1, waiting for transfers between devices, on_device(): got = lax.all_to_all(outgoing, ALL, 0, 0, tiled=True)  21.7 us
    ppermute x6, waiting for transfers between devices, on_device(): lax.ppermute(send, dp, ROUTES[group][step])  21.6 us
    all_to_all x1, starting transfers between devices, on_device(): got = lax.all_to_all(outgoing, ALL, 0, 0, tiled=True)  12.9 us
    ppermute x6, starting transfers between devices, on_device(): lax.ppermute(send, dp, ROUTES[group][step])  10.5 us
    ppermute x6, starting transfers between devices, along_y(): lax.ppermute(value, 'y', [(i, (i + step) % 4) for i in range(4)])  9.49 us
    ppermute x6, waiting for transfers between devices, along_y(): lax.ppermute(value, 'y', [(i, (i + step) % 4) for i in range(4)])  8 us
    all_to_all x1, waiting for transfers between devices, on_device(): lax.all_to_all(ortho.reshape(DEVICES, 1, COLS), ALL, 0, 0, tiled=True)  7.29 us
    all_to_all x1, starting transfers between devices, on_device(): lax.all_to_all(ortho.reshape(DEVICES, 1, COLS), ALL, 0, 0, tiled=True)  6.29 us
  transfers between devices with their start and end apart: 16, of which 12 were waited for; matrix products, arithmetic and copies ran while one was open for 0% of the time, Pallas kernels for 5%

profile of v4, /device:TPU:1, one launch (start us, length us, event | category | flops | bytes accessed | tf_op | source)
XLA Modules:
  0.0 117.9 jit_solution(9733756057642450810)
XLA Ops:
  0.6 1.2 %cross.3 = bf16[2,32,8192]{2,1,0:T(8,128)(2,1)S(1)} custom-call(bf16[2,64,16384]{2,1,0:T(8,128)(2,1)} %bitcast.12), custom_call_target="tpu_custom_call" | custom-call | bytes 4194304 | tf_op jit(solution)/shard_map/cross/pallas_call | solution.py:246
  1.9 3.3 %collective-permute-start.4 = (bf16[2,32,8192]{2,1,0:T(8,128)(2,1)S(1)}, bf16[2,32,8192]{2,1,0:T(8,128)(2,1)S(1)}, u32[]{:S(2)}, u32[]{:S(2)}) collective-permute-start(bf16[2,32,8192]{2,1,0:T(8,128)(2,1)S(1)} %cross.3), channel_id=1, source_target_pairs={{0,4},{4,0},{1,5},{5,1},{2,6},{6,2},{3,7},{7,3},{8,12},{12,8},{9,1... | collective-permute-start | bytes 3145736 | tf_op jit(solution)/shard_map/ppermute | solution.py:302
  5.2 1.2 %cross.2 = bf16[2,32,8192]{2,1,0:T(8,128)(2,1)S(1)} custom-call(bf16[2,64,16384]{2,1,0:T(8,128)(2,1)} %bitcast.13), custom_call_target="tpu_custom_call" | custom-call | bytes 4194304 | tf_op jit(solution)/shard_map/cross/pallas_call | solution.py:246
  8.4 3.9 %collective-permute-start.5 = (f32[64,4,8,128]{3,2,1,0:T(8,128)S(1)}, f32[64,4,8,128]{3,2,1,0:T(8,128)S(1)}, u32[]{:S(2)}, u32[]{:S(2)}) collective-permute-start(f32[64,4,8,128]{3,2,1,0:T(8,128)S(1)} %get-tuple-element.33), channel_id=1, source_target_pairs={{0,24},{4,228},{8,16},{12,236},{16,8},{20,244},{24,0},{28,252},{32... | collective-permute-start | bytes 3145736 | tf_op jit(solution)/shard_map/ppermute | solution.py:307
  14.4 10.3 %collective-permute-done.5.got = f32[64,4,8,128]{3,2,1,0:T(8,128)S(1)} collective-permute-done((f32[64,4,8,128]{3,2,1,0:T(8,128)S(1)}, f32[64,4,8,128]{3,2,1,0:T(8,128)S(1)}, u32[]{:S(2)}, u32[]{:S(2)}) %collective-permute-start.5) | collective-permute-done | bytes 1048608 | tf_op jit(solution)/shard_map/ppermute | solution.py:307
  24.9 2.5 %collective-permute-start.6 = (f32[64,2,8,128]{3,2,1,0:T(8,128)S(1)}, f32[64,2,8,128]{3,2,1,0:T(8,128)S(1)}, u32[]{:S(2)}, u32[]{:S(2)}) collective-permute-start(f32[64,2,8,128]{3,2,1,0:T(8,128)S(1)} %get-tuple-element.35), channel_id=1, source_target_pairs={{0,224},{4,28},{8,232},{12,20},{16,240},{20,12},{24,248},{28,4},{3... | collective-permute-start | bytes 1572872 | tf_op jit(solution)/shard_map/ppermute | solution.py:307
  28.3 1.3 %collective-permute-start.2 = (f32[64,2,8,128]{3,2,1,0:T(8,128)S(1)}, f32[64,2,8,128]{3,2,1,0:T(8,128)S(1)}, u32[]{:S(2)}, u32[]{:S(2)}) collective-permute-start(f32[64,2,8,128]{3,2,1,0:T(8,128)S(1)} %get-tuple-element.29), channel_id=1, source_target_pairs={{0,32},{4,12},{8,40},{12,4},{16,48},{20,28},{24,56},{28,20},{32,0}... | collective-permute-start | bytes 1572872 | tf_op jit(solution)/shard_map/ppermute | solution.py:307
  29.6 4.9 %collective-permute-done.6.got = f32[64,2,8,128]{3,2,1,0:T(8,128)S(1)} collective-permute-done((f32[64,2,8,128]{3,2,1,0:T(8,128)S(1)}, f32[64,2,8,128]{3,2,1,0:T(8,128)S(1)}, u32[]{:S(2)}, u32[]{:S(2)}) %collective-permute-start.6) | collective-permute-done | bytes 524320 | tf_op jit(solution)/shard_map/ppermute | solution.py:307
  34.7 1.9 %collective-permute-done.2.got = f32[64,2,8,128]{3,2,1,0:T(8,128)S(1)} collective-permute-done((f32[64,2,8,128]{3,2,1,0:T(8,128)S(1)}, f32[64,2,8,128]{3,2,1,0:T(8,128)S(1)}, u32[]{:S(2)}, u32[]{:S(2)}) %collective-permute-start.2) | collective-permute-done | bytes 524320 | tf_op jit(solution)/shard_map/ppermute | solution.py:307
  36.8 2.6 %collective-permute-start.3 = (f32[64,8,128]{2,1,0:T(8,128)S(1)}, f32[64,8,128]{2,1,0:T(8,128)S(1)}, u32[]{:S(2)}, u32[]{:S(2)}) collective-permute-start(f32[64,8,128]{2,1,0:T(8,128)S(1)} %get-tuple-element.31), channel_id=1, source_target_pairs={{0,24},{4,28},{8,16},{12,20},{16,8},{20,12},{24,0},{28,4},{32,56},... | collective-permute-start | bytes 786440 | tf_op jit(solution)/shard_map/ppermute | solution.py:307
  40.4 2.9 %collective-permute-done.3.got_a_ref = f32[64,8,128]{2,1,0:T(8,128)S(1)} collective-permute-done((f32[64,8,128]{2,1,0:T(8,128)S(1)}, f32[64,8,128]{2,1,0:T(8,128)S(1)}, u32[]{:S(2)}, u32[]{:S(2)}) %collective-permute-start.3) | collective-permute-done | bytes 262176 | tf_op jit(solution)/shard_map/ppermute | solution.py:307
  43.3 1.7 %pack.1 = f32[256,8,128]{2,1,0:T(8,128)} custom-call(s32[128]{0:T(128)S(1)} %multiply_add_fusion.target_ref, f32[64,8,128]{2,1,0:T(8,128)S(1)} %get-tuple-element.30.a_ref, f32[64,8,128]{2,1,0:T(8,128)S(1)} %collective-permute-done.3.got_a_ref, f32[64,8,128]{2,1,0:T(8,128)S(1)} %get-tuple-element.36.b_ref, f32[64,8,128]{2,1,0:T(8,128)S(1)} %collective-permute-done.7.got_b_ref), custom_call_target="tpu_custom_call" | custom-call | bytes 4194304 | tf_op jit(solution)/shard_map/pack/pallas_call | solution.py:310
  45.0 12.9 %all-to-all-start = ((f32[256,8,128]{2,1,0:T(8,128)}), f32[256,8,128]{2,1,0:T(8,128)S(1)}, u32[]{:S(2)}, u32[]{:S(2)}) async-start(f32[256,8,128]{2,1,0:T(8,128)} %pack.1), calls=%async_computation | async-start | bytes 2097152 | tf_op jit(solution)/shard_map/all_to_all | solution.py:311
  57.9 2.7 %collective-permute-start.10 = (f32[64,256]{1,0:T(8,128)S(1)}, f32[64,256]{1,0:T(8,128)S(1)}, u32[]{:S(2)}, u32[]{:S(2)}) collective-permute-start(f32[64,256]{1,0:T(8,128)S(1)} %get-tuple-element.40), channel_id=1, source_target_pairs={{0,3},{1,0},{2,1},{3,2},{4,7},{5,4},{6,5},{7,6},{8,11},{9,8},{10,9... | collective-permute-start | bytes 196616 | tf_op jit(solution)/shard_map/ppermute | solution.py:292
  60.6 1.7 %collective-permute-start.9 = (f32[64,256]{1,0:T(8,128)S(1)}, f32[64,256]{1,0:T(8,128)S(1)}, u32[]{:S(2)}, u32[]{:S(2)}) collective-permute-start(f32[64,256]{1,0:T(8,128)S(1)} %get-tuple-element.39), channel_id=1, source_target_pairs={{0,2},{1,3},{2,0},{3,1},{4,6},{5,7},{6,4},{7,5},{8,10},{9,11},{10,... | collective-permute-start | bytes 196616 | tf_op jit(solution)/shard_map/ppermute | solution.py:292
  62.5 3.9 %collective-permute-done.8.mom1_ref = f32[64,256]{1,0:T(8,128)S(1)} collective-permute-done((f32[64,256]{1,0:T(8,128)S(1)}, f32[64,256]{1,0:T(8,128)S(1)}, u32[]{:S(2)}, u32[]{:S(2)}) %collective-permute-start.8) | collective-permute-done | bytes 65568 | tf_op jit(solution)/shard_map/ppermute | solution.py:292
  67.2 21.7 %all-to-all-done.got_ref = f32[256,8,128]{2,1,0:T(8,128)S(1)} async-done(((f32[256,8,128]{2,1,0:T(8,128)}), f32[256,8,128]{2,1,0:T(8,128)S(1)}, u32[]{:S(2)}, u32[]{:S(2)}) %all-to-all-start) | async-done | bytes 1048608 | tf_op jit(solution)/shard_map/all_to_all | solution.py:311
  89.0 5.7 %work.1 = (f32[512,128]{1,0:T(8,128)}, f32[64,256]{1,0:T(8,128)S(1)}, f32[64,256]{1,0:T(8,128)S(1)}, f32[64,256]{1,0:T(8,128)S(1)}, f32[64,256]{1,0:T(8,128)S(1)}) custom-call(s32[1,128]{1,0:T(1,128)S(1)} %bitcast_add_fusion.target_ref, f32[256,8,128]{2,1,0:T(8,128)S(1)} %all-to-all-done.got_ref, f32[3,64,256]{2,1,0:T(8,128)S(1)} %bitcast.11, ...), custom_call_target="tpu_custom_call" | custom-call | flops 1509949440 | bytes 4194304 | tf_op jit(solution)/shard_map/work/pallas_call | solution.py:313
  94.7 6.3 %all-to-all-start.1 = ((f32[256,1,256]{2,1,0:T(1,128)}), f32[256,1,256]{2,1,0:T(1,128)S(1)}, u32[]{:S(2)}, u32[]{:S(2)}) async-start(f32[256,1,256]{2,1,0:T(1,128)} %bitcast.5), calls=%async_computation.1 | async-start | bytes 524288 | tf_op jit(solution)/shard_map/all_to_all | solution.py:316
  101.0 1.5 %collective-permute-start.11 = (f32[64,256]{1,0:T(8,128)S(1)}, f32[64,256]{1,0:T(8,128)S(1)}, u32[]{:S(2)}, u32[]{:S(2)}) collective-permute-start(f32[64,256]{1,0:T(8,128)S(1)} %get-tuple-element.43), channel_id=1, source_target_pairs={{0,1},{1,2},{2,3},{3,0},{4,5},{5,6},{6,7},{7,4},{8,9},{9,10},{10,1... | collective-permute-start | bytes 196616 | tf_op jit(solution)/shard_map/ppermute | solution.py:292
  102.5 2.4 %collective-permute-start.12 = (f32[64,256]{1,0:T(8,128)S(1)}, f32[64,256]{1,0:T(8,128)S(1)}, u32[]{:S(2)}, u32[]{:S(2)}) collective-permute-start(f32[64,256]{1,0:T(8,128)S(1)} %get-tuple-element.44), channel_id=1, source_target_pairs={{0,2},{1,3},{2,0},{3,1},{4,6},{5,7},{6,4},{7,5},{8,10},{9,11},{10,... | collective-permute-start | bytes 196616 | tf_op jit(solution)/shard_map/ppermute | solution.py:292
  106.0 3.1 %collective-permute-done.12.new2_ref = f32[64,256]{1,0:T(8,128)S(1)} collective-permute-done((f32[64,256]{1,0:T(8,128)S(1)}, f32[64,256]{1,0:T(8,128)S(1)}, u32[]{:S(2)}, u32[]{:S(2)}) %collective-permute-start.12) | collective-permute-done | bytes 65568 | tf_op jit(solution)/shard_map/ppermute | solution.py:292
  109.1 7.3 %all-to-all-done.1.got_ref = f32[256,1,256]{2,1,0:T(1,128)S(1)} async-done(((f32[256,1,256]{2,1,0:T(1,128)}), f32[256,1,256]{2,1,0:T(1,128)S(1)}, u32[]{:S(2)}, u32[]{:S(2)}) %all-to-all-start.1) | async-done | bytes 262176 | tf_op jit(solution)/shard_map/all_to_all | solution.py:316
  116.4 1.5 %finish.1 = (f32[3,64,256]{2,1,0:T(8,128)}, f32[2,1,16384]{2,1,0:T(1,128)}, f32[2,1,16384]{2,1,0:T(1,128)}) custom-call(s32[128]{0:T(128)S(1)} %multiply_add_fusion.target_ref, f32[256,1,256]{2,1,0:T(1,128)S(1)} %all-to-all-done.1.got_ref, f32[2,1,16384]{2,1,0:T(1,128)S(1)} %copy-done.1, f32[64,256]{1,0:T(8,128)S(1)} %get-tuple-element.42.own_ref, ...), custom_call_target="tpu_custom_call" | custom-call | bytes 4194304 | tf_op jit(solution)/shard_map/finish/pallas_call | solution.py:319
  (31 shorter events, 8.6 us)
Async XLA Ops:
  1.9 5.9 %collective-permute-start.4 = (bf16[2,32,8192]{2,1,0:T(8,128)(2,1)S(1)}, bf16[2,32,8192]{2,1,0:T(8,128)(2,1)S(1)}, u32[]{:S(2)}, u32[]{:S(2)}) collective-permute-start(bf16[2,32,8192]{2,1,0:T(8,128)(2,1)S(1)} %cross.3), channel_id=1, source_target_pairs={{0,4},{4,0},{1,5},{5,1},{2,6},{6,2},{3,7},{7,3},{8,12},{12,8},{9,1... | collective-permute-start | bytes 3145736 | tf_op jit(solution)/shard_map/ppermute | solution.py:302
  6.4 7.2 %collective-permute-start = (bf16[2,32,8192]{2,1,0:T(8,128)(2,1)S(1)}, bf16[2,32,8192]{2,1,0:T(8,128)(2,1)S(1)}, u32[]{:S(2)}, u32[]{:S(2)}) collective-permute-start(bf16[2,32,8192]{2,1,0:T(8,128)(2,1)S(1)} %cross.2), channel_id=1, source_target_pairs={{0,4},{4,0},{1,5},{5,1},{2,6},{6,2},{3,7},{7,3},{8,12},{12,8},{9,1... | collective-permute-start | bytes 3145736 | tf_op jit(solution)/shard_map/ppermute | solution.py:302
  8.4 16.2 %collective-permute-start.5 = (f32[64,4,8,128]{3,2,1,0:T(8,128)S(1)}, f32[64,4,8,128]{3,2,1,0:T(8,128)S(1)}, u32[]{:S(2)}, u32[]{:S(2)}) collective-permute-start(f32[64,4,8,128]{3,2,1,0:T(8,128)S(1)} %get-tuple-element.33), channel_id=1, source_target_pairs={{0,24},{4,228},{8,16},{12,236},{16,8},{20,244},{24,0},{28,252},{32... | collective-permute-start | bytes 3145736 | tf_op jit(solution)/shard_map/ppermute | solution.py:307
  13.6 25.8 %copy-start.2 = (s32[128,1]{0,1:T(1,128)S(1)}, s32[128,1]{0,1:T(1,128)}, u32[]{:S(2)}) copy-start(s32[128,1]{0,1:T(1,128)} %param.7) | copy-start | bytes 1540
  14.3 13.7 %collective-permute-start.1 = (f32[64,4,8,128]{3,2,1,0:T(8,128)S(1)}, f32[64,4,8,128]{3,2,1,0:T(8,128)S(1)}, u32[]{:S(2)}, u32[]{:S(2)}) collective-permute-start(f32[64,4,8,128]{3,2,1,0:T(8,128)S(1)} %get-tuple-element.27), channel_id=1, source_target_pairs={{0,8},{4,36},{8,0},{12,44},{16,24},{20,52},{24,16},{28,60},{32,40}... | collective-permute-start | bytes 3145736 | tf_op jit(solution)/shard_map/ppermute | solution.py:307
  24.9 9.6 %collective-permute-start.6 = (f32[64,2,8,128]{3,2,1,0:T(8,128)S(1)}, f32[64,2,8,128]{3,2,1,0:T(8,128)S(1)}, u32[]{:S(2)}, u32[]{:S(2)}) collective-permute-start(f32[64,2,8,128]{3,2,1,0:T(8,128)S(1)} %get-tuple-element.35), channel_id=1, source_target_pairs={{0,224},{4,28},{8,232},{12,20},{16,240},{20,12},{24,248},{28,4},{3... | collective-permute-start | bytes 1572872 | tf_op jit(solution)/shard_map/ppermute | solution.py:307
  28.0 29.9 %copy-start = (f32[1,3,64,256]{3,2,1,0:T(8,128)S(1)}, f32[1,3,64,256]{3,2,1,0:T(8,128)}, u32[]{:S(2)}) copy-start(f32[1,3,64,256]{3,2,1,0:T(8,128)} %param.5) | copy-start | bytes 589828
  28.3 8.4 %collective-permute-start.2 = (f32[64,2,8,128]{3,2,1,0:T(8,128)S(1)}, f32[64,2,8,128]{3,2,1,0:T(8,128)S(1)}, u32[]{:S(2)}, u32[]{:S(2)}) collective-permute-start(f32[64,2,8,128]{3,2,1,0:T(8,128)S(1)} %get-tuple-element.29), channel_id=1, source_target_pairs={{0,32},{4,12},{8,40},{12,4},{16,48},{20,28},{24,56},{28,20},{32,0}... | collective-permute-start | bytes 1572872 | tf_op jit(solution)/shard_map/ppermute | solution.py:307
  34.6 5.7 %collective-permute-start.7 = (f32[64,8,128]{2,1,0:T(8,128)S(1)}, f32[64,8,128]{2,1,0:T(8,128)S(1)}, u32[]{:S(2)}, u32[]{:S(2)}) collective-permute-start(f32[64,8,128]{2,1,0:T(8,128)S(1)} %get-tuple-element.37), channel_id=1, source_target_pairs={{0,8},{4,12},{8,0},{12,4},{16,24},{20,28},{24,16},{28,20},{32,40},... | collective-permute-start | bytes 786440 | tf_op jit(solution)/shard_map/ppermute | solution.py:307
  36.8 6.5 %collective-permute-start.3 = (f32[64,8,128]{2,1,0:T(8,128)S(1)}, f32[64,8,128]{2,1,0:T(8,128)S(1)}, u32[]{:S(2)}, u32[]{:S(2)}) collective-permute-start(f32[64,8,128]{2,1,0:T(8,128)S(1)} %get-tuple-element.31), channel_id=1, source_target_pairs={{0,24},{4,28},{8,16},{12,20},{16,8},{20,12},{24,0},{28,4},{32,56},... | collective-permute-start | bytes 786440 | tf_op jit(solution)/shard_map/ppermute | solution.py:307
  45.0 71.4 %copy-start.1 = (f32[2,1,16384]{2,1,0:T(1,128)S(1)}, f32[2,1,16384]{2,1,0:T(1,128)}, u32[]{:S(2)}) copy-start(f32[2,1,16384]{2,1,0:T(1,128)} %weights_ref.1) | copy-start | bytes 393220
  45.0 44.0 %all-to-all-start = ((f32[256,8,128]{2,1,0:T(8,128)}), f32[256,8,128]{2,1,0:T(8,128)S(1)}, u32[]{:S(2)}, u32[]{:S(2)}) async-start(f32[256,8,128]{2,1,0:T(8,128)} %pack.1), calls=%async_computation | async-start | bytes 2097152 | tf_op jit(solution)/shard_map/all_to_all | solution.py:311
  57.9 4.6 %collective-permute-start.10 = (f32[64,256]{1,0:T(8,128)S(1)}, f32[64,256]{1,0:T(8,128)S(1)}, u32[]{:S(2)}, u32[]{:S(2)}) collective-permute-start(f32[64,256]{1,0:T(8,128)S(1)} %get-tuple-element.40), channel_id=1, source_target_pairs={{0,3},{1,0},{2,1},{3,2},{4,7},{5,4},{6,5},{7,6},{8,11},{9,8},{10,9... | collective-permute-start | bytes 196616 | tf_op jit(solution)/shard_map/ppermute | solution.py:292
  60.6 5.8 %collective-permute-start.8 = (f32[64,256]{1,0:T(8,128)S(1)}, f32[64,256]{1,0:T(8,128)S(1)}, u32[]{:S(2)}, u32[]{:S(2)}) collective-permute-start(f32[64,256]{1,0:T(8,128)S(1)} %get-tuple-element.38), channel_id=1, source_target_pairs={{0,1},{1,2},{2,3},{3,0},{4,5},{5,6},{6,7},{7,4},{8,9},{9,10},{10,1... | collective-permute-start | bytes 196616 | tf_op jit(solution)/shard_map/ppermute | solution.py:292
  60.6 6.6 %collective-permute-start.9 = (f32[64,256]{1,0:T(8,128)S(1)}, f32[64,256]{1,0:T(8,128)S(1)}, u32[]{:S(2)}, u32[]{:S(2)}) collective-permute-start(f32[64,256]{1,0:T(8,128)S(1)} %get-tuple-element.39), channel_id=1, source_target_pairs={{0,2},{1,3},{2,0},{3,1},{4,6},{5,7},{6,4},{7,5},{8,10},{9,11},{10,... | collective-permute-start | bytes 196616 | tf_op jit(solution)/shard_map/ppermute | solution.py:292
  94.7 21.7 %all-to-all-start.1 = ((f32[256,1,256]{2,1,0:T(1,128)}), f32[256,1,256]{2,1,0:T(1,128)S(1)}, u32[]{:S(2)}, u32[]{:S(2)}) async-start(f32[256,1,256]{2,1,0:T(1,128)} %bitcast.5), calls=%async_computation.1 | async-start | bytes 524288 | tf_op jit(solution)/shard_map/all_to_all | solution.py:316
  101.0 5.0 %collective-permute-start.11 = (f32[64,256]{1,0:T(8,128)S(1)}, f32[64,256]{1,0:T(8,128)S(1)}, u32[]{:S(2)}, u32[]{:S(2)}) collective-permute-start(f32[64,256]{1,0:T(8,128)S(1)} %get-tuple-element.43), channel_id=1, source_target_pairs={{0,1},{1,2},{2,3},{3,0},{4,5},{5,6},{6,7},{7,4},{8,9},{9,10},{10,1... | collective-permute-start | bytes 196616 | tf_op jit(solution)/shard_map/ppermute | solution.py:292
  102.5 6.7 %collective-permute-start.12 = (f32[64,256]{1,0:T(8,128)S(1)}, f32[64,256]{1,0:T(8,128)S(1)}, u32[]{:S(2)}, u32[]{:S(2)}) collective-permute-start(f32[64,256]{1,0:T(8,128)S(1)} %get-tuple-element.44), channel_id=1, source_target_pairs={{0,2},{1,3},{2,0},{3,1},{4,6},{5,7},{6,4},{7,5},{8,10},{9,11},{10,... | collective-permute-start | bytes 196616 | tf_op jit(solution)/shard_map/ppermute | solution.py:292
  104.9 4.2 %collective-permute-start.13 = (f32[64,256]{1,0:T(8,128)S(1)}, f32[64,256]{1,0:T(8,128)S(1)}, u32[]{:S(2)}, u32[]{:S(2)}) collective-permute-start(f32[64,256]{1,0:T(8,128)S(1)} %get-tuple-element.45), channel_id=1, source_target_pairs={{0,3},{1,0},{2,1},{3,2},{4,7},{5,4},{6,5},{7,6},{8,11},{9,8},{10,9... | collective-permute-start | bytes 196616 | tf_op jit(solution)/shard_map/ppermute | solution.py:292

commit v5 on v4

v5 whole, which is shorter than its diff:
```python
import functools
import math

import jax
import jax.numpy as jnp
from jax import lax
from jax.experimental import pallas as pl
from jax.experimental.pallas import tpu as pltpu
from jax.sharding import Mesh, PartitionSpec as P

HEADS = 64
RANK = 256
COLS = 256
L = 2
ITERS = 5
MATS = L * HEADS
CAP = 3
SIZES = (16, 16, 16, 16)
KINDS = (0, 1, 0, 1)
FIRST = tuple(sum(SIZES[:group]) for group in range(len(SIZES)))
OWNERS = 64
DEVICES = 256
ALL = ("y", "z", "x", "core")

quintic_a = 3.4445
quintic_b = -4.775
quintic_c = 2.0315
momentum_beta = 0.95
learn_rate = 0.02
decay_rate = 0.1
rms_factor = 0.2
norm_epsilon = 1e-07
VMEM_LIMIT = 32 * 1024 * 1024

f32 = jnp.float32
bf16 = jnp.bfloat16


def targets(table):
    owners = table[:, 0]
    index = jnp.arange(MATS, dtype=jnp.int32)
    before = (owners[:, None] == owners[None, :]) & (index[:, None] < index[None, :])
    slots = jnp.sum(before.astype(jnp.int32), axis=0)
    return owners, slots


def params():
    return pltpu.CompilerParams(vmem_limit_bytes=VMEM_LIMIT)


def lanes_of(head, half):
    return pl.ds(pl.multiple_of(head * COLS + half * 128, 128), 128)


def rows_of(block, size):
    return pl.ds(pl.multiple_of(block * size, size), size)


def bits():
    x = lax.axis_index("x")
    second = x // 2
    return (x + second) % 2, second, lax.axis_index("z") % 2


def middle_bit(kind):
    one, two, three = bits()
    return jnp.where(lax.axis_index("core") == 0, three, two if kind else one)


def rows_kernel(mine, grad_ref, *refs):
    *outs, sems = refs
    core = lax.axis_index("core")
    rows = rows_of(core if mine else 1 - core, 32)
    copies = []
    for group, out in enumerate(outs):
        lanes = slice(FIRST[group] * COLS, (FIRST[group] + SIZES[group]) * COLS)
        for layer in range(L):
            copies.append(pltpu.make_async_copy(grad_ref.at[layer, rows, lanes], out.at[layer], sems.at[group, layer]))
    for copy in copies:
        copy.start()
    for copy in copies:
        copy.wait()


def total(own_ref, got_ref, layer, rows, lanes):
    return own_ref[layer, rows, lanes].astype(f32) + got_ref[layer, rows, lanes].astype(f32)


def first_kernel(kind, size, own_ref, got_ref, send, keep):
    one, two, three = bits()

    @pl.when(lax.axis_index("core") == 0)
    def _():
        @pl.loop(0, size, unroll=2)
        def _(head):
            for layer in range(L):
                at = layer * size + head
                for value, out in ((1 - (two if kind else one), send), ((two if kind else one), keep)):
                    for block in range(2):
                        if kind:
                            both = total(own_ref, got_ref, layer, slice(block * 16, block * 16 + 16), lanes_of(head, value))
                        else:
                            both = total(own_ref, got_ref, layer, rows_of(value, 16), lanes_of(head, block))
                        out[at, 2 * block] = both[:8]
                        out[at, 2 * block + 1] = both[8:]

    @pl.when(lax.axis_index("core") == 1)
    def _():
        @pl.loop(0, size, unroll=2)
        def _(head):
            for layer in range(L):
                at = layer * size + head
                for row in range(2):
                    for lane in range(2):
                        both = total(own_ref, got_ref, layer, slice(row * 16, row * 16 + 16), lanes_of(head, lane))
                        tile = 2 * row + lane if kind else 2 * lane + row
                        send[at, tile] = jnp.where(three == 0, both[8:], both[:8])
                        keep[at, tile] = jnp.where(three == 0, both[:8], both[8:])


def second_kernel(kind, size, kept, got, send, keep):
    bit = middle_bit(kind)

    @pl.loop(0, L * size, unroll=4)
    def _(at):
        for block in range(2):
            for tile, out in ((2 * block + 1 - bit, send), (2 * block + bit, keep)):
                out[at, block] = kept[at, tile] + got[at, tile]


def third_kernel(kind, size, kept, got, send, keep):
    one, two, _ = bits()
    bit = one if kind else two

    @pl.loop(0, L * size, unroll=4)
    def _(at):
        send[at] = kept[at, 1 - bit] + got[at, 1 - bit]
        keep[at] = kept[at, bit] + got[at, bit]


def pack_kernel(place_ref, *refs):
    out_ref = refs[-1]
    for group, size in enumerate(SIZES):
        for layer in range(L):
            for head in range(size):
                where = place_ref[layer * HEADS + FIRST[group] + head]
                out_ref[where] = refs[2 * group][layer * size + head] + refs[2 * group + 1][layer * size + head]


def halves(value):
    high = value.astype(bf16)
    return high, (value - high.astype(f32)).astype(bf16)


def times(left, right, transposed):
    dims = (((1,), (1 if transposed else 0,)), ((), ()))

    def dot(a, b):
        return lax.dot_general(a, b, dims, preferred_element_type=f32)

    (lh, ll), (rh, rl) = left, right
    return dot(lh, rh) + (dot(lh, rl) + dot(ll, rh))


def newton(advance):
    norm = jnp.sqrt(jnp.sum(advance * advance))
    iterate = advance / (norm + norm_epsilon)
    for _ in range(ITERS):
        parts = halves(iterate)
        gram = times(parts, parts, True)
        gram_parts = halves(gram)
        poly = quintic_b * gram + quintic_c * times(gram_parts, gram_parts, False)
        iterate = quintic_a * iterate + times(halves(poly), parts, False)
    return iterate


def update_kernel(place_ref, got_ref, mom_ref, fresh_ref, own_ref, send1_ref, send2_ref, send3_ref, adv):
    me = (lax.axis_index("z") * 4 + lax.axis_index("x")) * 2 + lax.axis_index("core")
    for slot in range(CAP):
        live = jnp.max(jnp.where(place_ref[...] == me * CAP + slot, 1, 0)) > 0
        for x, (one, two) in enumerate(((0, 0), (1, 0), (1, 1), (0, 1))):
            lanes = slice(two * 128, (two + 1) * 128)
            for core in range(2):
                for three in range(2):
                    rows = slice((4 * core + 2 * one + three) * 8, (4 * core + 2 * one + three + 1) * 8)
                    parts = [got_ref[((z * 4 + x) * 2 + core) * CAP + slot] for z in range(three, 8, 2)]
                    g = jnp.where(live, (parts[0] + parts[1]) + (parts[2] + parts[3]), 0.0)
                    new = jnp.where(live, momentum_beta * mom_ref[slot, rows, lanes] + g, 0.0)
                    fresh_ref[slot, rows, lanes] = new
                    adv[slot, rows, lanes] = g + momentum_beta * new
    y = lax.axis_index("y")
    for step, out in enumerate((own_ref, send1_ref, send2_ref, send3_ref)):
        out[...] = adv[jnp.minimum((y + step) % 4, CAP - 1)]


def work_kernel(own_ref, got1_ref, got2_ref, got3_ref, out_ref, adv):
    y = lax.axis_index("y")
    for step, ref in enumerate((own_ref, got1_ref, got2_ref, got3_ref)):
        adv[rows_of((y + 4 - step) % 4, 64), :] = ref[...]
    ortho = newton(adv[...])
    for half in range(2):
        out_ref[pl.ds(half, RANK, stride=2), :] = ortho[:, half * 128 : (half + 1) * 128]


def finish_kernel(target_ref, got_ref, weights_ref, step_ref, new_ref, gathered):
    for at in range(MATS):
        gathered[2 * at : 2 * at + 2, :] = got_ref[pl.ds(2 * target_ref[at], 2), :]
    scale = rms_factor * math.sqrt(max(RANK, COLS))
    step = scale * gathered[...] + decay_rate * weights_ref[...]
    step_ref[...] = step
    new_ref[...] = weights_ref[...] - learn_rate * step


def shape(*dims, dtype=f32):
    return jax.ShapeDtypeStruct(dims, dtype)


def call(kernel, outs, ins, scratch=(), flops=0, moved=1 << 10):
    many = isinstance(outs, tuple)
    out_spec = pl.BlockSpec(memory_space=pltpu.VMEM)
    return pl.pallas_call(
        kernel,
        out_shape=outs,
        in_specs=[pl.BlockSpec(memory_space=pltpu.SMEM if kind == "s" else pltpu.VMEM) for kind in ins],
        out_specs=tuple(out_spec for _ in outs) if many else out_spec,
        scratch_shapes=[pltpu.VMEM(dims, f32) for dims in scratch],
        compiler_params=params(),
        cost_estimate=pl.CostEstimate(flops=flops, bytes_accessed=moved, transcendentals=0),
        name=getattr(kernel, "func", kernel).__name__.removesuffix("_kernel"),
    )


def rows_of_heads(gradient, mine):
    return pl.pallas_call(
        functools.partial(rows_kernel, mine),
        out_shape=tuple(shape(L, 32, size * COLS, dtype=bf16) for size in SIZES),
        in_specs=[pl.BlockSpec(memory_space=pltpu.HBM)],
        out_specs=tuple(pl.BlockSpec(memory_space=pltpu.VMEM) for _ in SIZES),
        scratch_shapes=[pltpu.SemaphoreType.DMA((len(SIZES), L))],
        compiler_params=params(),
        cost_estimate=pl.CostEstimate(flops=0, bytes_accessed=1 << 10, transcendentals=0),
        name="own" if mine else "cross",
    )(pltpu.with_memory_space_constraint(gradient, pltpu.HBM))


def route(moves):
    pairs = []
    for z in range(8):
        for x in range(4):
            for core, move in enumerate(moves):
                to_z, to_x = move(z, x)
                pairs.append(((z * 4 + x) * 2 + core, (to_z * 4 + to_x) * 2 + core))
    return pairs


def near(z, x):
    return z, x ^ 1


def far(z, x):
    return z, 3 - x


def pair(z, x):
    return z ^ 1, x


def link(z, x):
    return (z + 1 if z % 2 else z - 1) % 8, x


ROUTES = (
    (route((near, pair)), route((pair, near)), route((far, far))),
    (route((far, link)), route((link, far)), route((near, near))),
)


def along_y(values):
    return [
        lax.ppermute(value, "y", [(i, (i + step) % 4) for i in range(4)]) for step, value in enumerate(values, start=1)
    ]


def on_device(gradient, momentum, weights, table):
    owners, slots = targets(table)
    local = gradient[0]

    dp = ("z", "x", "core")
    crossed = [lax.ppermute(rows, "core", [(0, 1), (1, 0)]) for rows in rows_of_heads(local, False)]
    parts = list(zip(rows_of_heads(local, True), crossed))
    for step, (kernel, dims) in enumerate(((first_kernel, (4, 8, 128)), (second_kernel, (2, 8, 128)), (third_kernel, (8, 128)))):
        for group, (kind, size) in enumerate(zip(KINDS, SIZES)):
            send, keep = call(functools.partial(kernel, kind, size), (shape(L * size, *dims),) * 2, "vv")(*parts[group])
            parts[group] = keep, lax.ppermute(send, dp, ROUTES[kind][step])

    place = owners * CAP + slots
    outgoing = call(pack_kernel, shape(OWNERS * CAP, 8, 128), "s" + "vv" * len(SIZES))(place, *sum(parts, ()))
    got = lax.all_to_all(outgoing, dp, 0, 0, tiled=True)
    outs = (shape(CAP, 64, COLS),) + (shape(64, COLS),) * 4
    fresh, mine, *sends = call(update_kernel, outs, "vvv", [(CAP, 64, COLS)])(place.reshape(1, MATS), got, momentum[0])
    ortho = call(work_kernel, shape(2 * RANK, 128), "vvvv", [(RANK, COLS)], 15 * 3 * 2 * 256**3)(mine, *along_y(sends))
    returned = lax.all_to_all(ortho.reshape(DEVICES, 1, COLS), ALL, 0, 0, tiled=True).reshape(2 * DEVICES, 128)
    step_update, new_weights = call(finish_kernel, (shape(2 * MATS, 128),) * 2, "svv", [(2 * MATS, 128)])(
        slots * OWNERS + owners, returned, weights.reshape(2 * MATS, 128)
    )
    return fresh[None], step_update.reshape(weights.shape), new_weights.reshape(weights.shape)


def solution(mesh):
    fine = Mesh(mesh.devices.reshape(8, 4, 2, 4), ("z", "x", "core", "y"))
    dp = ("z", "x", "core")
    return jax.shard_map(
        on_device,
        mesh=fine,
        in_specs=(
            P(dp, None, "y", None),
            P(dp, None, "y", None),
            P(None, ("y",) + dp, None),
            P(),
        ),
        out_specs=(
            P(dp, None, "y", None),
            P(None, ("y",) + dp, None),
            P(None, ("y",) + dp, None),
        ),
        check_vma=False,
    )
```

time: 118 us -> 115 us (0.975)
  blocking collectives: 0 us -> 24.7 us
  waiting for transfers between devices: 58.6 us -> 36.4 us
  starting transfers between devices: 42.5 us -> 39.2 us
  Pallas kernels: 15.9 us -> 13.9 us
    all_to_all x0 -> x1, blocking collectives: none -> 24.7 us  [on_device(): lax.all_to_all(ortho.reshape(DEVICES, 1, COLS), ALL, 0, 0, tiled=True)]
    ppermute x8 -> x16, waiting for transfers between devices: 21.6 us -> 11 us  [the longest x12 11 us: on_device(): parts[group] = (keep, lax.ppermute(send, dp, ROUTES[kind][step]))]
    ppermute x8 -> x16, starting transfers between devices: 13.9 us -> 22.2 us  [the longest x12 18.3 us: on_device(): parts[group] = (keep, lax.ppermute(send, dp, ROUTES[kind][step]))]
    all_to_all x2 -> x1, starting transfers between devices: 19.2 us -> 12.1 us  [on_device(): got = lax.all_to_all(outgoing, dp, 0, 0, tiled=True)]
    all_to_all x2 -> x1, waiting for transfers between devices: 29 us -> 22.7 us  [on_device(): got = lax.all_to_all(outgoing, dp, 0, 0, tiled=True)]
    ppermute x6 -> x3, waiting for transfers between devices: 8 us -> 2.63 us  [along_y(): lax.ppermute(value, 'y', [(i, (i + step) % 4) for i in range(4)])]
    ppermute x6 -> x3, starting transfers between devices: 9.49 us -> 4.99 us  [along_y(): lax.ppermute(value, 'y', [(i, (i + step) % 4) for i in range(4)])]
    pallas_call x14 -> x18, Pallas kernels: 15.9 us -> 13.9 us  [the longest x1 4.78 us: on_device(): call(work_kernel, shape(2 * RANK, 128), 'vvvv', [(RANK, COLS)], 15 * 3 *...]
  transfers between devices with their start and end apart: 16 -> 20, of which waited for: 12 -> 9; matrix products, arithmetic and copies ran while one was open for 0% -> 0% of each run, Pallas kernels for 5% -> 3%
where the time goes in v5:
time: 115 us
  starting transfers between devices  39.2 us (34%)
  waiting for transfers between devices  36.4 us (32%)
  blocking collectives  24.7 us (21%)
  Pallas kernels  13.9 us (12%)
    all_to_all x1, blocking collectives, on_device(): lax.all_to_all(ortho.reshape(DEVICES, 1, COLS), ALL, 0, 0, tiled=True)  24.7 us
    all_to_all x1, waiting for transfers between devices, on_device(): got = lax.all_to_all(outgoing, dp, 0, 0, tiled=True)  22.7 us
    ppermute x12, starting transfers between devices, on_device(): parts[group] = (keep, lax.ppermute(send, dp, ROUTES[kind][step]))  18.3 us
    all_to_all x1, starting transfers between devices, on_device(): got = lax.all_to_all(outgoing, dp, 0, 0, tiled=True)  12.1 us
    ppermute x12, waiting for transfers between devices, on_device(): parts[group] = (keep, lax.ppermute(send, dp, ROUTES[kind][step]))  11 us
    ppermute x3, starting transfers between devices, along_y(): lax.ppermute(value, 'y', [(i, (i + step) % 4) for i in range(4)])  4.99 us
    pallas_call x1, Pallas kernels, on_device(): call(work_kernel, shape(2 * RANK, 128), 'vvvv', [(RANK, COLS)], 15 * 3 *...  4.78 us
    ppermute x4, starting transfers between devices, on_device(): lax.ppermute(rows, 'core', [(0, 1), (1, 0)])  3.94 us
  transfers between devices with their start and end apart: 20, of which 9 were waited for; matrix products, arithmetic and copies ran while one was open for 0% of the time, Pallas kernels for 3%

profile of v5, /device:TPU:1, one launch (start us, length us, event | category | flops | bytes accessed | tf_op | source)
XLA Modules:
  0.0 115.2 jit_solution(17543534555801442785)
XLA Ops:
  0.6 1.6 %cross.1 = (bf16[2,32,4096]{2,1,0:T(8,128)(2,1)S(1)}, bf16[2,32,4096]{2,1,0:T(8,128)(2,1)S(1)}, bf16[2,32,4096]{2,1,0:T(8,128)(2,1)S(1)}, bf16[2,32,4096]{2,1,0:T(8,128)(2,1)S(1)}) custom-call(bf16[2,64,16384]{2,1,0:T(8,128)(2,1)} %bitcast.19), custom_call_target="tpu_custom_call" | custom-call | bytes 1024 | tf_op jit(solution)/shard_map/cross/pallas_call | solution.py:234
  2.2 3.3 %collective-permute-start.12 = (bf16[2,32,4096]{2,1,0:T(8,128)(2,1)S(1)}, bf16[2,32,4096]{2,1,0:T(8,128)(2,1)S(1)}, u32[]{:S(2)}, u32[]{:S(2)}) collective-permute-start(bf16[2,32,4096]{2,1,0:T(8,128)(2,1)S(1)} %get-tuple-element.67), channel_id=1, source_target_pairs={{0,4},{4,0},{1,5},{5,1},{2,6},{6,2},{3,7},{7,3},{8,12},{12,8},{9,1... | collective-permute-start | bytes 1572872 | tf_op jit(solution)/shard_map/ppermute | solution.py:289
  6.2 1.6 %own.1 = (bf16[2,32,4096]{2,1,0:T(8,128)(2,1)S(1)}, bf16[2,32,4096]{2,1,0:T(8,128)(2,1)S(1)}, bf16[2,32,4096]{2,1,0:T(8,128)(2,1)S(1)}, bf16[2,32,4096]{2,1,0:T(8,128)(2,1)S(1)}) custom-call(bf16[2,64,16384]{2,1,0:T(8,128)(2,1)} %bitcast.20), custom_call_target="tpu_custom_call" | custom-call | bytes 1024 | tf_op jit(solution)/shard_map/own/pallas_call | solution.py:234
  8.1 3.9 %collective-permute-start.13 = (f32[32,4,8,128]{3,2,1,0:T(8,128)S(1)}, f32[32,4,8,128]{3,2,1,0:T(8,128)S(1)}, u32[]{:S(2)}, u32[]{:S(2)}) collective-permute-start(f32[32,4,8,128]{3,2,1,0:T(8,128)S(1)} %get-tuple-element.69), channel_id=1, source_target_pairs={{0,24},{4,228},{8,16},{12,236},{16,8},{20,244},{24,0},{28,252},{32... | collective-permute-start | bytes 1572872 | tf_op jit(solution)/shard_map/ppermute | solution.py:294
  12.8 1.5 %collective-permute-start.5 = (f32[32,4,8,128]{3,2,1,0:T(8,128)S(1)}, f32[32,4,8,128]{3,2,1,0:T(8,128)S(1)}, u32[]{:S(2)}, u32[]{:S(2)}) collective-permute-start(f32[32,4,8,128]{3,2,1,0:T(8,128)S(1)} %get-tuple-element.53), channel_id=1, source_target_pairs={{0,24},{4,228},{8,16},{12,236},{16,8},{20,244},{24,0},{28,252},{32... | collective-permute-start | bytes 1572872 | tf_op jit(solution)/shard_map/ppermute | solution.py:294
  15.4 3.5 %collective-permute-done.13.got = f32[32,4,8,128]{3,2,1,0:T(8,128)S(1)} collective-permute-done((f32[32,4,8,128]{3,2,1,0:T(8,128)S(1)}, f32[32,4,8,128]{3,2,1,0:T(8,128)S(1)}, u32[]{:S(2)}, u32[]{:S(2)}) %collective-permute-start.13) | collective-permute-done | bytes 524320 | tf_op jit(solution)/shard_map/ppermute | solution.py:294
  19.0 2.6 %collective-permute-start.14 = (f32[32,2,8,128]{3,2,1,0:T(8,128)S(1)}, f32[32,2,8,128]{3,2,1,0:T(8,128)S(1)}, u32[]{:S(2)}, u32[]{:S(2)}) collective-permute-start(f32[32,2,8,128]{3,2,1,0:T(8,128)S(1)} %get-tuple-element.71), channel_id=1, source_target_pairs={{0,224},{4,28},{8,232},{12,20},{16,240},{20,12},{24,248},{28,4},{3... | collective-permute-start | bytes 786440 | tf_op jit(solution)/shard_map/ppermute | solution.py:294
  22.2 2.3 %collective-permute-done.5.got = f32[32,4,8,128]{3,2,1,0:T(8,128)S(1)} collective-permute-done((f32[32,4,8,128]{3,2,1,0:T(8,128)S(1)}, f32[32,4,8,128]{3,2,1,0:T(8,128)S(1)}, u32[]{:S(2)}, u32[]{:S(2)}) %collective-permute-start.5) | collective-permute-done | bytes 524320 | tf_op jit(solution)/shard_map/ppermute | solution.py:294
  24.7 2.3 %collective-permute-start.6 = (f32[32,2,8,128]{3,2,1,0:T(8,128)S(1)}, f32[32,2,8,128]{3,2,1,0:T(8,128)S(1)}, u32[]{:S(2)}, u32[]{:S(2)}) collective-permute-start(f32[32,2,8,128]{3,2,1,0:T(8,128)S(1)} %get-tuple-element.55), channel_id=1, source_target_pairs={{0,224},{4,28},{8,232},{12,20},{16,240},{20,12},{24,248},{28,4},{3... | collective-permute-start | bytes 786440 | tf_op jit(solution)/shard_map/ppermute | solution.py:294
  27.1 1.5 %collective-permute-start.2 = (f32[32,2,8,128]{3,2,1,0:T(8,128)S(1)}, f32[32,2,8,128]{3,2,1,0:T(8,128)S(1)}, u32[]{:S(2)}, u32[]{:S(2)}) collective-permute-start(f32[32,2,8,128]{3,2,1,0:T(8,128)S(1)} %get-tuple-element.47), channel_id=1, source_target_pairs={{0,32},{4,12},{8,40},{12,4},{16,48},{20,28},{24,56},{28,20},{32,0}... | collective-permute-start | bytes 786440 | tf_op jit(solution)/shard_map/ppermute | solution.py:294
  29.0 2.0 %collective-permute-start.11 = (f32[32,8,128]{2,1,0:T(8,128)S(1)}, f32[32,8,128]{2,1,0:T(8,128)S(1)}, u32[]{:S(2)}, u32[]{:S(2)}) collective-permute-start(f32[32,8,128]{2,1,0:T(8,128)S(1)} %get-tuple-element.65), channel_id=1, source_target_pairs={{0,24},{4,28},{8,16},{12,20},{16,8},{20,12},{24,0},{28,4},{32,56},... | collective-permute-start | bytes 393224 | tf_op jit(solution)/shard_map/ppermute | solution.py:294
  31.2 1.3 %collective-permute-start.7 = (f32[32,8,128]{2,1,0:T(8,128)S(1)}, f32[32,8,128]{2,1,0:T(8,128)S(1)}, u32[]{:S(2)}, u32[]{:S(2)}) collective-permute-start(f32[32,8,128]{2,1,0:T(8,128)S(1)} %get-tuple-element.57), channel_id=1, source_target_pairs={{0,8},{4,12},{8,0},{12,4},{16,24},{20,28},{24,16},{28,20},{32,40},... | collective-permute-start | bytes 393224 | tf_op jit(solution)/shard_map/ppermute | solution.py:294
  32.7 1.7 %collective-permute-start.3 = (f32[32,8,128]{2,1,0:T(8,128)S(1)}, f32[32,8,128]{2,1,0:T(8,128)S(1)}, u32[]{:S(2)}, u32[]{:S(2)}) collective-permute-start(f32[32,8,128]{2,1,0:T(8,128)S(1)} %get-tuple-element.49), channel_id=1, source_target_pairs={{0,24},{4,28},{8,16},{12,20},{16,8},{20,12},{24,0},{28,4},{32,56},... | collective-permute-start | bytes 393224 | tf_op jit(solution)/shard_map/ppermute | solution.py:294
  34.5 1.7 %collective-permute-done.7.refs_3_ = f32[32,8,128]{2,1,0:T(8,128)S(1)} collective-permute-done((f32[32,8,128]{2,1,0:T(8,128)S(1)}, f32[32,8,128]{2,1,0:T(8,128)S(1)}, u32[]{:S(2)}, u32[]{:S(2)}) %collective-permute-start.7) | collective-permute-done | bytes 131104 | tf_op jit(solution)/shard_map/ppermute | solution.py:294
  36.1 3.3 %collective-permute-done.3.refs_1_ = f32[32,8,128]{2,1,0:T(8,128)S(1)} collective-permute-done((f32[32,8,128]{2,1,0:T(8,128)S(1)}, f32[32,8,128]{2,1,0:T(8,128)S(1)}, u32[]{:S(2)}, u32[]{:S(2)}) %collective-permute-start.3) | collective-permute-done | bytes 131104 | tf_op jit(solution)/shard_map/ppermute | solution.py:294
  39.4 1.5 %pack.1 = f32[192,8,128]{2,1,0:T(8,128)} custom-call(s32[128]{0:T(128)S(1)} %get-tuple-element.91.place_ref, f32[32,8,128]{2,1,0:T(8,128)S(1)} %get-tuple-element.48.refs_0_, f32[32,8,128]{2,1,0:T(8,128)S(1)} %collective-permute-done.3.refs_1_, f32[32,8,128]{2,1,0:T(8,128)S(1)} %get-tuple-element.56.refs_2_, ...), custom_call_target="tpu_custom_call" | custom-call | bytes 1024 | tf_op jit(solution)/shard_map/pack/pallas_call | solution.py:297
  40.9 12.1 %all-to-all-start = ((f32[192,8,128]{2,1,0:T(8,128)}), f32[192,8,128]{2,1,0:T(8,128)S(1)}, u32[]{:S(2)}, u32[]{:S(2)}) async-start(f32[192,8,128]{2,1,0:T(8,128)} %pack.1), calls=%async_computation | async-start | bytes 1572864 | tf_op jit(solution)/shard_map/all_to_all | solution.py:298
  53.0 22.7 %all-to-all-done.got_ref = f32[192,8,128]{2,1,0:T(8,128)S(1)} async-done(((f32[192,8,128]{2,1,0:T(8,128)}), f32[192,8,128]{2,1,0:T(8,128)S(1)}, u32[]{:S(2)}, u32[]{:S(2)}) %all-to-all-start) | async-done | bytes 786464 | tf_op jit(solution)/shard_map/all_to_all | solution.py:298
  76.7 1.3 %collective-permute-start.16 = (f32[64,256]{1,0:T(8,128)S(1)}, f32[64,256]{1,0:T(8,128)S(1)}, u32[]{:S(2)}, u32[]{:S(2)}) collective-permute-start(f32[64,256]{1,0:T(8,128)S(1)} %get-tuple-element.76), channel_id=1, source_target_pairs={{0,1},{1,2},{2,3},{3,0},{4,5},{5,6},{6,7},{7,4},{8,9},{9,10},{10,1... | collective-permute-start | bytes 196616 | tf_op jit(solution)/shard_map/ppermute | solution.py:280
  78.0 2.6 %collective-permute-start.17 = (f32[64,256]{1,0:T(8,128)S(1)}, f32[64,256]{1,0:T(8,128)S(1)}, u32[]{:S(2)}, u32[]{:S(2)}) collective-permute-start(f32[64,256]{1,0:T(8,128)S(1)} %get-tuple-element.77), channel_id=1, source_target_pairs={{0,2},{1,3},{2,0},{3,1},{4,6},{5,7},{6,4},{7,5},{8,10},{9,11},{10,... | collective-permute-start | bytes 196616 | tf_op jit(solution)/shard_map/ppermute | solution.py:280
  81.7 1.4 %collective-permute-done.17.got2_ref = f32[64,256]{1,0:T(8,128)S(1)} collective-permute-done((f32[64,256]{1,0:T(8,128)S(1)}, f32[64,256]{1,0:T(8,128)S(1)}, u32[]{:S(2)}, u32[]{:S(2)}) %collective-permute-start.17) | collective-permute-done | bytes 65568 | tf_op jit(solution)/shard_map/ppermute | solution.py:280
  84.3 4.8 %work.1 = f32[512,128]{1,0:T(8,128)S(1)} custom-call(f32[64,256]{1,0:T(8,128)S(1)} %get-tuple-element.75.own_ref, f32[64,256]{1,0:T(8,128)S(1)} %collective-permute-done.16.got1_ref, f32[64,256]{1,0:T(8,128)S(1)} %collective-permute-done.17.got2_ref, f32[64,256]{1,0:T(8,128)S(1)} %collective-permute-done.18.got3_ref), custom_call_target="tpu_custom_call" | custom-call | flops 1509949440 | bytes 1024 | tf_op jit(solution)/shard_map/work/pallas_call | solution.py:301
  89.1 24.7 %all_to_all.10 = f32[256,1,256]{2,1,0:T(1,128)S(1)} all-to-all(f32[256,1,256]{2,1,0:T(1,128)S(1)} %bitcast.16), channel_id=1, replica_groups=mesh['z'=8,'x'=4,'core'=2,'y'=4] {'y','z','x','core'}, dimensions={0} | all-to-all | bytes 524288 | tf_op jit(solution)/shard_map/all_to_all | solution.py:302
  113.8 1.4 %finish.1 = (f32[256,128]{1,0:T(8,128)}, f32[256,128]{1,0:T(8,128)}) custom-call(s32[128]{0:T(128)S(1)} %get-tuple-element.90.target_ref, f32[512,128]{1,0:T(8,128)S(1)} %bitcast.15, f32[256,128]{1,0:T(8,128)S(1)} %bitcast.18), custom_call_target="tpu_custom_call" | custom-call | bytes 1024 | tf_op jit(solution)/shard_map/finish/pallas_call | solution.py:303
  (44 shorter events, 7.9 us)
Async XLA Ops:
  2.2 5.5 %collective-permute-start.12 = (bf16[2,32,4096]{2,1,0:T(8,128)(2,1)S(1)}, bf16[2,32,4096]{2,1,0:T(8,128)(2,1)S(1)}, u32[]{:S(2)}, u32[]{:S(2)}) collective-permute-start(bf16[2,32,4096]{2,1,0:T(8,128)(2,1)S(1)} %get-tuple-element.67), channel_id=1, source_target_pairs={{0,4},{4,0},{1,5},{5,1},{2,6},{6,2},{3,7},{7,3},{8,12},{12,8},{9,1... | collective-permute-start | bytes 1572872 | tf_op jit(solution)/shard_map/ppermute | solution.py:289
  5.5 6.5 %collective-permute-start.8 = (bf16[2,32,4096]{2,1,0:T(8,128)(2,1)S(1)}, bf16[2,32,4096]{2,1,0:T(8,128)(2,1)S(1)}, u32[]{:S(2)}, u32[]{:S(2)}) collective-permute-start(bf16[2,32,4096]{2,1,0:T(8,128)(2,1)S(1)} %get-tuple-element.59), channel_id=1, source_target_pairs={{0,4},{4,0},{1,5},{5,1},{2,6},{6,2},{3,7},{7,3},{8,12},{12,8},{9,1... | collective-permute-start | bytes 1572872 | tf_op jit(solution)/shard_map/ppermute | solution.py:289
  5.6 6.8 %collective-permute-start.4 = (bf16[2,32,4096]{2,1,0:T(8,128)(2,1)S(1)}, bf16[2,32,4096]{2,1,0:T(8,128)(2,1)S(1)}, u32[]{:S(2)}, u32[]{:S(2)}) collective-permute-start(bf16[2,32,4096]{2,1,0:T(8,128)(2,1)S(1)} %get-tuple-element.51), channel_id=1, source_target_pairs={{0,4},{4,0},{1,5},{5,1},{2,6},{6,2},{3,7},{7,3},{8,12},{12,8},{9,1... | collective-permute-start | bytes 1572872 | tf_op jit(solution)/shard_map/ppermute | solution.py:289
  6.1 8.2 %collective-permute-start = (bf16[2,32,4096]{2,1,0:T(8,128)(2,1)S(1)}, bf16[2,32,4096]{2,1,0:T(8,128)(2,1)S(1)}, u32[]{:S(2)}, u32[]{:S(2)}) collective-permute-start(bf16[2,32,4096]{2,1,0:T(8,128)(2,1)S(1)} %get-tuple-element.43), channel_id=1, source_target_pairs={{0,4},{4,0},{1,5},{5,1},{2,6},{6,2},{3,7},{7,3},{8,12},{12,8},{9,1... | collective-permute-start | bytes 1572872 | tf_op jit(solution)/shard_map/ppermute | solution.py:289
  7.7 20.9 %copy-start.2 = (s32[128,1]{0,1:T(1,128)S(1)}, s32[128,1]{0,1:T(1,128)}, u32[]{:S(2)}) copy-start(s32[128,1]{0,1:T(1,128)} %param.7) | copy-start | bytes 1540
  8.1 10.8 %collective-permute-start.13 = (f32[32,4,8,128]{3,2,1,0:T(8,128)S(1)}, f32[32,4,8,128]{3,2,1,0:T(8,128)S(1)}, u32[]{:S(2)}, u32[]{:S(2)}) collective-permute-start(f32[32,4,8,128]{3,2,1,0:T(8,128)S(1)} %get-tuple-element.69), channel_id=1, source_target_pairs={{0,24},{4,228},{8,16},{12,236},{16,8},{20,244},{24,0},{28,252},{32... | collective-permute-start | bytes 1572872 | tf_op jit(solution)/shard_map/ppermute | solution.py:294
  12.4 9.3 %collective-permute-start.9 = (f32[32,4,8,128]{3,2,1,0:T(8,128)S(1)}, f32[32,4,8,128]{3,2,1,0:T(8,128)S(1)}, u32[]{:S(2)}, u32[]{:S(2)}) collective-permute-start(f32[32,4,8,128]{3,2,1,0:T(8,128)S(1)} %get-tuple-element.61), channel_id=1, source_target_pairs={{0,8},{4,36},{8,0},{12,44},{16,24},{20,52},{24,16},{28,60},{32,40}... | collective-permute-start | bytes 1572872 | tf_op jit(solution)/shard_map/ppermute | solution.py:294
  12.8 11.7 %collective-permute-start.5 = (f32[32,4,8,128]{3,2,1,0:T(8,128)S(1)}, f32[32,4,8,128]{3,2,1,0:T(8,128)S(1)}, u32[]{:S(2)}, u32[]{:S(2)}) collective-permute-start(f32[32,4,8,128]{3,2,1,0:T(8,128)S(1)} %get-tuple-element.53), channel_id=1, source_target_pairs={{0,24},{4,228},{8,16},{12,236},{16,8},{20,244},{24,0},{28,252},{32... | collective-permute-start | bytes 1572872 | tf_op jit(solution)/shard_map/ppermute | solution.py:294
  14.6 12.3 %collective-permute-start.1 = (f32[32,4,8,128]{3,2,1,0:T(8,128)S(1)}, f32[32,4,8,128]{3,2,1,0:T(8,128)S(1)}, u32[]{:S(2)}, u32[]{:S(2)}) collective-permute-start(f32[32,4,8,128]{3,2,1,0:T(8,128)S(1)} %get-tuple-element.45), channel_id=1, source_target_pairs={{0,8},{4,36},{8,0},{12,44},{16,24},{20,52},{24,16},{28,60},{32,40}... | collective-permute-start | bytes 1572872 | tf_op jit(solution)/shard_map/ppermute | solution.py:294
  19.0 9.7 %collective-permute-start.14 = (f32[32,2,8,128]{3,2,1,0:T(8,128)S(1)}, f32[32,2,8,128]{3,2,1,0:T(8,128)S(1)}, u32[]{:S(2)}, u32[]{:S(2)}) collective-permute-start(f32[32,2,8,128]{3,2,1,0:T(8,128)S(1)} %get-tuple-element.71), channel_id=1, source_target_pairs={{0,224},{4,28},{8,232},{12,20},{16,240},{20,12},{24,248},{28,4},{3... | collective-permute-start | bytes 786440 | tf_op jit(solution)/shard_map/ppermute | solution.py:294
  21.6 54.1 %copy-start = (f32[1,3,64,256]{3,2,1,0:T(8,128)S(1)}, f32[1,3,64,256]{3,2,1,0:T(8,128)}, u32[]{:S(2)}) copy-start(f32[1,3,64,256]{3,2,1,0:T(8,128)} %param.5) | copy-start | bytes 589828
  21.7 7.2 %collective-permute-start.10 = (f32[32,2,8,128]{3,2,1,0:T(8,128)S(1)}, f32[32,2,8,128]{3,2,1,0:T(8,128)S(1)}, u32[]{:S(2)}, u32[]{:S(2)}) collective-permute-start(f32[32,2,8,128]{3,2,1,0:T(8,128)S(1)} %get-tuple-element.63), channel_id=1, source_target_pairs={{0,32},{4,12},{8,40},{12,4},{16,48},{20,28},{24,56},{28,20},{32,0}... | collective-permute-start | bytes 786440 | tf_op jit(solution)/shard_map/ppermute | solution.py:294
  24.7 6.5 %collective-permute-start.6 = (f32[32,2,8,128]{3,2,1,0:T(8,128)S(1)}, f32[32,2,8,128]{3,2,1,0:T(8,128)S(1)}, u32[]{:S(2)}, u32[]{:S(2)}) collective-permute-start(f32[32,2,8,128]{3,2,1,0:T(8,128)S(1)} %get-tuple-element.55), channel_id=1, source_target_pairs={{0,224},{4,28},{8,232},{12,20},{16,240},{20,12},{24,248},{28,4},{3... | collective-permute-start | bytes 786440 | tf_op jit(solution)/shard_map/ppermute | solution.py:294
  27.1 5.6 %collective-permute-start.2 = (f32[32,2,8,128]{3,2,1,0:T(8,128)S(1)}, f32[32,2,8,128]{3,2,1,0:T(8,128)S(1)}, u32[]{:S(2)}, u32[]{:S(2)}) collective-permute-start(f32[32,2,8,128]{3,2,1,0:T(8,128)S(1)} %get-tuple-element.47), channel_id=1, source_target_pairs={{0,32},{4,12},{8,40},{12,4},{16,48},{20,28},{24,56},{28,20},{32,0}... | collective-permute-start | bytes 786440 | tf_op jit(solution)/shard_map/ppermute | solution.py:294
  28.8 5.7 %collective-permute-start.15 = (f32[32,8,128]{2,1,0:T(8,128)S(1)}, f32[32,8,128]{2,1,0:T(8,128)S(1)}, u32[]{:S(2)}, u32[]{:S(2)}) collective-permute-start(f32[32,8,128]{2,1,0:T(8,128)S(1)} %get-tuple-element.73), channel_id=1, source_target_pairs={{0,8},{4,12},{8,0},{12,4},{16,24},{20,28},{24,16},{28,20},{32,40},... | collective-permute-start | bytes 393224 | tf_op jit(solution)/shard_map/ppermute | solution.py:294
  29.0 5.5 %collective-permute-start.11 = (f32[32,8,128]{2,1,0:T(8,128)S(1)}, f32[32,8,128]{2,1,0:T(8,128)S(1)}, u32[]{:S(2)}, u32[]{:S(2)}) collective-permute-start(f32[32,8,128]{2,1,0:T(8,128)S(1)} %get-tuple-element.65), channel_id=1, source_target_pairs={{0,24},{4,28},{8,16},{12,20},{16,8},{20,12},{24,0},{28,4},{32,56},... | collective-permute-start | bytes 393224 | tf_op jit(solution)/shard_map/ppermute | solution.py:294
  31.2 4.9 %collective-permute-start.7 = (f32[32,8,128]{2,1,0:T(8,128)S(1)}, f32[32,8,128]{2,1,0:T(8,128)S(1)}, u32[]{:S(2)}, u32[]{:S(2)}) collective-permute-start(f32[32,8,128]{2,1,0:T(8,128)S(1)} %get-tuple-element.57), channel_id=1, source_target_pairs={{0,8},{4,12},{8,0},{12,4},{16,24},{20,28},{24,16},{28,20},{32,40},... | collective-permute-start | bytes 393224 | tf_op jit(solution)/shard_map/ppermute | solution.py:294
  32.7 6.7 %collective-permute-start.3 = (f32[32,8,128]{2,1,0:T(8,128)S(1)}, f32[32,8,128]{2,1,0:T(8,128)S(1)}, u32[]{:S(2)}, u32[]{:S(2)}) collective-permute-start(f32[32,8,128]{2,1,0:T(8,128)S(1)} %get-tuple-element.49), channel_id=1, source_target_pairs={{0,24},{4,28},{8,16},{12,20},{16,8},{20,12},{24,0},{28,4},{32,56},... | collective-permute-start | bytes 393224 | tf_op jit(solution)/shard_map/ppermute | solution.py:294
  40.9 72.9 %copy-start.1 = (f32[2,1,16384]{2,1,0:T(1,128)S(1)}, f32[2,1,16384]{2,1,0:T(1,128)}, u32[]{:S(2)}) copy-start(f32[2,1,16384]{2,1,0:T(1,128)} %param.6) | copy-start | bytes 393220
  40.9 34.8 %all-to-all-start = ((f32[192,8,128]{2,1,0:T(8,128)}), f32[192,8,128]{2,1,0:T(8,128)S(1)}, u32[]{:S(2)}, u32[]{:S(2)}) async-start(f32[192,8,128]{2,1,0:T(8,128)} %pack.1), calls=%async_computation | async-start | bytes 1572864 | tf_op jit(solution)/shard_map/all_to_all | solution.py:298
  76.7 5.0 %collective-permute-start.16 = (f32[64,256]{1,0:T(8,128)S(1)}, f32[64,256]{1,0:T(8,128)S(1)}, u32[]{:S(2)}, u32[]{:S(2)}) collective-permute-start(f32[64,256]{1,0:T(8,128)S(1)} %get-tuple-element.76), channel_id=1, source_target_pairs={{0,1},{1,2},{2,3},{3,0},{4,5},{5,6},{6,7},{7,4},{8,9},{9,10},{10,1... | collective-permute-start | bytes 196616 | tf_op jit(solution)/shard_map/ppermute | solution.py:280
  78.0 5.1 %collective-permute-start.17 = (f32[64,256]{1,0:T(8,128)S(1)}, f32[64,256]{1,0:T(8,128)S(1)}, u32[]{:S(2)}, u32[]{:S(2)}) collective-permute-start(f32[64,256]{1,0:T(8,128)S(1)} %get-tuple-element.77), channel_id=1, source_target_pairs={{0,2},{1,3},{2,0},{3,1},{4,6},{5,7},{6,4},{7,5},{8,10},{9,11},{10,... | collective-permute-start | bytes 196616 | tf_op jit(solution)/shard_map/ppermute | solution.py:280
  80.6 3.7 %collective-permute-start.18 = (f32[64,256]{1,0:T(8,128)S(1)}, f32[64,256]{1,0:T(8,128)S(1)}, u32[]{:S(2)}, u32[]{:S(2)}) collective-permute-start(f32[64,256]{1,0:T(8,128)S(1)} %get-tuple-element.78), channel_id=1, source_target_pairs={{0,3},{1,0},{2,1},{3,2},{4,7},{5,4},{6,5},{7,6},{8,11},{9,8},{10,9... | collective-permute-start | bytes 196616 | tf_op jit(solution)/shard_map/ppermute | solution.py:280

commit v6 on v5

--- a/solution.py
+++ b/solution.py
@@ -15,7 +15,7 @@
 ITERS = 5
 MATS = L * HEADS
 CAP = 3
-SIZES = (16, 16, 16, 16)
+SIZES = (22, 22, 10, 10)
 KINDS = (0, 1, 0, 1)
 FIRST = tuple(sum(SIZES[:group]) for group in range(len(SIZES)))
 OWNERS = 64
@@ -128,23 +128,31 @@
                 out[at, block] = kept[at, tile] + got[at, tile]
 
 
-def third_kernel(kind, size, kept, got, send, keep):
+def third_kernel(kind, *refs):
+    send, keep = refs[-2:]
     one, two, _ = bits()
     bit = one if kind else two
-
-    @pl.loop(0, L * size, unroll=4)
-    def _(at):
-        send[at] = kept[at, 1 - bit] + got[at, 1 - bit]
-        keep[at] = kept[at, bit] + got[at, bit]
-
-
-def pack_kernel(place_ref, *refs):
-    out_ref = refs[-1]
-    for group, size in enumerate(SIZES):
+    begin = 0
+    for turn, count in enumerate(L * size for group, size in enumerate(SIZES) if KINDS[group] == kind):
+        kept, got = refs[2 * turn : 2 * turn + 2]
+
+        @pl.loop(0, count, unroll=4)
+        def _(at, kept=kept, got=got, begin=begin):
+            send[begin + at] = kept[at, 1 - bit] + got[at, 1 - bit]
+            keep[begin + at] = kept[at, bit] + got[at, bit]
+
+        begin += count
+
+
+def pack_kernel(place_ref, a_ref, got_a_ref, b_ref, got_b_ref, out_ref):
+    begin = [0, 0]
+    for kind, first, size in zip(KINDS, FIRST, SIZES):
+        kept, got = (b_ref, got_b_ref) if kind else (a_ref, got_a_ref)
         for layer in range(L):
             for head in range(size):
-                where = place_ref[layer * HEADS + FIRST[group] + head]
-                out_ref[where] = refs[2 * group][layer * size + head] + refs[2 * group + 1][layer * size + head]
+                at = begin[kind] + layer * size + head
+                out_ref[place_ref[layer * HEADS + first + head]] = kept[at] + got[at]
+        begin[kind] += L * size
 
 
 def halves(value):
@@ -288,13 +296,19 @@
     dp = ("z", "x", "core")
     crossed = [lax.ppermute(rows, "core", [(0, 1), (1, 0)]) for rows in rows_of_heads(local, False)]
     parts = list(zip(rows_of_heads(local, True), crossed))
-    for step, (kernel, dims) in enumerate(((first_kernel, (4, 8, 128)), (second_kernel, (2, 8, 128)), (third_kernel, (8, 128)))):
+    for step, (kernel, dims) in enumerate(((first_kernel, (4, 8, 128)), (second_kernel, (2, 8, 128)))):
         for group, (kind, size) in enumerate(zip(KINDS, SIZES)):
             send, keep = call(functools.partial(kernel, kind, size), (shape(L * size, *dims),) * 2, "vv")(*parts[group])
             parts[group] = keep, lax.ppermute(send, dp, ROUTES[kind][step])
+    last = ()
+    for kind in range(2):
+        held = sum((part for part, is_kind in zip(parts, KINDS) if is_kind == kind), ())
+        outs = (shape(sum(part.shape[0] for part in held[::2]), 8, 128),) * 2
+        send, keep = call(functools.partial(third_kernel, kind), outs, "v" * len(held))(*held)
+        last += keep, lax.ppermute(send, dp, ROUTES[kind][2])
 
     place = owners * CAP + slots
-    outgoing = call(pack_kernel, shape(OWNERS * CAP, 8, 128), "s" + "vv" * len(SIZES))(place, *sum(parts, ()))
+    outgoing = call(pack_kernel, shape(OWNERS * CAP, 8, 128), "svvvv")(place, *last)
     got = lax.all_to_all(outgoing, dp, 0, 0, tiled=True)
     outs = (shape(CAP, 64, COLS),) + (shape(64, COLS),) * 4
     fresh, mine, *sends = call(update_kernel, outs, "vvv", [(CAP, 64, COLS)])(place.reshape(1, MATS), got, momentum[0])

time: 115 us -> 113 us (0.983)
  starting transfers between devices: 39.2 us -> 34.8 us
  waiting for transfers between devices: 36.4 us -> 39.4 us
    ppermute x12 -> x8, starting transfers between devices: 18.3 us -> 13.2 us  [on_device(): parts[group] = (keep, lax.ppermute(send, dp, ROUTES[kind][step]))]
    ppermute x0 -> x2, waiting for transfers between devices: none -> 4.8 us  [on_device(): last += (keep, lax.ppermute(send, dp, ROUTES[kind][2]))]
    ppermute x12 -> x8, waiting for transfers between devices: 11 us -> 8 us  [on_device(): parts[group] = (keep, lax.ppermute(send, dp, ROUTES[kind][step]))]
    ppermute x0 -> x2, starting transfers between devices: none -> 1.7 us  [on_device(): last += (keep, lax.ppermute(send, dp, ROUTES[kind][2]))]
    ppermute x4, waiting for transfers between devices: 0.01 us -> 1.27 us  [on_device(): lax.ppermute(rows, 'core', [(0, 1), (1, 0)])]
    all_to_all x1, starting transfers between devices: 12.1 us -> 10.8 us  [on_device(): got = lax.all_to_all(outgoing, dp, 0, 0, tiled=True)]
  transfers between devices with their start and end apart: 20 -> 18, of which waited for: 9 -> 10; matrix products, arithmetic and copies ran while one was open for 0% -> 0% of each run, Pallas kernels for 3% -> 3%
where the time goes in v6:
time: 113 us
  waiting for transfers between devices  39.4 us (35%)
  starting transfers between devices  34.8 us (31%)
  blocking collectives  24.7 us (22%)
  Pallas kernels  13.3 us (12%)
    all_to_all x1, blocking collectives, on_device(): lax.all_to_all(ortho.reshape(DEVICES, 1, COLS), ALL, 0, 0, tiled=True)  24.7 us
    all_to_all x1, waiting for transfers between devices, on_device(): got = lax.all_to_all(outgoing, dp, 0, 0, tiled=True)  22.7 us
    ppermute x8, starting transfers between devices, on_device(): parts[group] = (keep, lax.ppermute(send, dp, ROUTES[kind][step]))  13.2 us
    all_to_all x1, starting transfers between devices, on_device(): got = lax.all_to_all(outgoing, dp, 0, 0, tiled=True)  10.8 us
    ppermute x8, waiting for transfers between devices, on_device(): parts[group] = (keep, lax.ppermute(send, dp, ROUTES[kind][step]))  8 us
    ppermute x3, starting transfers between devices, along_y(): lax.ppermute(value, 'y', [(i, (i + step) % 4) for i in range(4)])  4.99 us
    ppermute x2, waiting for transfers between devices, on_device(): last += (keep, lax.ppermute(send, dp, ROUTES[kind][2]))  4.8 us
    pallas_call x1, Pallas kernels, on_device(): call(work_kernel, shape(2 * RANK, 128), 'vvvv', [(RANK, COLS)], 15 * 3 *...  4.78 us
  transfers between devices with their start and end apart: 18, of which 10 were waited for; matrix products, arithmetic and copies ran while one was open for 0% of the time, Pallas kernels for 3%

profile of v6, /device:TPU:1, one launch (start us, length us, event | category | flops | bytes accessed | tf_op | source)
XLA Modules:
  0.0 113.1 jit_solution(10789621298381319470)
XLA Ops:
  0.6 1.6 %cross.1 = (bf16[2,32,5632]{2,1,0:T(8,128)(2,1)S(1)}, bf16[2,32,5632]{2,1,0:T(8,128)(2,1)S(1)}, bf16[2,32,2560]{2,1,0:T(8,128)(2,1)S(1)}, bf16[2,32,2560]{2,1,0:T(8,128)(2,1)S(1)}) custom-call(bf16[2,64,16384]{2,1,0:T(8,128)(2,1)} %bitcast.19), custom_call_target="tpu_custom_call" | custom-call | bytes 1024 | tf_op jit(solution)/shard_map/cross/pallas_call | solution.py:242
  2.2 3.3 %collective-permute-start.7 = (bf16[2,32,5632]{2,1,0:T(8,128)(2,1)S(1)}, bf16[2,32,5632]{2,1,0:T(8,128)(2,1)S(1)}, u32[]{:S(2)}, u32[]{:S(2)}) collective-permute-start(bf16[2,32,5632]{2,1,0:T(8,128)(2,1)S(1)} %get-tuple-element.53), channel_id=1, source_target_pairs={{0,4},{4,0},{1,5},{5,1},{2,6},{6,2},{3,7},{7,3},{8,12},{12,8},{9,1... | collective-permute-start | bytes 2162696 | tf_op jit(solution)/shard_map/ppermute | solution.py:297
  5.6 1.6 %own.1 = (bf16[2,32,5632]{2,1,0:T(8,128)(2,1)S(1)}, bf16[2,32,5632]{2,1,0:T(8,128)(2,1)S(1)}, bf16[2,32,2560]{2,1,0:T(8,128)(2,1)S(1)}, bf16[2,32,2560]{2,1,0:T(8,128)(2,1)S(1)}) custom-call(bf16[2,64,16384]{2,1,0:T(8,128)(2,1)} %bitcast.20), custom_call_target="tpu_custom_call" | custom-call | bytes 1024 | tf_op jit(solution)/shard_map/own/pallas_call | solution.py:242
  7.6 3.9 %collective-permute-start.8 = (f32[44,4,8,128]{3,2,1,0:T(8,128)S(1)}, f32[44,4,8,128]{3,2,1,0:T(8,128)S(1)}, u32[]{:S(2)}, u32[]{:S(2)}) collective-permute-start(f32[44,4,8,128]{3,2,1,0:T(8,128)S(1)} %get-tuple-element.55), channel_id=1, source_target_pairs={{0,24},{4,228},{8,16},{12,236},{16,8},{20,244},{24,0},{28,252},{32... | collective-permute-start | bytes 2162696 | tf_op jit(solution)/shard_map/ppermute | solution.py:302
  12.5 1.1 collective-permute-done.10.got_ref
  13.7 3.0 %collective-permute-start.11 = (f32[20,4,8,128]{3,2,1,0:T(8,128)S(1)}, f32[20,4,8,128]{3,2,1,0:T(8,128)S(1)}, u32[]{:S(2)}, u32[]{:S(2)}) collective-permute-start(f32[20,4,8,128]{3,2,1,0:T(8,128)S(1)} %get-tuple-element.61), channel_id=1, source_target_pairs={{0,24},{4,228},{8,16},{12,236},{16,8},{20,244},{24,0},{28,252},{32... | collective-permute-start | bytes 983048 | tf_op jit(solution)/shard_map/ppermute | solution.py:302
  16.9 3.6 %collective-permute-done.8.got = f32[44,4,8,128]{3,2,1,0:T(8,128)S(1)} collective-permute-done((f32[44,4,8,128]{3,2,1,0:T(8,128)S(1)}, f32[44,4,8,128]{3,2,1,0:T(8,128)S(1)}, u32[]{:S(2)}, u32[]{:S(2)}) %collective-permute-start.8) | collective-permute-done | bytes 720928 | tf_op jit(solution)/shard_map/ppermute | solution.py:302
  20.7 2.6 %collective-permute-start.9 = (f32[44,2,8,128]{3,2,1,0:T(8,128)S(1)}, f32[44,2,8,128]{3,2,1,0:T(8,128)S(1)}, u32[]{:S(2)}, u32[]{:S(2)}) collective-permute-start(f32[44,2,8,128]{3,2,1,0:T(8,128)S(1)} %get-tuple-element.57), channel_id=1, source_target_pairs={{0,224},{4,28},{8,232},{12,20},{16,240},{20,12},{24,248},{28,4},{3... | collective-permute-start | bytes 1081352 | tf_op jit(solution)/shard_map/ppermute | solution.py:302
  23.9 2.5 %collective-permute-start.12 = (f32[20,2,8,128]{3,2,1,0:T(8,128)S(1)}, f32[20,2,8,128]{3,2,1,0:T(8,128)S(1)}, u32[]{:S(2)}, u32[]{:S(2)}) collective-permute-start(f32[20,2,8,128]{3,2,1,0:T(8,128)S(1)} %get-tuple-element.63), channel_id=1, source_target_pairs={{0,224},{4,28},{8,232},{12,20},{16,240},{20,12},{24,248},{28,4},{3... | collective-permute-start | bytes 491528 | tf_op jit(solution)/shard_map/ppermute | solution.py:302
  27.2 3.1 %collective-permute-done.12.refs_3_ = f32[20,2,8,128]{3,2,1,0:T(8,128)S(1)} collective-permute-done((f32[20,2,8,128]{3,2,1,0:T(8,128)S(1)}, f32[20,2,8,128]{3,2,1,0:T(8,128)S(1)}, u32[]{:S(2)}, u32[]{:S(2)}) %collective-permute-start.12) | collective-permute-done | bytes 163872 | tf_op jit(solution)/shard_map/ppermute | solution.py:302
  30.6 1.3 %collective-permute-done.5.refs_3_ = f32[20,2,8,128]{3,2,1,0:T(8,128)S(1)} collective-permute-done((f32[20,2,8,128]{3,2,1,0:T(8,128)S(1)}, f32[20,2,8,128]{3,2,1,0:T(8,128)S(1)}, u32[]{:S(2)}, u32[]{:S(2)}) %collective-permute-start.5) | collective-permute-done | bytes 163872 | tf_op jit(solution)/shard_map/ppermute | solution.py:302
  32.0 1.6 %collective-permute-start.6 = (f32[64,8,128]{2,1,0:T(8,128)S(1)}, f32[64,8,128]{2,1,0:T(8,128)S(1)}, u32[]{:S(2)}, u32[]{:S(2)}) collective-permute-start(f32[64,8,128]{2,1,0:T(8,128)S(1)} %get-tuple-element.51), channel_id=1, source_target_pairs={{0,24},{4,28},{8,16},{12,20},{16,8},{20,12},{24,0},{28,4},{32,56},... | collective-permute-start | bytes 786440 | tf_op jit(solution)/shard_map/ppermute | solution.py:308
  33.7 2.8 %collective-permute-done.13.got_b_ref = f32[64,8,128]{2,1,0:T(8,128)S(1)} collective-permute-done((f32[64,8,128]{2,1,0:T(8,128)S(1)}, f32[64,8,128]{2,1,0:T(8,128)S(1)}, u32[]{:S(2)}, u32[]{:S(2)}) %collective-permute-start.13) | collective-permute-done | bytes 262176 | tf_op jit(solution)/shard_map/ppermute | solution.py:308
  36.6 2.0 %collective-permute-done.6.got_a_ref = f32[64,8,128]{2,1,0:T(8,128)S(1)} collective-permute-done((f32[64,8,128]{2,1,0:T(8,128)S(1)}, f32[64,8,128]{2,1,0:T(8,128)S(1)}, u32[]{:S(2)}, u32[]{:S(2)}) %collective-permute-start.6) | collective-permute-done | bytes 262176 | tf_op jit(solution)/shard_map/ppermute | solution.py:308
  38.5 1.5 %pack.1 = f32[192,8,128]{2,1,0:T(8,128)} custom-call(s32[128]{0:T(128)S(1)} %get-tuple-element.83.place_ref, f32[64,8,128]{2,1,0:T(8,128)S(1)} %get-tuple-element.50.a_ref, f32[64,8,128]{2,1,0:T(8,128)S(1)} %collective-permute-done.6.got_a_ref, f32[64,8,128]{2,1,0:T(8,128)S(1)} %get-tuple-element.64.b_ref, f32[64,8,128]{2,1,0:T(8,128)S(1)} %collective-permute-done.13.got_b_ref), custom_call_target="tpu_custom_call" | custom-call | bytes 1024 | tf_op jit(solution)/shard_map/pack/pallas_call | solution.py:311
  40.1 10.8 %all-to-all-start = ((f32[192,8,128]{2,1,0:T(8,128)}), f32[192,8,128]{2,1,0:T(8,128)S(1)}, u32[]{:S(2)}, u32[]{:S(2)}) async-start(f32[192,8,128]{2,1,0:T(8,128)} %pack.1), calls=%async_computation | async-start | bytes 1572864 | tf_op jit(solution)/shard_map/all_to_all | solution.py:312
  50.9 22.7 %all-to-all-done.got_ref = f32[192,8,128]{2,1,0:T(8,128)S(1)} async-done(((f32[192,8,128]{2,1,0:T(8,128)}), f32[192,8,128]{2,1,0:T(8,128)S(1)}, u32[]{:S(2)}, u32[]{:S(2)}) %all-to-all-start) | async-done | bytes 786464 | tf_op jit(solution)/shard_map/all_to_all | solution.py:312
  74.6 1.3 %collective-permute-start.14 = (f32[64,256]{1,0:T(8,128)S(1)}, f32[64,256]{1,0:T(8,128)S(1)}, u32[]{:S(2)}, u32[]{:S(2)}) collective-permute-start(f32[64,256]{1,0:T(8,128)S(1)} %get-tuple-element.68), channel_id=1, source_target_pairs={{0,1},{1,2},{2,3},{3,0},{4,5},{5,6},{6,7},{7,4},{8,9},{9,10},{10,1... | collective-permute-start | bytes 196616 | tf_op jit(solution)/shard_map/ppermute | solution.py:288
  75.9 2.6 %collective-permute-start.15 = (f32[64,256]{1,0:T(8,128)S(1)}, f32[64,256]{1,0:T(8,128)S(1)}, u32[]{:S(2)}, u32[]{:S(2)}) collective-permute-start(f32[64,256]{1,0:T(8,128)S(1)} %get-tuple-element.69), channel_id=1, source_target_pairs={{0,2},{1,3},{2,0},{3,1},{4,6},{5,7},{6,4},{7,5},{8,10},{9,11},{10,... | collective-permute-start | bytes 196616 | tf_op jit(solution)/shard_map/ppermute | solution.py:288
  79.6 1.4 %collective-permute-done.15.got2_ref = f32[64,256]{1,0:T(8,128)S(1)} collective-permute-done((f32[64,256]{1,0:T(8,128)S(1)}, f32[64,256]{1,0:T(8,128)S(1)}, u32[]{:S(2)}, u32[]{:S(2)}) %collective-permute-start.15) | collective-permute-done | bytes 65568 | tf_op jit(solution)/shard_map/ppermute | solution.py:288
  81.0 1.2 %collective-permute-done.16.got3_ref = f32[64,256]{1,0:T(8,128)S(1)} collective-permute-done((f32[64,256]{1,0:T(8,128)S(1)}, f32[64,256]{1,0:T(8,128)S(1)}, u32[]{:S(2)}, u32[]{:S(2)}) %collective-permute-start.16) | collective-permute-done | bytes 65568 | tf_op jit(solution)/shard_map/ppermute | solution.py:288
  82.3 4.8 %work.1 = f32[512,128]{1,0:T(8,128)S(1)} custom-call(f32[64,256]{1,0:T(8,128)S(1)} %get-tuple-element.67.own_ref, f32[64,256]{1,0:T(8,128)S(1)} %collective-permute-done.14.got1_ref, f32[64,256]{1,0:T(8,128)S(1)} %collective-permute-done.15.got2_ref, f32[64,256]{1,0:T(8,128)S(1)} %collective-permute-done.16.got3_ref), custom_call_target="tpu_custom_call" | custom-call | flops 1509949440 | bytes 1024 | tf_op jit(solution)/shard_map/work/pallas_call | solution.py:315
  87.0 24.7 %all_to_all.10 = f32[256,1,256]{2,1,0:T(1,128)S(1)} all-to-all(f32[256,1,256]{2,1,0:T(1,128)S(1)} %bitcast.16), channel_id=1, replica_groups=mesh['z'=8,'x'=4,'core'=2,'y'=4] {'y','z','x','core'}, dimensions={0} | all-to-all | bytes 524288 | tf_op jit(solution)/shard_map/all_to_all | solution.py:316
  111.8 1.4 %finish.1 = (f32[256,128]{1,0:T(8,128)}, f32[256,128]{1,0:T(8,128)}) custom-call(s32[128]{0:T(128)S(1)} %get-tuple-element.82.target_ref, f32[512,128]{1,0:T(8,128)S(1)} %bitcast.15, f32[256,128]{1,0:T(8,128)S(1)} %bitcast.18), custom_call_target="tpu_custom_call" | custom-call | bytes 1024 | tf_op jit(solution)/shard_map/finish/pallas_call | solution.py:317
  (38 shorter events, 5.8 us)
Async XLA Ops:
  2.2 5.1 %collective-permute-start.7 = (bf16[2,32,5632]{2,1,0:T(8,128)(2,1)S(1)}, bf16[2,32,5632]{2,1,0:T(8,128)(2,1)S(1)}, u32[]{:S(2)}, u32[]{:S(2)}) collective-permute-start(bf16[2,32,5632]{2,1,0:T(8,128)(2,1)S(1)} %get-tuple-element.53), channel_id=1, source_target_pairs={{0,4},{4,0},{1,5},{5,1},{2,6},{6,2},{3,7},{7,3},{8,12},{12,8},{9,1... | collective-permute-start | bytes 2162696 | tf_op jit(solution)/shard_map/ppermute | solution.py:297
  5.5 6.0 %collective-permute-start = (bf16[2,32,5632]{2,1,0:T(8,128)(2,1)S(1)}, bf16[2,32,5632]{2,1,0:T(8,128)(2,1)S(1)}, u32[]{:S(2)}, u32[]{:S(2)}) collective-permute-start(bf16[2,32,5632]{2,1,0:T(8,128)(2,1)S(1)} %get-tuple-element.39), channel_id=1, source_target_pairs={{0,4},{4,0},{1,5},{5,1},{2,6},{6,2},{3,7},{7,3},{8,12},{12,8},{9,1... | collective-permute-start | bytes 2162696 | tf_op jit(solution)/shard_map/ppermute | solution.py:297
  7.6 12.9 %collective-permute-start.8 = (f32[44,4,8,128]{3,2,1,0:T(8,128)S(1)}, f32[44,4,8,128]{3,2,1,0:T(8,128)S(1)}, u32[]{:S(2)}, u32[]{:S(2)}) collective-permute-start(f32[44,4,8,128]{3,2,1,0:T(8,128)S(1)} %get-tuple-element.55), channel_id=1, source_target_pairs={{0,24},{4,228},{8,16},{12,236},{16,8},{20,244},{24,0},{28,252},{32... | collective-permute-start | bytes 2162696 | tf_op jit(solution)/shard_map/ppermute | solution.py:302
  11.5 22.1 %copy-start.2 = (s32[128,1]{0,1:T(1,128)S(1)}, s32[128,1]{0,1:T(1,128)}, u32[]{:S(2)}) copy-start(s32[128,1]{0,1:T(1,128)} %param.7) | copy-start | bytes 1540
  11.8 11.5 %collective-permute-start.1 = (f32[44,4,8,128]{3,2,1,0:T(8,128)S(1)}, f32[44,4,8,128]{3,2,1,0:T(8,128)S(1)}, u32[]{:S(2)}, u32[]{:S(2)}) collective-permute-start(f32[44,4,8,128]{3,2,1,0:T(8,128)S(1)} %get-tuple-element.41), channel_id=1, source_target_pairs={{0,8},{4,36},{8,0},{12,44},{16,24},{20,52},{24,16},{28,60},{32,40}... | collective-permute-start | bytes 2162696 | tf_op jit(solution)/shard_map/ppermute | solution.py:302
  11.9 1.7 %collective-permute-start.10 = (bf16[2,32,2560]{2,1,0:T(8,128)(2,1)S(1)}, bf16[2,32,2560]{2,1,0:T(8,128)(2,1)S(1)}, u32[]{:S(2)}, u32[]{:S(2)}) collective-permute-start(bf16[2,32,2560]{2,1,0:T(8,128)(2,1)S(1)} %get-tuple-element.59), channel_id=1, source_target_pairs={{0,4},{4,0},{1,5},{5,1},{2,6},{6,2},{3,7},{7,3},{8,12},{12,8},{9,1... | collective-permute-start | bytes 983048 | tf_op jit(solution)/shard_map/ppermute | solution.py:297
  12.0 4.7 %collective-permute-start.3 = (bf16[2,32,2560]{2,1,0:T(8,128)(2,1)S(1)}, bf16[2,32,2560]{2,1,0:T(8,128)(2,1)S(1)}, u32[]{:S(2)}, u32[]{:S(2)}) collective-permute-start(bf16[2,32,2560]{2,1,0:T(8,128)(2,1)S(1)} %get-tuple-element.45), channel_id=1, source_target_pairs={{0,4},{4,0},{1,5},{5,1},{2,6},{6,2},{3,7},{7,3},{8,12},{12,8},{9,1... | collective-permute-start | bytes 983048 | tf_op jit(solution)/shard_map/ppermute | solution.py:297
  13.7 10.1 %collective-permute-start.11 = (f32[20,4,8,128]{3,2,1,0:T(8,128)S(1)}, f32[20,4,8,128]{3,2,1,0:T(8,128)S(1)}, u32[]{:S(2)}, u32[]{:S(2)}) collective-permute-start(f32[20,4,8,128]{3,2,1,0:T(8,128)S(1)} %get-tuple-element.61), channel_id=1, source_target_pairs={{0,24},{4,228},{8,16},{12,236},{16,8},{20,244},{24,0},{28,252},{32... | collective-permute-start | bytes 983048 | tf_op jit(solution)/shard_map/ppermute | solution.py:302
  16.8 9.5 %collective-permute-start.4 = (f32[20,4,8,128]{3,2,1,0:T(8,128)S(1)}, f32[20,4,8,128]{3,2,1,0:T(8,128)S(1)}, u32[]{:S(2)}, u32[]{:S(2)}) collective-permute-start(f32[20,4,8,128]{3,2,1,0:T(8,128)S(1)} %get-tuple-element.47), channel_id=1, source_target_pairs={{0,8},{4,36},{8,0},{12,44},{16,24},{20,52},{24,16},{28,60},{32,40}... | collective-permute-start | bytes 983048 | tf_op jit(solution)/shard_map/ppermute | solution.py:302
  20.7 53.0 %copy-start = (f32[1,3,64,256]{3,2,1,0:T(8,128)S(1)}, f32[1,3,64,256]{3,2,1,0:T(8,128)}, u32[]{:S(2)}) copy-start(f32[1,3,64,256]{3,2,1,0:T(8,128)} %param.5) | copy-start | bytes 589828
  20.7 9.6 %collective-permute-start.9 = (f32[44,2,8,128]{3,2,1,0:T(8,128)S(1)}, f32[44,2,8,128]{3,2,1,0:T(8,128)S(1)}, u32[]{:S(2)}, u32[]{:S(2)}) collective-permute-start(f32[44,2,8,128]{3,2,1,0:T(8,128)S(1)} %get-tuple-element.57), channel_id=1, source_target_pairs={{0,224},{4,28},{8,232},{12,20},{16,240},{20,12},{24,248},{28,4},{3... | collective-permute-start | bytes 1081352 | tf_op jit(solution)/shard_map/ppermute | solution.py:302
  23.5 8.4 %collective-permute-start.2 = (f32[44,2,8,128]{3,2,1,0:T(8,128)S(1)}, f32[44,2,8,128]{3,2,1,0:T(8,128)S(1)}, u32[]{:S(2)}, u32[]{:S(2)}) collective-permute-start(f32[44,2,8,128]{3,2,1,0:T(8,128)S(1)} %get-tuple-element.43), channel_id=1, source_target_pairs={{0,32},{4,12},{8,40},{12,4},{16,48},{20,28},{24,56},{28,20},{32,0}... | collective-permute-start | bytes 1081352 | tf_op jit(solution)/shard_map/ppermute | solution.py:302
  23.9 6.4 %collective-permute-start.12 = (f32[20,2,8,128]{3,2,1,0:T(8,128)S(1)}, f32[20,2,8,128]{3,2,1,0:T(8,128)S(1)}, u32[]{:S(2)}, u32[]{:S(2)}) collective-permute-start(f32[20,2,8,128]{3,2,1,0:T(8,128)S(1)} %get-tuple-element.63), channel_id=1, source_target_pairs={{0,224},{4,28},{8,232},{12,20},{16,240},{20,12},{24,248},{28,4},{3... | collective-permute-start | bytes 491528 | tf_op jit(solution)/shard_map/ppermute | solution.py:302
  26.5 5.4 %collective-permute-start.5 = (f32[20,2,8,128]{3,2,1,0:T(8,128)S(1)}, f32[20,2,8,128]{3,2,1,0:T(8,128)S(1)}, u32[]{:S(2)}, u32[]{:S(2)}) collective-permute-start(f32[20,2,8,128]{3,2,1,0:T(8,128)S(1)} %get-tuple-element.49), channel_id=1, source_target_pairs={{0,32},{4,12},{8,40},{12,4},{16,48},{20,28},{24,56},{28,20},{32,0}... | collective-permute-start | bytes 491528 | tf_op jit(solution)/shard_map/ppermute | solution.py:302
  30.5 6.1 %collective-permute-start.13 = (f32[64,8,128]{2,1,0:T(8,128)S(1)}, f32[64,8,128]{2,1,0:T(8,128)S(1)}, u32[]{:S(2)}, u32[]{:S(2)}) collective-permute-start(f32[64,8,128]{2,1,0:T(8,128)S(1)} %get-tuple-element.65), channel_id=1, source_target_pairs={{0,8},{4,12},{8,0},{12,4},{16,24},{20,28},{24,16},{28,20},{32,40},... | collective-permute-start | bytes 786440 | tf_op jit(solution)/shard_map/ppermute | solution.py:308
  32.0 6.5 %collective-permute-start.6 = (f32[64,8,128]{2,1,0:T(8,128)S(1)}, f32[64,8,128]{2,1,0:T(8,128)S(1)}, u32[]{:S(2)}, u32[]{:S(2)}) collective-permute-start(f32[64,8,128]{2,1,0:T(8,128)S(1)} %get-tuple-element.51), channel_id=1, source_target_pairs={{0,24},{4,28},{8,16},{12,20},{16,8},{20,12},{24,0},{28,4},{32,56},... | collective-permute-start | bytes 786440 | tf_op jit(solution)/shard_map/ppermute | solution.py:308
  40.1 71.7 %copy-start.1 = (f32[2,1,16384]{2,1,0:T(1,128)S(1)}, f32[2,1,16384]{2,1,0:T(1,128)}, u32[]{:S(2)}) copy-start(f32[2,1,16384]{2,1,0:T(1,128)} %param.6) | copy-start | bytes 393220
  40.1 33.6 %all-to-all-start = ((f32[192,8,128]{2,1,0:T(8,128)}), f32[192,8,128]{2,1,0:T(8,128)S(1)}, u32[]{:S(2)}, u32[]{:S(2)}) async-start(f32[192,8,128]{2,1,0:T(8,128)} %pack.1), calls=%async_computation | async-start | bytes 1572864 | tf_op jit(solution)/shard_map/all_to_all | solution.py:312
  74.6 5.0 %collective-permute-start.14 = (f32[64,256]{1,0:T(8,128)S(1)}, f32[64,256]{1,0:T(8,128)S(1)}, u32[]{:S(2)}, u32[]{:S(2)}) collective-permute-start(f32[64,256]{1,0:T(8,128)S(1)} %get-tuple-element.68), channel_id=1, source_target_pairs={{0,1},{1,2},{2,3},{3,0},{4,5},{5,6},{6,7},{7,4},{8,9},{9,10},{10,1... | collective-permute-start | bytes 196616 | tf_op jit(solution)/shard_map/ppermute | solution.py:288
  75.9 5.1 %collective-permute-start.15 = (f32[64,256]{1,0:T(8,128)S(1)}, f32[64,256]{1,0:T(8,128)S(1)}, u32[]{:S(2)}, u32[]{:S(2)}) collective-permute-start(f32[64,256]{1,0:T(8,128)S(1)} %get-tuple-element.69), channel_id=1, source_target_pairs={{0,2},{1,3},{2,0},{3,1},{4,6},{5,7},{6,4},{7,5},{8,10},{9,11},{10,... | collective-permute-start | bytes 196616 | tf_op jit(solution)/shard_map/ppermute | solution.py:288
  78.6 3.7 %collective-permute-start.16 = (f32[64,256]{1,0:T(8,128)S(1)}, f32[64,256]{1,0:T(8,128)S(1)}, u32[]{:S(2)}, u32[]{:S(2)}) collective-permute-start(f32[64,256]{1,0:T(8,128)S(1)} %get-tuple-element.70), channel_id=1, source_target_pairs={{0,3},{1,0},{2,1},{3,2},{4,7},{5,4},{6,5},{7,6},{8,11},{9,8},{10,9... | collective-permute-start | bytes 196616 | tf_op jit(solution)/shard_map/ppermute | solution.py:288

commit v7 on v6

--- a/solution.py
+++ b/solution.py
@@ -67,15 +67,15 @@
     return jnp.where(lax.axis_index("core") == 0, three, two if kind else one)
 
 
-def rows_kernel(mine, grad_ref, *refs):
+def rows_kernel(mine, groups, grad_ref, *refs):
     *outs, sems = refs
     core = lax.axis_index("core")
     rows = rows_of(core if mine else 1 - core, 32)
     copies = []
-    for group, out in enumerate(outs):
+    for turn, (group, out) in enumerate(zip(groups, outs)):
         lanes = slice(FIRST[group] * COLS, (FIRST[group] + SIZES[group]) * COLS)
         for layer in range(L):
-            copies.append(pltpu.make_async_copy(grad_ref.at[layer, rows, lanes], out.at[layer], sems.at[group, layer]))
+            copies.append(pltpu.make_async_copy(grad_ref.at[layer, rows, lanes], out.at[layer], sems.at[turn, layer]))
     for copy in copies:
         copy.start()
     for copy in copies:
@@ -238,13 +238,13 @@
     )
 
 
-def rows_of_heads(gradient, mine):
+def rows_of_heads(gradient, mine, groups):
     return pl.pallas_call(
-        functools.partial(rows_kernel, mine),
-        out_shape=tuple(shape(L, 32, size * COLS, dtype=bf16) for size in SIZES),
+        functools.partial(rows_kernel, mine, groups),
+        out_shape=tuple(shape(L, 32, SIZES[group] * COLS, dtype=bf16) for group in groups),
         in_specs=[pl.BlockSpec(memory_space=pltpu.HBM)],
-        out_specs=tuple(pl.BlockSpec(memory_space=pltpu.VMEM) for _ in SIZES),
-        scratch_shapes=[pltpu.SemaphoreType.DMA((len(SIZES), L))],
+        out_specs=tuple(pl.BlockSpec(memory_space=pltpu.VMEM) for _ in groups),
+        scratch_shapes=[pltpu.SemaphoreType.DMA((len(groups), L))],
         compiler_params=params(),
         cost_estimate=pl.CostEstimate(flops=0, bytes_accessed=1 << 10, transcendentals=0),
         name="own" if mine else "cross",
@@ -284,9 +284,10 @@
 
 
 def along_y(values):
-    return [
-        lax.ppermute(value, "y", [(i, (i + step) % 4) for i in range(4)]) for step, value in enumerate(values, start=1)
-    ]
+    one, two, three = values
+    two = lax.ppermute(two, "y", [(i, (i + 2) % 4) for i in range(4)])
+    one, three = (lax.ppermute(value, "y", [(i, (i + step) % 4) for i in range(4)]) for step, value in ((1, one), (3, three)))
+    return one, two, three
 
 
 def on_device(gradient, momentum, weights, table):
@@ -294,8 +295,9 @@
     local = gradient[0]
 
     dp = ("z", "x", "core")
-    crossed = [lax.ppermute(rows, "core", [(0, 1), (1, 0)]) for rows in rows_of_heads(local, False)]
-    parts = list(zip(rows_of_heads(local, True), crossed))
+    crossed = sum((rows_of_heads(local, False, groups) for groups in ((0, 1), (2, 3))), ())
+    crossed = [lax.ppermute(rows, "core", [(0, 1), (1, 0)]) for rows in crossed]
+    parts = list(zip(sum((rows_of_heads(local, True, groups) for groups in ((0, 1), (2, 3))), ()), crossed))
     for step, (kernel, dims) in enumerate(((first_kernel, (4, 8, 128)), (second_kernel, (2, 8, 128)))):
         for group, (kind, size) in enumerate(zip(KINDS, SIZES)):
             send, keep = call(functools.partial(kernel, kind, size), (shape(L * size, *dims),) * 2, "vv")(*parts[group])

time: 113 us -> 113 us (level)
  waiting for transfers between devices: 39.4 us -> 37.2 us
  Pallas kernels: 13.3 us -> 15.2 us
    ppermute x3 -> x2, starting transfers between devices: 4.99 us -> 2.37 us  [along_y(): lax.ppermute(value, 'y', [(i, (i + step) % 4) for i in range(4)])]
    ppermute x4 -> x5, starting transfers between devices: 4.02 us -> 6.64 us  [the longest x4 4.02 us: on_device(): crossed = [lax.ppermute(rows, 'core', [(0, 1), (1, 0)]) for rows in crossed]]
    pallas_call x2 -> x4, Pallas kernels: 3.14 us -> 5.08 us  [rows_of_heads(): pl.pallas_call(functools.partial(rows_kernel, mine, groups), out_shape=tu...]
    ppermute x3 -> x2, waiting for transfers between devices: 2.63 us -> 1.24 us  [along_y(): lax.ppermute(value, 'y', [(i, (i + step) % 4) for i in range(4)])]
    ppermute x8, waiting for transfers between devices: 8 us -> 6.64 us  [on_device(): parts[group] = (keep, lax.ppermute(send, dp, ROUTES[kind][step]))]
  transfers between devices with their start and end apart: 18 -> 18, of which waited for: 10 -> 9; matrix products, arithmetic and copies ran while one was open for 0% -> 0% of each run, Pallas kernels for 3% -> 5%
where the time goes in v7:
time: 113 us
  waiting for transfers between devices  37.2 us (33%)
  starting transfers between devices  34.8 us (31%)
  blocking collectives  24.7 us (22%)
  Pallas kernels  15.2 us (13%)
    all_to_all x1, blocking collectives, on_device(): lax.all_to_all(ortho.reshape(DEVICES, 1, COLS), ALL, 0, 0, tiled=True)  24.7 us
    all_to_all x1, waiting for transfers between devices, on_device(): got = lax.all_to_all(outgoing, dp, 0, 0, tiled=True)  22.7 us
    ppermute x8, starting transfers between devices, on_device(): parts[group] = (keep, lax.ppermute(send, dp, ROUTES[kind][step]))  13.3 us
    all_to_all x1, starting transfers between devices, on_device(): got = lax.all_to_all(outgoing, dp, 0, 0, tiled=True)  10.8 us
    ppermute x8, waiting for transfers between devices, on_device(): parts[group] = (keep, lax.ppermute(send, dp, ROUTES[kind][step]))  6.64 us
    pallas_call x4, Pallas kernels, rows_of_heads(): pl.pallas_call(functools.partial(rows_kernel, mine, groups), out_shape=tu...  5.08 us
    ppermute x2, waiting for transfers between devices, on_device(): last += (keep, lax.ppermute(send, dp, ROUTES[kind][2]))  4.8 us
    pallas_call x1, Pallas kernels, on_device(): call(work_kernel, shape(2 * RANK, 128), 'vvvv', [(RANK, COLS)], 15 * 3 *...  4.78 us
  transfers between devices with their start and end apart: 18, of which 9 were waited for; matrix products, arithmetic and copies ran while one was open for 0% of the time, Pallas kernels for 5%

profile of v7, /device:TPU:1, one launch (start us, length us, event | category | flops | bytes accessed | tf_op | source)
XLA Modules:
  0.0 112.9 jit_solution(13462803069102239311)
XLA Ops:
  0.6 1.4 %cross.2 = (bf16[2,32,5632]{2,1,0:T(8,128)(2,1)S(1)}, bf16[2,32,5632]{2,1,0:T(8,128)(2,1)S(1)}) custom-call(bf16[2,64,16384]{2,1,0:T(8,128)(2,1)} %bitcast.19), custom_call_target="tpu_custom_call" | custom-call | bytes 1024 | tf_op jit(solution)/shard_map/cross/pallas_call | solution.py:242
  2.0 3.3 %collective-permute-start.7 = (bf16[2,32,5632]{2,1,0:T(8,128)(2,1)S(1)}, bf16[2,32,5632]{2,1,0:T(8,128)(2,1)S(1)}, u32[]{:S(2)}, u32[]{:S(2)}) collective-permute-start(bf16[2,32,5632]{2,1,0:T(8,128)(2,1)S(1)} %get-tuple-element.53), channel_id=1, source_target_pairs={{0,4},{4,0},{1,5},{5,1},{2,6},{6,2},{3,7},{7,3},{8,12},{12,8},{9,1... | collective-permute-start | bytes 2162696 | tf_op jit(solution)/shard_map/ppermute | solution.py:299
  5.4 1.3 %own.2 = (bf16[2,32,5632]{2,1,0:T(8,128)(2,1)S(1)}, bf16[2,32,5632]{2,1,0:T(8,128)(2,1)S(1)}) custom-call(bf16[2,64,16384]{2,1,0:T(8,128)(2,1)} %bitcast.20), custom_call_target="tpu_custom_call" | custom-call | bytes 1024 | tf_op jit(solution)/shard_map/own/pallas_call | solution.py:242
  7.4 3.9 %collective-permute-start.8 = (f32[44,4,8,128]{3,2,1,0:T(8,128)S(1)}, f32[44,4,8,128]{3,2,1,0:T(8,128)S(1)}, u32[]{:S(2)}, u32[]{:S(2)}) collective-permute-start(f32[44,4,8,128]{3,2,1,0:T(8,128)S(1)} %get-tuple-element.55), channel_id=1, source_target_pairs={{0,24},{4,228},{8,16},{12,236},{16,8},{20,244},{24,0},{28,252},{32... | collective-permute-start | bytes 2162696 | tf_op jit(solution)/shard_map/ppermute | solution.py:304
  11.7 1.2 %cross.3 = (bf16[2,32,2560]{2,1,0:T(8,128)(2,1)S(1)}, bf16[2,32,2560]{2,1,0:T(8,128)(2,1)S(1)}) custom-call(bf16[2,64,16384]{2,1,0:T(8,128)(2,1)} %bitcast.21), custom_call_target="tpu_custom_call" | custom-call | bytes 1024 | tf_op jit(solution)/shard_map/cross/pallas_call | solution.py:242
  14.8 3.0 %collective-permute-start.11 = (f32[20,4,8,128]{3,2,1,0:T(8,128)S(1)}, f32[20,4,8,128]{3,2,1,0:T(8,128)S(1)}, u32[]{:S(2)}, u32[]{:S(2)}) collective-permute-start(f32[20,4,8,128]{3,2,1,0:T(8,128)S(1)} %get-tuple-element.61), channel_id=1, source_target_pairs={{0,24},{4,228},{8,16},{12,236},{16,8},{20,244},{24,0},{28,252},{32... | collective-permute-start | bytes 983048 | tf_op jit(solution)/shard_map/ppermute | solution.py:304
  18.1 2.2 %collective-permute-done.8.got = f32[44,4,8,128]{3,2,1,0:T(8,128)S(1)} collective-permute-done((f32[44,4,8,128]{3,2,1,0:T(8,128)S(1)}, f32[44,4,8,128]{3,2,1,0:T(8,128)S(1)}, u32[]{:S(2)}, u32[]{:S(2)}) %collective-permute-start.8) | collective-permute-done | bytes 720928 | tf_op jit(solution)/shard_map/ppermute | solution.py:304
  20.5 2.6 %collective-permute-start.9 = (f32[44,2,8,128]{3,2,1,0:T(8,128)S(1)}, f32[44,2,8,128]{3,2,1,0:T(8,128)S(1)}, u32[]{:S(2)}, u32[]{:S(2)}) collective-permute-start(f32[44,2,8,128]{3,2,1,0:T(8,128)S(1)} %get-tuple-element.57), channel_id=1, source_target_pairs={{0,224},{4,28},{8,232},{12,20},{16,240},{20,12},{24,248},{28,4},{3... | collective-permute-start | bytes 1081352 | tf_op jit(solution)/shard_map/ppermute | solution.py:304
  23.7 2.5 %collective-permute-start.12 = (f32[20,2,8,128]{3,2,1,0:T(8,128)S(1)}, f32[20,2,8,128]{3,2,1,0:T(8,128)S(1)}, u32[]{:S(2)}, u32[]{:S(2)}) collective-permute-start(f32[20,2,8,128]{3,2,1,0:T(8,128)S(1)} %get-tuple-element.63), channel_id=1, source_target_pairs={{0,224},{4,28},{8,232},{12,20},{16,240},{20,12},{24,248},{28,4},{3... | collective-permute-start | bytes 491528 | tf_op jit(solution)/shard_map/ppermute | solution.py:304
  27.0 3.1 %collective-permute-done.12.refs_3_ = f32[20,2,8,128]{3,2,1,0:T(8,128)S(1)} collective-permute-done((f32[20,2,8,128]{3,2,1,0:T(8,128)S(1)}, f32[20,2,8,128]{3,2,1,0:T(8,128)S(1)}, u32[]{:S(2)}, u32[]{:S(2)}) %collective-permute-start.12) | collective-permute-done | bytes 163872 | tf_op jit(solution)/shard_map/ppermute | solution.py:304
  30.4 1.3 %collective-permute-done.5.refs_3_ = f32[20,2,8,128]{3,2,1,0:T(8,128)S(1)} collective-permute-done((f32[20,2,8,128]{3,2,1,0:T(8,128)S(1)}, f32[20,2,8,128]{3,2,1,0:T(8,128)S(1)}, u32[]{:S(2)}, u32[]{:S(2)}) %collective-permute-start.5) | collective-permute-done | bytes 163872 | tf_op jit(solution)/shard_map/ppermute | solution.py:304
  31.8 1.6 %collective-permute-start.6 = (f32[64,8,128]{2,1,0:T(8,128)S(1)}, f32[64,8,128]{2,1,0:T(8,128)S(1)}, u32[]{:S(2)}, u32[]{:S(2)}) collective-permute-start(f32[64,8,128]{2,1,0:T(8,128)S(1)} %get-tuple-element.51), channel_id=1, source_target_pairs={{0,24},{4,28},{8,16},{12,20},{16,8},{20,12},{24,0},{28,4},{32,56},... | collective-permute-start | bytes 786440 | tf_op jit(solution)/shard_map/ppermute | solution.py:310
  33.5 2.8 %collective-permute-done.13.got_b_ref = f32[64,8,128]{2,1,0:T(8,128)S(1)} collective-permute-done((f32[64,8,128]{2,1,0:T(8,128)S(1)}, f32[64,8,128]{2,1,0:T(8,128)S(1)}, u32[]{:S(2)}, u32[]{:S(2)}) %collective-permute-start.13) | collective-permute-done | bytes 262176 | tf_op jit(solution)/shard_map/ppermute | solution.py:310
  36.3 2.0 %collective-permute-done.6.got_a_ref = f32[64,8,128]{2,1,0:T(8,128)S(1)} collective-permute-done((f32[64,8,128]{2,1,0:T(8,128)S(1)}, f32[64,8,128]{2,1,0:T(8,128)S(1)}, u32[]{:S(2)}, u32[]{:S(2)}) %collective-permute-start.6) | collective-permute-done | bytes 262176 | tf_op jit(solution)/shard_map/ppermute | solution.py:310
  38.3 1.5 %pack.1 = f32[192,8,128]{2,1,0:T(8,128)} custom-call(s32[128]{0:T(128)S(1)} %get-tuple-element.83.place_ref, f32[64,8,128]{2,1,0:T(8,128)S(1)} %get-tuple-element.50.a_ref, f32[64,8,128]{2,1,0:T(8,128)S(1)} %collective-permute-done.6.got_a_ref, f32[64,8,128]{2,1,0:T(8,128)S(1)} %get-tuple-element.64.b_ref, f32[64,8,128]{2,1,0:T(8,128)S(1)} %collective-permute-done.13.got_b_ref), custom_call_target="tpu_custom_call" | custom-call | bytes 1024 | tf_op jit(solution)/shard_map/pack/pallas_call | solution.py:313
  39.8 10.8 %all-to-all-start = ((f32[192,8,128]{2,1,0:T(8,128)}), f32[192,8,128]{2,1,0:T(8,128)S(1)}, u32[]{:S(2)}, u32[]{:S(2)}) async-start(f32[192,8,128]{2,1,0:T(8,128)} %pack.1), calls=%async_computation | async-start | bytes 1572864 | tf_op jit(solution)/shard_map/all_to_all | solution.py:314
  50.7 22.7 %all-to-all-done.got_ref = f32[192,8,128]{2,1,0:T(8,128)S(1)} async-done(((f32[192,8,128]{2,1,0:T(8,128)}), f32[192,8,128]{2,1,0:T(8,128)S(1)}, u32[]{:S(2)}, u32[]{:S(2)}) %all-to-all-start) | async-done | bytes 786464 | tf_op jit(solution)/shard_map/all_to_all | solution.py:314
  74.4 1.3 %collective-permute-start.14 = (f32[64,256]{1,0:T(8,128)S(1)}, f32[64,256]{1,0:T(8,128)S(1)}, u32[]{:S(2)}, u32[]{:S(2)}) collective-permute-start(f32[64,256]{1,0:T(8,128)S(1)} %get-tuple-element.68), channel_id=1, source_target_pairs={{0,1},{1,2},{2,3},{3,0},{4,5},{5,6},{6,7},{7,4},{8,9},{9,10},{10,1... | collective-permute-start | bytes 196616 | tf_op jit(solution)/shard_map/ppermute | solution.py:289
  75.7 2.6 %collective-permute-start.15 = (f32[64,256]{1,0:T(8,128)S(1)}, f32[64,256]{1,0:T(8,128)S(1)}, u32[]{:S(2)}, u32[]{:S(2)}) collective-permute-start(f32[64,256]{1,0:T(8,128)S(1)} %get-tuple-element.69), channel_id=1, source_target_pairs={{0,2},{1,3},{2,0},{3,1},{4,6},{5,7},{6,4},{7,5},{8,10},{9,11},{10,... | collective-permute-start | bytes 196616 | tf_op jit(solution)/shard_map/ppermute | solution.py:288
  79.4 1.4 %collective-permute-done.15.got2_ref = f32[64,256]{1,0:T(8,128)S(1)} collective-permute-done((f32[64,256]{1,0:T(8,128)S(1)}, f32[64,256]{1,0:T(8,128)S(1)}, u32[]{:S(2)}, u32[]{:S(2)}) %collective-permute-start.15) | collective-permute-done | bytes 65568 | tf_op jit(solution)/shard_map/ppermute | solution.py:288
  80.8 1.2 %collective-permute-done.16.got3_ref = f32[64,256]{1,0:T(8,128)S(1)} collective-permute-done((f32[64,256]{1,0:T(8,128)S(1)}, f32[64,256]{1,0:T(8,128)S(1)}, u32[]{:S(2)}, u32[]{:S(2)}) %collective-permute-start.16) | collective-permute-done | bytes 65568 | tf_op jit(solution)/shard_map/ppermute | solution.py:289
  82.0 4.8 %work.1 = f32[512,128]{1,0:T(8,128)S(1)} custom-call(f32[64,256]{1,0:T(8,128)S(1)} %get-tuple-element.67.own_ref, f32[64,256]{1,0:T(8,128)S(1)} %collective-permute-done.14.got1_ref, f32[64,256]{1,0:T(8,128)S(1)} %collective-permute-done.15.got2_ref, f32[64,256]{1,0:T(8,128)S(1)} %collective-permute-done.16.got3_ref), custom_call_target="tpu_custom_call" | custom-call | flops 1509949440 | bytes 1024 | tf_op jit(solution)/shard_map/work/pallas_call | solution.py:317
  86.8 24.7 %all_to_all.10 = f32[256,1,256]{2,1,0:T(1,128)S(1)} all-to-all(f32[256,1,256]{2,1,0:T(1,128)S(1)} %bitcast.16), channel_id=1, replica_groups=mesh['z'=8,'x'=4,'core'=2,'y'=4] {'y','z','x','core'}, dimensions={0} | all-to-all | bytes 524288 | tf_op jit(solution)/shard_map/all_to_all | solution.py:318
  111.5 1.4 %finish.1 = (f32[256,128]{1,0:T(8,128)}, f32[256,128]{1,0:T(8,128)}) custom-call(s32[128]{0:T(128)S(1)} %get-tuple-element.82.target_ref, f32[512,128]{1,0:T(8,128)S(1)} %bitcast.15, f32[256,128]{1,0:T(8,128)S(1)} %bitcast.18), custom_call_target="tpu_custom_call" | custom-call | bytes 1024 | tf_op jit(solution)/shard_map/finish/pallas_call | solution.py:319
  (40 shorter events, 7.3 us)
Async XLA Ops:
  2.0 5.1 %collective-permute-start.7 = (bf16[2,32,5632]{2,1,0:T(8,128)(2,1)S(1)}, bf16[2,32,5632]{2,1,0:T(8,128)(2,1)S(1)}, u32[]{:S(2)}, u32[]{:S(2)}) collective-permute-start(bf16[2,32,5632]{2,1,0:T(8,128)(2,1)S(1)} %get-tuple-element.53), channel_id=1, source_target_pairs={{0,4},{4,0},{1,5},{5,1},{2,6},{6,2},{3,7},{7,3},{8,12},{12,8},{9,1... | collective-permute-start | bytes 2162696 | tf_op jit(solution)/shard_map/ppermute | solution.py:299
  5.3 6.0 %collective-permute-start = (bf16[2,32,5632]{2,1,0:T(8,128)(2,1)S(1)}, bf16[2,32,5632]{2,1,0:T(8,128)(2,1)S(1)}, u32[]{:S(2)}, u32[]{:S(2)}) collective-permute-start(bf16[2,32,5632]{2,1,0:T(8,128)(2,1)S(1)} %get-tuple-element.39), channel_id=1, source_target_pairs={{0,4},{4,0},{1,5},{5,1},{2,6},{6,2},{3,7},{7,3},{8,12},{12,8},{9,1... | collective-permute-start | bytes 2162696 | tf_op jit(solution)/shard_map/ppermute | solution.py:299
  7.4 12.9 %collective-permute-start.8 = (f32[44,4,8,128]{3,2,1,0:T(8,128)S(1)}, f32[44,4,8,128]{3,2,1,0:T(8,128)S(1)}, u32[]{:S(2)}, u32[]{:S(2)}) collective-permute-start(f32[44,4,8,128]{3,2,1,0:T(8,128)S(1)} %get-tuple-element.55), channel_id=1, source_target_pairs={{0,24},{4,228},{8,16},{12,236},{16,8},{20,244},{24,0},{28,252},{32... | collective-permute-start | bytes 2162696 | tf_op jit(solution)/shard_map/ppermute | solution.py:304
  11.6 11.5 %collective-permute-start.1 = (f32[44,4,8,128]{3,2,1,0:T(8,128)S(1)}, f32[44,4,8,128]{3,2,1,0:T(8,128)S(1)}, u32[]{:S(2)}, u32[]{:S(2)}) collective-permute-start(f32[44,4,8,128]{3,2,1,0:T(8,128)S(1)} %get-tuple-element.41), channel_id=1, source_target_pairs={{0,8},{4,36},{8,0},{12,44},{16,24},{20,52},{24,16},{28,60},{32,40}... | collective-permute-start | bytes 2162696 | tf_op jit(solution)/shard_map/ppermute | solution.py:304
  12.9 1.8 %collective-permute-start.10 = (bf16[2,32,2560]{2,1,0:T(8,128)(2,1)S(1)}, bf16[2,32,2560]{2,1,0:T(8,128)(2,1)S(1)}, u32[]{:S(2)}, u32[]{:S(2)}) collective-permute-start(bf16[2,32,2560]{2,1,0:T(8,128)(2,1)S(1)} %get-tuple-element.59), channel_id=1, source_target_pairs={{0,4},{4,0},{1,5},{5,1},{2,6},{6,2},{3,7},{7,3},{8,12},{12,8},{9,1... | collective-permute-start | bytes 983048 | tf_op jit(solution)/shard_map/ppermute | solution.py:299
  13.0 4.9 %collective-permute-start.3 = (bf16[2,32,2560]{2,1,0:T(8,128)(2,1)S(1)}, bf16[2,32,2560]{2,1,0:T(8,128)(2,1)S(1)}, u32[]{:S(2)}, u32[]{:S(2)}) collective-permute-start(bf16[2,32,2560]{2,1,0:T(8,128)(2,1)S(1)} %get-tuple-element.45), channel_id=1, source_target_pairs={{0,4},{4,0},{1,5},{5,1},{2,6},{6,2},{3,7},{7,3},{8,12},{12,8},{9,1... | collective-permute-start | bytes 983048 | tf_op jit(solution)/shard_map/ppermute | solution.py:299
  14.7 18.7 %copy-start.2 = (s32[128,1]{0,1:T(1,128)S(1)}, s32[128,1]{0,1:T(1,128)}, u32[]{:S(2)}) copy-start(s32[128,1]{0,1:T(1,128)} %param.7) | copy-start | bytes 1540
  14.8 8.7 %collective-permute-start.11 = (f32[20,4,8,128]{3,2,1,0:T(8,128)S(1)}, f32[20,4,8,128]{3,2,1,0:T(8,128)S(1)}, u32[]{:S(2)}, u32[]{:S(2)}) collective-permute-start(f32[20,4,8,128]{3,2,1,0:T(8,128)S(1)} %get-tuple-element.61), channel_id=1, source_target_pairs={{0,24},{4,228},{8,16},{12,236},{16,8},{20,244},{24,0},{28,252},{32... | collective-permute-start | bytes 983048 | tf_op jit(solution)/shard_map/ppermute | solution.py:304
  18.0 8.2 %collective-permute-start.4 = (f32[20,4,8,128]{3,2,1,0:T(8,128)S(1)}, f32[20,4,8,128]{3,2,1,0:T(8,128)S(1)}, u32[]{:S(2)}, u32[]{:S(2)}) collective-permute-start(f32[20,4,8,128]{3,2,1,0:T(8,128)S(1)} %get-tuple-element.47), channel_id=1, source_target_pairs={{0,8},{4,36},{8,0},{12,44},{16,24},{20,52},{24,16},{28,60},{32,40}... | collective-permute-start | bytes 983048 | tf_op jit(solution)/shard_map/ppermute | solution.py:304
  20.5 53.0 %copy-start = (f32[1,3,64,256]{3,2,1,0:T(8,128)S(1)}, f32[1,3,64,256]{3,2,1,0:T(8,128)}, u32[]{:S(2)}) copy-start(f32[1,3,64,256]{3,2,1,0:T(8,128)} %param.5) | copy-start | bytes 589828
  20.5 9.6 %collective-permute-start.9 = (f32[44,2,8,128]{3,2,1,0:T(8,128)S(1)}, f32[44,2,8,128]{3,2,1,0:T(8,128)S(1)}, u32[]{:S(2)}, u32[]{:S(2)}) collective-permute-start(f32[44,2,8,128]{3,2,1,0:T(8,128)S(1)} %get-tuple-element.57), channel_id=1, source_target_pairs={{0,224},{4,28},{8,232},{12,20},{16,240},{20,12},{24,248},{28,4},{3... | collective-permute-start | bytes 1081352 | tf_op jit(solution)/shard_map/ppermute | solution.py:304
  23.2 8.4 %collective-permute-start.2 = (f32[44,2,8,128]{3,2,1,0:T(8,128)S(1)}, f32[44,2,8,128]{3,2,1,0:T(8,128)S(1)}, u32[]{:S(2)}, u32[]{:S(2)}) collective-permute-start(f32[44,2,8,128]{3,2,1,0:T(8,128)S(1)} %get-tuple-element.43), channel_id=1, source_target_pairs={{0,32},{4,12},{8,40},{12,4},{16,48},{20,28},{24,56},{28,20},{32,0}... | collective-permute-start | bytes 1081352 | tf_op jit(solution)/shard_map/ppermute | solution.py:304
  23.7 6.4 %collective-permute-start.12 = (f32[20,2,8,128]{3,2,1,0:T(8,128)S(1)}, f32[20,2,8,128]{3,2,1,0:T(8,128)S(1)}, u32[]{:S(2)}, u32[]{:S(2)}) collective-permute-start(f32[20,2,8,128]{3,2,1,0:T(8,128)S(1)} %get-tuple-element.63), channel_id=1, source_target_pairs={{0,224},{4,28},{8,232},{12,20},{16,240},{20,12},{24,248},{28,4},{3... | collective-permute-start | bytes 491528 | tf_op jit(solution)/shard_map/ppermute | solution.py:304
  26.2 5.4 %collective-permute-start.5 = (f32[20,2,8,128]{3,2,1,0:T(8,128)S(1)}, f32[20,2,8,128]{3,2,1,0:T(8,128)S(1)}, u32[]{:S(2)}, u32[]{:S(2)}) collective-permute-start(f32[20,2,8,128]{3,2,1,0:T(8,128)S(1)} %get-tuple-element.49), channel_id=1, source_target_pairs={{0,32},{4,12},{8,40},{12,4},{16,48},{20,28},{24,56},{28,20},{32,0}... | collective-permute-start | bytes 491528 | tf_op jit(solution)/shard_map/ppermute | solution.py:304
  30.3 6.1 %collective-permute-start.13 = (f32[64,8,128]{2,1,0:T(8,128)S(1)}, f32[64,8,128]{2,1,0:T(8,128)S(1)}, u32[]{:S(2)}, u32[]{:S(2)}) collective-permute-start(f32[64,8,128]{2,1,0:T(8,128)S(1)} %get-tuple-element.65), channel_id=1, source_target_pairs={{0,8},{4,12},{8,0},{12,4},{16,24},{20,28},{24,16},{28,20},{32,40},... | collective-permute-start | bytes 786440 | tf_op jit(solution)/shard_map/ppermute | solution.py:310
  31.8 6.5 %collective-permute-start.6 = (f32[64,8,128]{2,1,0:T(8,128)S(1)}, f32[64,8,128]{2,1,0:T(8,128)S(1)}, u32[]{:S(2)}, u32[]{:S(2)}) collective-permute-start(f32[64,8,128]{2,1,0:T(8,128)S(1)} %get-tuple-element.51), channel_id=1, source_target_pairs={{0,24},{4,28},{8,16},{12,20},{16,8},{20,12},{24,0},{28,4},{32,56},... | collective-permute-start | bytes 786440 | tf_op jit(solution)/shard_map/ppermute | solution.py:310
  39.8 71.7 %copy-start.1 = (f32[2,1,16384]{2,1,0:T(1,128)S(1)}, f32[2,1,16384]{2,1,0:T(1,128)}, u32[]{:S(2)}) copy-start(f32[2,1,16384]{2,1,0:T(1,128)} %param.6) | copy-start | bytes 393220
  39.8 33.6 %all-to-all-start = ((f32[192,8,128]{2,1,0:T(8,128)}), f32[192,8,128]{2,1,0:T(8,128)S(1)}, u32[]{:S(2)}, u32[]{:S(2)}) async-start(f32[192,8,128]{2,1,0:T(8,128)} %pack.1), calls=%async_computation | async-start | bytes 1572864 | tf_op jit(solution)/shard_map/all_to_all | solution.py:314
  74.4 5.0 %collective-permute-start.14 = (f32[64,256]{1,0:T(8,128)S(1)}, f32[64,256]{1,0:T(8,128)S(1)}, u32[]{:S(2)}, u32[]{:S(2)}) collective-permute-start(f32[64,256]{1,0:T(8,128)S(1)} %get-tuple-element.68), channel_id=1, source_target_pairs={{0,1},{1,2},{2,3},{3,0},{4,5},{5,6},{6,7},{7,4},{8,9},{9,10},{10,1... | collective-permute-start | bytes 196616 | tf_op jit(solution)/shard_map/ppermute | solution.py:289
  75.7 5.1 %collective-permute-start.15 = (f32[64,256]{1,0:T(8,128)S(1)}, f32[64,256]{1,0:T(8,128)S(1)}, u32[]{:S(2)}, u32[]{:S(2)}) collective-permute-start(f32[64,256]{1,0:T(8,128)S(1)} %get-tuple-element.69), channel_id=1, source_target_pairs={{0,2},{1,3},{2,0},{3,1},{4,6},{5,7},{6,4},{7,5},{8,10},{9,11},{10,... | collective-permute-start | bytes 196616 | tf_op jit(solution)/shard_map/ppermute | solution.py:288
  78.3 3.7 %collective-permute-start.16 = (f32[64,256]{1,0:T(8,128)S(1)}, f32[64,256]{1,0:T(8,128)S(1)}, u32[]{:S(2)}, u32[]{:S(2)}) collective-permute-start(f32[64,256]{1,0:T(8,128)S(1)} %get-tuple-element.70), channel_id=1, source_target_pairs={{0,3},{1,0},{2,1},{3,2},{4,7},{5,4},{6,5},{7,6},{8,11},{9,8},{10,9... | collective-permute-start | bytes 196616 | tf_op jit(solution)/shard_map/ppermute | solution.py:289
